TPU v7x, 512 devices: a whole 4x4x16 slice. The times are simulated.
512 devices in a mesh: blk: 32 (over z, y_lo), roll: 16 (over x, y_hi, core).
Axes of the slice: x: 4, y: 4 (y_hi: 2, y_lo: 2; y = y_hi * 2 + y_lo), z: 16, core: 2. Of those that a mesh axis runs over, the one named last changes fastest.
Arguments:
- p_query: bfloat16 [512, 4096], P('roll', 'blk'), may hold values from -6 to 6
- p_key: bfloat16 [512, 512], P(('blk', 'roll')), may hold values from -6 to 6
- p_value: bfloat16 [512, 512], P(('blk', 'roll')), may hold values from -6 to 6
- p_out: bfloat16 [512, 4096], P('roll', 'blk'), may hold values from -6 to 6
- p_grad: bfloat16 [512, 4096], P('roll', 'blk'), may hold values from -3 to 3
- p_lse: float32 [512, 32], P('roll', 'blk')
- r_query: bfloat16 [16, 3072, 4096], P('roll', 'blk'), may hold values from -6 to 6
- r_key: bfloat16 [16, 3072, 512], P('roll', 'blk'), may hold values from -6 to 6
- r_value: bfloat16 [16, 3072, 512], P('roll', 'blk'), may hold values from -6 to 6
- r_out: bfloat16 [16, 3072, 4096], P('roll', 'blk'), may hold values from -6 to 6
- r_grad: bfloat16 [16, 3072, 4096], P('roll', 'blk'), may hold values from -3 to 3
- r_lse: float32 [16, 3072, 32], P('roll', 'blk')
- lengths: int32 [16], P('roll'), may hold values from 1024 to 3072, as said below
Outputs:
- p_dq: bfloat16 [512, 4096], P('roll', 'blk')
- p_dk: bfloat16 [512, 512], P(('blk', 'roll'))
- p_dv: bfloat16 [512, 512], P(('blk', 'roll'))
- r_dq: bfloat16 [16, 3072, 4096], P('roll', 'blk')
- r_dk: bfloat16 [16, 3072, 512], P('roll', 'blk')
- r_dv: bfloat16 [16, 3072, 512], P('roll', 'blk')
Inputs may be any that keep to these rules, and one draw needn't show every extreme that they name: `lengths`: each length is a multiple of 16 and some rollout fills all 3072 positions.
All inputs are finite; a program needn't handle non-finite values.
Results may differ from a plain program's by a relative error of at most 0.018.
Values may be sent and summed in bfloat16 or wider, within the bound.
No kernel may reach another device: no remote copies, remote signals or barrier semaphores. Data moves between devices by JAX's collectives and lax.ppermute only.
A program may use at most 64 MiB of HBM per device.

v0:
```python
import jax
import jax.numpy as jnp
from jax import lax
from jax.sharding import PartitionSpec as P

HQ = 32
KVH = 4
HD = 128
GRP = 8


def passed_along(block, axis, distance):
    devices = range(lax.axis_size(axis))
    route = [((i - distance) % len(devices), i) for i in devices]
    return lax.ppermute(block, axis, route)


def group_pass(query, grads, lse_rows, delta_rows, keys, values, allowed):
    scale = HD ** (-0.5)
    scores = jnp.einsum("rqd,cd->qrc", query, keys, preferred_element_type=jnp.float32) * scale
    probs = jnp.where(allowed[None], jnp.exp(scores - lse_rows.T[:, :, None]), 0.0)
    dprobs = jnp.einsum("rqd,cd->qrc", grads, values, preferred_element_type=jnp.float32)
    dscores = (probs * (dprobs - delta_rows.T[:, :, None])).astype(jnp.bfloat16)
    weights = probs.astype(jnp.bfloat16)
    dquery = jnp.einsum("qrc,cd->rqd", dscores, keys, preferred_element_type=jnp.float32) * scale
    dkeys = jnp.einsum("qrc,rqd->cd", dscores, query, preferred_element_type=jnp.float32) * scale
    dvalues = jnp.einsum("qrc,rqd->cd", weights, grads, preferred_element_type=jnp.float32)
    return (dquery, dkeys, dvalues)


def attend(query, grads, lse_rows, delta_rows, keys, values, allowed):
    height = query.shape[0]
    width = GRP * HD
    query_parts = []
    key_parts = []
    value_parts = []
    for group in range(KVH):
        dquery, dkeys, dvalues = group_pass(
            query[:, group * width : (group + 1) * width].reshape(height, GRP, HD),
            grads[:, group * width : (group + 1) * width].reshape(height, GRP, HD),
            lse_rows[:, group * GRP : (group + 1) * GRP],
            delta_rows[:, group * GRP : (group + 1) * GRP],
            keys[:, group * HD : (group + 1) * HD],
            values[:, group * HD : (group + 1) * HD],
            allowed,
        )
        query_parts.append(dquery.reshape(height, width))
        key_parts.append(dkeys)
        value_parts.append(dvalues)
    return (
        jnp.concatenate(query_parts, axis=1),
        jnp.stack([jnp.concatenate(key_parts, axis=1), jnp.concatenate(value_parts, axis=1)]),
    )


def row_delta(grads, outputs):
    height = grads.shape[0]
    heads = grads.shape[1] // HD
    return jnp.sum(
        grads.reshape(height, heads, HD).astype(jnp.float32)
        * outputs.reshape(height, heads, HD).astype(jnp.float32),
        axis=2,
    )


def on_device(
    p_query,
    p_key,
    p_value,
    p_out,
    p_grad,
    p_lse,
    r_query,
    r_key,
    r_value,
    r_out,
    r_grad,
    r_lse,
    lengths,
):
    blocks = lax.axis_size("blk")
    owner = lax.axis_index("blk")
    member = lax.axis_index("roll")
    prompt_rows = p_query.shape[0]
    head_count = p_query.shape[1] // HD
    rollout_rows = r_query.shape[1]
    prompt_len = prompt_rows * lax.axis_size("roll")
    kv_width = KVH * HD
    queries = r_query[0]
    grads = r_grad[0]
    lse_rows = r_lse[0]
    delta = row_delta(grads, r_out[0])
    prompt_delta = row_delta(p_grad, p_out)
    prompt_pos = member * prompt_rows + jnp.arange(prompt_rows)
    rollout_pos = owner * rollout_rows + jnp.arange(rollout_rows)
    live = rollout_pos < lengths[0]
    pairs = jnp.stack([p_key, p_value])
    query_grads = jnp.zeros((rollout_rows, HQ * HD), jnp.float32)
    prompt_acc = jnp.zeros((2, prompt_len, kv_width), jnp.float32)
    prompt_dq = jnp.zeros((prompt_rows, head_count * HD), jnp.float32)
    whole = lax.all_gather(pairs, ("blk", "roll"), axis=1, tiled=True)
    prompt_prompt_dq = prompt_dq
    count = whole.shape[1]
    key_pos = jnp.arange(count)
    allowed = jnp.broadcast_to(live[:, None], (rollout_rows, count))
    query_add, pair_add = attend(queries, grads, lse_rows, delta, whole[0], whole[1], allowed)
    prompt_query_grads = query_add
    causal = prompt_pos[:, None] >= key_pos[None, :]
    head = owner * head_count + 0
    column = head // GRP * HD
    keys = lax.dynamic_slice_in_dim(whole[0], column, HD, 1)
    values = lax.dynamic_slice_in_dim(whole[1], column, HD, 1)
    dquery, dkeys, dvalues = group_pass(
        p_query[:, None], p_grad[:, None], p_lse, prompt_delta, keys, values, causal
    )
    prompt_prompt_dq = prompt_prompt_dq.at[:, 0:HD].add(dquery[:, 0])
    zero = jnp.zeros((), jnp.int32)
    current = lax.dynamic_slice(pair_add, (zero, zero, column), (2, count, HD))
    pair_add = lax.dynamic_update_slice(
        pair_add, current + jnp.stack([dkeys, dvalues]), (zero, zero, column)
    )
    prompt_prompt_acc = pair_add
    query_grads = prompt_query_grads
    prompt_acc = prompt_prompt_acc
    prompt_dq = prompt_prompt_dq
    prompt_pieces = pairs

    def cycle_step(step, state):
        key_values, grad_sums, query_grads, prompt_pieces, prompt_acc, prompt_dq = state
        source = (owner - step) % blocks
        key_pos = source * rollout_rows + jnp.arange(rollout_rows)
        allowed = live[:, None] & (rollout_pos[:, None] >= key_pos[None, :])

        def compute_block():
            return attend(queries, grads, lse_rows, delta, key_values[0], key_values[1], allowed)

        def empty_block():
            return (
                jnp.zeros((rollout_rows, HQ * HD), jnp.float32),
                jnp.zeros(grad_sums.shape, jnp.float32),
            )

        query_add, pair_add = lax.cond(jnp.any(allowed), compute_block, empty_block)
        query_grads = query_grads + query_add
        grad_sums = (grad_sums.astype(jnp.float32) + pair_add).astype(jnp.bfloat16)
        key_values, grad_sums = passed_along((key_values, grad_sums), "blk", 1)
        return (key_values, grad_sums, query_grads, prompt_pieces, prompt_acc, prompt_dq)

    rollout_pairs = jnp.stack([r_key[0], r_value[0]])
    rollout_sums = jnp.zeros(rollout_pairs.shape, jnp.bfloat16)
    state = (rollout_pairs, rollout_sums, query_grads, prompt_pieces, prompt_acc, prompt_dq)
    rollout_pairs, rollout_sums, query_grads, prompt_pieces, prompt_acc, prompt_dq = lax.fori_loop(
        0, blocks, cycle_step, state
    )
    reduced = lax.psum_scatter(prompt_acc, ("blk", "roll"), scatter_dimension=1, tiled=True)
    return (
        prompt_dq.astype(jnp.bfloat16),
        reduced[0].astype(jnp.bfloat16),
        reduced[1].astype(jnp.bfloat16),
        query_grads[None].astype(jnp.bfloat16),
        rollout_sums[0][None],
        rollout_sums[1][None],
    )


def solution(mesh):
    placed = (
        P("roll", "blk"),
        P(("blk", "roll"), None),
        P(("blk", "roll"), None),
        P("roll", "blk"),
        P("roll", "blk"),
        P("roll", "blk"),
        P("roll", "blk", None),
        P("roll", "blk", None),
        P("roll", "blk", None),
        P("roll", "blk", None),
        P("roll", "blk", None),
        P("roll", "blk", None),
        P("roll"),
    )
    return jax.shard_map(
        on_device,
        mesh=mesh,
        in_specs=placed,
        out_specs=(
            P("roll", "blk"),
            P(("blk", "roll"), None),
            P(("blk", "roll"), None),
            P("roll", "blk", None),
            P("roll", "blk", None),
            P("roll", "blk", None),
        ),
        check_vma=False,
    )
```

profile of v0, /device:TPU:6, one launch (start us, length us, event | category | flops | bytes accessed | tf_op | source)
XLA Modules:
  0.0 1796.9 jit_solution(4911210430453903594)
XLA Ops:
  16.1 746.2 %all-gather.2.cloned.1.call-done = bf16[2,512,512]{2,0,1:T(2,128)(2,1)} async-done(((bf16[2,1,512]{2,0,1:T(2,128)(2,1)}), bf16[2,512,512]{2,0,1:T(2,128)(2,1)}) %all-gather.2.cloned.1.call-update) | async-done | bytes 1048592 | tf_op jit(solution)/shard_map/all_gather | solution.py:101
  762.3 3.4 fusion.164
  776.9 2.5 copy.119
  779.3 109.1 %all-reduce.2 = bf16[2,512,512]{2,0,1:T(2,128)(2,1)S(1)} all-reduce(f32[2,512,512]{2,0,1:T(2,128)} %copy.119), channel_id=2, replica_groups=mesh['blk'=32,'roll'=16] {'blk','roll'}, use_global_device_ids=true, to_apply=%region_2.3.clone | all-reduce | flops 524288 | bytes 3145728
  890.3 898.0 %while.23 = (s32[]{:T(128)}, bf16[2,96,512]{2,1,0:T(8,128)(2,1)}, bf16[2,96,512]{2,1,0:T(8,128)(2,1)}, f32[96,4096]{1,0:T(8,128)S(1)}, s32[]{:T(128)}, /*index=5...) while((s32[]{:T(128)}, bf16[2,96,512]{2,1,0:T(8,128)(2,1)}, ...), condition=%wide.region_7.8_spmd.clone.clone, body=%wide.region_3.7_spmd.clone.clone.sunk | while | flops 382283136 | bytes 31145144 | solution.py:152
  891.9 2.1 collective-permute-start
  896.8 9.0 conditional.4
  907.4 3.3 collective-permute-start.1
  911.1 8.0 collective-permute-done.1
  921.4 1.9 collective-permute-start
  927.9 11.9 collective-permute-start.1
  940.2 6.4 collective-permute-done.1
  948.9 1.9 collective-permute-start
  955.4 3.2 collective-permute-start.1
  959.0 16.9 collective-permute-done.1
  978.2 1.9 collective-permute-start
  988.6 15.0 collective-permute-done.1
  1005.8 1.9 collective-permute-start
  1015.8 16.2 collective-permute-done.1
  1044.4 15.1 collective-permute-done.1
  1071.8 15.2 collective-permute-done.1
  1099.3 17.0 collective-permute-done.1
  1128.6 15.2 collective-permute-done.1
  1156.0 16.6 collective-permute-done.1
  1183.7 2.9 collective-permute-done
  1186.6 13.5 collective-permute-done.1
  1212.4 17.2 collective-permute-done.1
  1241.9 15.2 collective-permute-done.1
  1270.0 14.6 collective-permute-done.1
  1297.4 14.7 collective-permute-done.1
  1324.3 15.2 collective-permute-done.1
  1351.8 15.2 collective-permute-done.1
  1379.3 17.2 collective-permute-done.1
  1408.8 17.2 collective-permute-done.1
  1438.2 15.2 collective-permute-done.1
  1464.6 2.3 collective-permute-done
  1466.9 14.0 collective-permute-done.1
  1493.5 14.9 collective-permute-done.1
  1520.7 15.5 collective-permute-done.1
  1548.5 16.7 collective-permute-done.1
  1578.1 16.0 collective-permute-done.1
  1606.4 16.4 collective-permute-done.1
  1635.1 15.2 collective-permute-done.1
  1662.5 15.2 collective-permute-done.1
  1690.0 15.2 collective-permute-done.1
  1717.5 15.2 collective-permute-done.1
  1745.0 15.2 collective-permute-done.1
  1772.5 15.2 collective-permute-done.1
  (577 shorter events, 386.7 us)
Async XLA Ops:
  7.2 755.1 %all-gather.2.cloned.1.call-start = ((), (), s32[]{:S(2)}) async-start(), calls=%async_computation | async-start | bytes 1050624 | tf_op jit(solution)/shard_map/all_gather | solution.py:101
  891.9 19.2 %collective-permute-start = (bf16[2,96,512]{2,1,0:T(8,128)(2,1)}, bf16[2,96,512]{2,1,0:T(8,128)(2,1)}, u32[]{:S(2)}, u32[]{:S(2)}) collective-permute-start(bf16[2,96,512]{2,1,0:T(8,128)(2,1)} %copy.313), channel_id=1, source_target_pairs={{496,0},{0,16},{16,32},{32,48},{48,64},{64,80},{80,96},{96,112},{1... | collective-permute-start | bytes 589832 | tf_op jit(solution)/shard_map/while/body/eval_jaxpr/ppermute | solution.py:15
  907.4 11.7 collective-permute-start.1
  921.4 18.8 %collective-permute-start = (bf16[2,96,512]{2,1,0:T(8,128)(2,1)}, bf16[2,96,512]{2,1,0:T(8,128)(2,1)}, u32[]{:S(2)}, u32[]{:S(2)}) collective-permute-start(bf16[2,96,512]{2,1,0:T(8,128)(2,1)} %copy.313), channel_id=1, source_target_pairs={{496,0},{0,16},{16,32},{32,48},{48,64},{64,80},{80,96},{96,112},{1... | collective-permute-start | bytes 589832 | tf_op jit(solution)/shard_map/while/body/eval_jaxpr/ppermute | solution.py:15
  927.9 18.7 %collective-permute-start.1 = (bf16[2,96,512]{2,1,0:T(8,128)(2,1)}, bf16[2,96,512]{2,1,0:T(8,128)(2,1)S(1)}, u32[]{:S(2)}, u32[]{:S(2)}) collective-permute-start(bf16[2,96,512]{2,1,0:T(8,128)(2,1)} %add_convert_fusion.2), channel_id=1, source_target_pairs={{496,0},{0,16},{16,32},{32,48},{48,64},{64,80},{80,96},{96,112},{1... | collective-permute-start | bytes 589832 | tf_op jit(solution)/shard_map/while/body/eval_jaxpr/ppermute | solution.py:15
  948.9 10.1 collective-permute-start
  955.4 20.5 %collective-permute-start.1 = (bf16[2,96,512]{2,1,0:T(8,128)(2,1)}, bf16[2,96,512]{2,1,0:T(8,128)(2,1)S(1)}, u32[]{:S(2)}, u32[]{:S(2)}) collective-permute-start(bf16[2,96,512]{2,1,0:T(8,128)(2,1)} %add_convert_fusion.2), channel_id=1, source_target_pairs={{496,0},{0,16},{16,32},{32,48},{48,64},{64,80},{80,96},{96,112},{1... | collective-permute-start | bytes 589832 | tf_op jit(solution)/shard_map/while/body/eval_jaxpr/ppermute | solution.py:15
  978.2 10.3 collective-permute-start
  984.7 18.9 %collective-permute-start.1 = (bf16[2,96,512]{2,1,0:T(8,128)(2,1)}, bf16[2,96,512]{2,1,0:T(8,128)(2,1)S(1)}, u32[]{:S(2)}, u32[]{:S(2)}) collective-permute-start(bf16[2,96,512]{2,1,0:T(8,128)(2,1)} %add_convert_fusion.2), channel_id=1, source_target_pairs={{496,0},{0,16},{16,32},{32,48},{48,64},{64,80},{80,96},{96,112},{1... | collective-permute-start | bytes 589832 | tf_op jit(solution)/shard_map/while/body/eval_jaxpr/ppermute | solution.py:15
  1005.8 10.0 collective-permute-start
  1012.3 19.7 %collective-permute-start.1 = (bf16[2,96,512]{2,1,0:T(8,128)(2,1)}, bf16[2,96,512]{2,1,0:T(8,128)(2,1)S(1)}, u32[]{:S(2)}, u32[]{:S(2)}) collective-permute-start(bf16[2,96,512]{2,1,0:T(8,128)(2,1)} %add_convert_fusion.2), channel_id=1, source_target_pairs={{496,0},{0,16},{16,32},{32,48},{48,64},{64,80},{80,96},{96,112},{1... | collective-permute-start | bytes 589832 | tf_op jit(solution)/shard_map/while/body/eval_jaxpr/ppermute | solution.py:15
  1034.3 10.1 collective-permute-start
  1040.8 18.7 %collective-permute-start.1 = (bf16[2,96,512]{2,1,0:T(8,128)(2,1)}, bf16[2,96,512]{2,1,0:T(8,128)(2,1)S(1)}, u32[]{:S(2)}, u32[]{:S(2)}) collective-permute-start(bf16[2,96,512]{2,1,0:T(8,128)(2,1)} %add_convert_fusion.2), channel_id=1, source_target_pairs={{496,0},{0,16},{16,32},{32,48},{48,64},{64,80},{80,96},{96,112},{1... | collective-permute-start | bytes 589832 | tf_op jit(solution)/shard_map/while/body/eval_jaxpr/ppermute | solution.py:15
  1061.8 10.0 collective-permute-start
  1068.3 18.7 %collective-permute-start.1 = (bf16[2,96,512]{2,1,0:T(8,128)(2,1)}, bf16[2,96,512]{2,1,0:T(8,128)(2,1)S(1)}, u32[]{:S(2)}, u32[]{:S(2)}) collective-permute-start(bf16[2,96,512]{2,1,0:T(8,128)(2,1)} %add_convert_fusion.2), channel_id=1, source_target_pairs={{496,0},{0,16},{16,32},{32,48},{48,64},{64,80},{80,96},{96,112},{1... | collective-permute-start | bytes 589832 | tf_op jit(solution)/shard_map/while/body/eval_jaxpr/ppermute | solution.py:15
  1089.3 10.0 collective-permute-start
  1095.8 20.5 %collective-permute-start.1 = (bf16[2,96,512]{2,1,0:T(8,128)(2,1)}, bf16[2,96,512]{2,1,0:T(8,128)(2,1)S(1)}, u32[]{:S(2)}, u32[]{:S(2)}) collective-permute-start(bf16[2,96,512]{2,1,0:T(8,128)(2,1)} %add_convert_fusion.2), channel_id=1, source_target_pairs={{496,0},{0,16},{16,32},{32,48},{48,64},{64,80},{80,96},{96,112},{1... | collective-permute-start | bytes 589832 | tf_op jit(solution)/shard_map/while/body/eval_jaxpr/ppermute | solution.py:15
  1125.1 18.7 %collective-permute-start.1 = (bf16[2,96,512]{2,1,0:T(8,128)(2,1)}, bf16[2,96,512]{2,1,0:T(8,128)(2,1)S(1)}, u32[]{:S(2)}, u32[]{:S(2)}) collective-permute-start(bf16[2,96,512]{2,1,0:T(8,128)(2,1)} %add_convert_fusion.2), channel_id=1, source_target_pairs={{496,0},{0,16},{16,32},{32,48},{48,64},{64,80},{80,96},{96,112},{1... | collective-permute-start | bytes 589832 | tf_op jit(solution)/shard_map/while/body/eval_jaxpr/ppermute | solution.py:15
  1152.6 20.1 %collective-permute-start.1 = (bf16[2,96,512]{2,1,0:T(8,128)(2,1)}, bf16[2,96,512]{2,1,0:T(8,128)(2,1)S(1)}, u32[]{:S(2)}, u32[]{:S(2)}) collective-permute-start(bf16[2,96,512]{2,1,0:T(8,128)(2,1)} %add_convert_fusion.2), channel_id=1, source_target_pairs={{496,0},{0,16},{16,32},{32,48},{48,64},{64,80},{80,96},{96,112},{1... | collective-permute-start | bytes 589832 | tf_op jit(solution)/shard_map/while/body/eval_jaxpr/ppermute | solution.py:15
  1174.9 11.7 collective-permute-start
  1181.4 18.7 %collective-permute-start.1 = (bf16[2,96,512]{2,1,0:T(8,128)(2,1)}, bf16[2,96,512]{2,1,0:T(8,128)(2,1)S(1)}, u32[]{:S(2)}, u32[]{:S(2)}) collective-permute-start(bf16[2,96,512]{2,1,0:T(8,128)(2,1)} %add_convert_fusion.2), channel_id=1, source_target_pairs={{496,0},{0,16},{16,32},{32,48},{48,64},{64,80},{80,96},{96,112},{1... | collective-permute-start | bytes 589832 | tf_op jit(solution)/shard_map/while/body/eval_jaxpr/ppermute | solution.py:15
  1208.9 20.7 %collective-permute-start.1 = (bf16[2,96,512]{2,1,0:T(8,128)(2,1)}, bf16[2,96,512]{2,1,0:T(8,128)(2,1)S(1)}, u32[]{:S(2)}, u32[]{:S(2)}) collective-permute-start(bf16[2,96,512]{2,1,0:T(8,128)(2,1)} %add_convert_fusion.2), channel_id=1, source_target_pairs={{496,0},{0,16},{16,32},{32,48},{48,64},{64,80},{80,96},{96,112},{1... | collective-permute-start | bytes 589832 | tf_op jit(solution)/shard_map/while/body/eval_jaxpr/ppermute | solution.py:15
  1238.4 18.7 %collective-permute-start.1 = (bf16[2,96,512]{2,1,0:T(8,128)(2,1)}, bf16[2,96,512]{2,1,0:T(8,128)(2,1)S(1)}, u32[]{:S(2)}, u32[]{:S(2)}) collective-permute-start(bf16[2,96,512]{2,1,0:T(8,128)(2,1)} %add_convert_fusion.2), channel_id=1, source_target_pairs={{496,0},{0,16},{16,32},{32,48},{48,64},{64,80},{80,96},{96,112},{1... | collective-permute-start | bytes 589832 | tf_op jit(solution)/shard_map/while/body/eval_jaxpr/ppermute | solution.py:15
  1259.4 10.6 collective-permute-start
  1265.9 18.7 %collective-permute-start.1 = (bf16[2,96,512]{2,1,0:T(8,128)(2,1)}, bf16[2,96,512]{2,1,0:T(8,128)(2,1)S(1)}, u32[]{:S(2)}, u32[]{:S(2)}) collective-permute-start(bf16[2,96,512]{2,1,0:T(8,128)(2,1)} %add_convert_fusion.2), channel_id=1, source_target_pairs={{496,0},{0,16},{16,32},{32,48},{48,64},{64,80},{80,96},{96,112},{1... | collective-permute-start | bytes 589832 | tf_op jit(solution)/shard_map/while/body/eval_jaxpr/ppermute | solution.py:15
  1286.8 10.5 collective-permute-start
  1293.3 18.7 %collective-permute-start.1 = (bf16[2,96,512]{2,1,0:T(8,128)(2,1)}, bf16[2,96,512]{2,1,0:T(8,128)(2,1)S(1)}, u32[]{:S(2)}, u32[]{:S(2)}) collective-permute-start(bf16[2,96,512]{2,1,0:T(8,128)(2,1)} %add_convert_fusion.2), channel_id=1, source_target_pairs={{496,0},{0,16},{16,32},{32,48},{48,64},{64,80},{80,96},{96,112},{1... | collective-permute-start | bytes 589832 | tf_op jit(solution)/shard_map/while/body/eval_jaxpr/ppermute | solution.py:15
  1320.8 18.7 %collective-permute-start.1 = (bf16[2,96,512]{2,1,0:T(8,128)(2,1)}, bf16[2,96,512]{2,1,0:T(8,128)(2,1)S(1)}, u32[]{:S(2)}, u32[]{:S(2)}) collective-permute-start(bf16[2,96,512]{2,1,0:T(8,128)(2,1)} %add_convert_fusion.2), channel_id=1, source_target_pairs={{496,0},{0,16},{16,32},{32,48},{48,64},{64,80},{80,96},{96,112},{1... | collective-permute-start | bytes 589832 | tf_op jit(solution)/shard_map/while/body/eval_jaxpr/ppermute | solution.py:15
  1348.3 18.7 %collective-permute-start.1 = (bf16[2,96,512]{2,1,0:T(8,128)(2,1)}, bf16[2,96,512]{2,1,0:T(8,128)(2,1)S(1)}, u32[]{:S(2)}, u32[]{:S(2)}) collective-permute-start(bf16[2,96,512]{2,1,0:T(8,128)(2,1)} %add_convert_fusion.2), channel_id=1, source_target_pairs={{496,0},{0,16},{16,32},{32,48},{48,64},{64,80},{80,96},{96,112},{1... | collective-permute-start | bytes 589832 | tf_op jit(solution)/shard_map/while/body/eval_jaxpr/ppermute | solution.py:15
  1375.8 20.7 %collective-permute-start.1 = (bf16[2,96,512]{2,1,0:T(8,128)(2,1)}, bf16[2,96,512]{2,1,0:T(8,128)(2,1)S(1)}, u32[]{:S(2)}, u32[]{:S(2)}) collective-permute-start(bf16[2,96,512]{2,1,0:T(8,128)(2,1)} %add_convert_fusion.2), channel_id=1, source_target_pairs={{496,0},{0,16},{16,32},{32,48},{48,64},{64,80},{80,96},{96,112},{1... | collective-permute-start | bytes 589832 | tf_op jit(solution)/shard_map/while/body/eval_jaxpr/ppermute | solution.py:15
  1405.3 20.7 %collective-permute-start.1 = (bf16[2,96,512]{2,1,0:T(8,128)(2,1)}, bf16[2,96,512]{2,1,0:T(8,128)(2,1)S(1)}, u32[]{:S(2)}, u32[]{:S(2)}) collective-permute-start(bf16[2,96,512]{2,1,0:T(8,128)(2,1)} %add_convert_fusion.2), channel_id=1, source_target_pairs={{496,0},{0,16},{16,32},{32,48},{48,64},{64,80},{80,96},{96,112},{1... | collective-permute-start | bytes 589832 | tf_op jit(solution)/shard_map/while/body/eval_jaxpr/ppermute | solution.py:15
  1434.8 18.7 %collective-permute-start.1 = (bf16[2,96,512]{2,1,0:T(8,128)(2,1)}, bf16[2,96,512]{2,1,0:T(8,128)(2,1)S(1)}, u32[]{:S(2)}, u32[]{:S(2)}) collective-permute-start(bf16[2,96,512]{2,1,0:T(8,128)(2,1)} %add_convert_fusion.2), channel_id=1, source_target_pairs={{496,0},{0,16},{16,32},{32,48},{48,64},{64,80},{80,96},{96,112},{1... | collective-permute-start | bytes 589832 | tf_op jit(solution)/shard_map/while/body/eval_jaxpr/ppermute | solution.py:15
  1455.8 11.2 collective-permute-start
  1462.3 18.7 %collective-permute-start.1 = (bf16[2,96,512]{2,1,0:T(8,128)(2,1)}, bf16[2,96,512]{2,1,0:T(8,128)(2,1)S(1)}, u32[]{:S(2)}, u32[]{:S(2)}) collective-permute-start(bf16[2,96,512]{2,1,0:T(8,128)(2,1)} %add_convert_fusion.2), channel_id=1, source_target_pairs={{496,0},{0,16},{16,32},{32,48},{48,64},{64,80},{80,96},{96,112},{1... | collective-permute-start | bytes 589832 | tf_op jit(solution)/shard_map/while/body/eval_jaxpr/ppermute | solution.py:15
  1483.2 10.3 collective-permute-start
  1489.7 18.7 %collective-permute-start.1 = (bf16[2,96,512]{2,1,0:T(8,128)(2,1)}, bf16[2,96,512]{2,1,0:T(8,128)(2,1)S(1)}, u32[]{:S(2)}, u32[]{:S(2)}) collective-permute-start(bf16[2,96,512]{2,1,0:T(8,128)(2,1)} %add_convert_fusion.2), channel_id=1, source_target_pairs={{496,0},{0,16},{16,32},{32,48},{48,64},{64,80},{80,96},{96,112},{1... | collective-permute-start | bytes 589832 | tf_op jit(solution)/shard_map/while/body/eval_jaxpr/ppermute | solution.py:15
  1517.2 19.0 %collective-permute-start.1 = (bf16[2,96,512]{2,1,0:T(8,128)(2,1)}, bf16[2,96,512]{2,1,0:T(8,128)(2,1)S(1)}, u32[]{:S(2)}, u32[]{:S(2)}) collective-permute-start(bf16[2,96,512]{2,1,0:T(8,128)(2,1)} %add_convert_fusion.2), channel_id=1, source_target_pairs={{496,0},{0,16},{16,32},{32,48},{48,64},{64,80},{80,96},{96,112},{1... | collective-permute-start | bytes 589832 | tf_op jit(solution)/shard_map/while/body/eval_jaxpr/ppermute | solution.py:15
  1545.0 20.2 %collective-permute-start.1 = (bf16[2,96,512]{2,1,0:T(8,128)(2,1)}, bf16[2,96,512]{2,1,0:T(8,128)(2,1)S(1)}, u32[]{:S(2)}, u32[]{:S(2)}) collective-permute-start(bf16[2,96,512]{2,1,0:T(8,128)(2,1)} %add_convert_fusion.2), channel_id=1, source_target_pairs={{496,0},{0,16},{16,32},{32,48},{48,64},{64,80},{80,96},{96,112},{1... | collective-permute-start | bytes 589832 | tf_op jit(solution)/shard_map/while/body/eval_jaxpr/ppermute | solution.py:15
  1567.5 10.6 collective-permute-start
  1574.0 20.1 %collective-permute-start.1 = (bf16[2,96,512]{2,1,0:T(8,128)(2,1)}, bf16[2,96,512]{2,1,0:T(8,128)(2,1)S(1)}, u32[]{:S(2)}, u32[]{:S(2)}) collective-permute-start(bf16[2,96,512]{2,1,0:T(8,128)(2,1)} %add_convert_fusion.2), channel_id=1, source_target_pairs={{496,0},{0,16},{16,32},{32,48},{48,64},{64,80},{80,96},{96,112},{1... | collective-permute-start | bytes 589832 | tf_op jit(solution)/shard_map/while/body/eval_jaxpr/ppermute | solution.py:15
  1602.9 19.9 %collective-permute-start.1 = (bf16[2,96,512]{2,1,0:T(8,128)(2,1)}, bf16[2,96,512]{2,1,0:T(8,128)(2,1)S(1)}, u32[]{:S(2)}, u32[]{:S(2)}) collective-permute-start(bf16[2,96,512]{2,1,0:T(8,128)(2,1)} %add_convert_fusion.2), channel_id=1, source_target_pairs={{496,0},{0,16},{16,32},{32,48},{48,64},{64,80},{80,96},{96,112},{1... | collective-permute-start | bytes 589832 | tf_op jit(solution)/shard_map/while/body/eval_jaxpr/ppermute | solution.py:15
  1631.6 18.7 %collective-permute-start.1 = (bf16[2,96,512]{2,1,0:T(8,128)(2,1)}, bf16[2,96,512]{2,1,0:T(8,128)(2,1)S(1)}, u32[]{:S(2)}, u32[]{:S(2)}) collective-permute-start(bf16[2,96,512]{2,1,0:T(8,128)(2,1)} %add_convert_fusion.2), channel_id=1, source_target_pairs={{496,0},{0,16},{16,32},{32,48},{48,64},{64,80},{80,96},{96,112},{1... | collective-permute-start | bytes 589832 | tf_op jit(solution)/shard_map/while/body/eval_jaxpr/ppermute | solution.py:15
  1652.6 10.0 collective-permute-start
  1659.1 18.7 %collective-permute-start.1 = (bf16[2,96,512]{2,1,0:T(8,128)(2,1)}, bf16[2,96,512]{2,1,0:T(8,128)(2,1)S(1)}, u32[]{:S(2)}, u32[]{:S(2)}) collective-permute-start(bf16[2,96,512]{2,1,0:T(8,128)(2,1)} %add_convert_fusion.2), channel_id=1, source_target_pairs={{496,0},{0,16},{16,32},{32,48},{48,64},{64,80},{80,96},{96,112},{1... | collective-permute-start | bytes 589832 | tf_op jit(solution)/shard_map/while/body/eval_jaxpr/ppermute | solution.py:15
  1686.5 18.7 %collective-permute-start.1 = (bf16[2,96,512]{2,1,0:T(8,128)(2,1)}, bf16[2,96,512]{2,1,0:T(8,128)(2,1)S(1)}, u32[]{:S(2)}, u32[]{:S(2)}) collective-permute-start(bf16[2,96,512]{2,1,0:T(8,128)(2,1)} %add_convert_fusion.2), channel_id=1, source_target_pairs={{496,0},{0,16},{16,32},{32,48},{48,64},{64,80},{80,96},{96,112},{1... | collective-permute-start | bytes 589832 | tf_op jit(solution)/shard_map/while/body/eval_jaxpr/ppermute | solution.py:15
  1714.0 18.7 %collective-permute-start.1 = (bf16[2,96,512]{2,1,0:T(8,128)(2,1)}, bf16[2,96,512]{2,1,0:T(8,128)(2,1)S(1)}, u32[]{:S(2)}, u32[]{:S(2)}) collective-permute-start(bf16[2,96,512]{2,1,0:T(8,128)(2,1)} %add_convert_fusion.2), channel_id=1, source_target_pairs={{496,0},{0,16},{16,32},{32,48},{48,64},{64,80},{80,96},{96,112},{1... | collective-permute-start | bytes 589832 | tf_op jit(solution)/shard_map/while/body/eval_jaxpr/ppermute | solution.py:15
  1741.5 18.7 %collective-permute-start.1 = (bf16[2,96,512]{2,1,0:T(8,128)(2,1)}, bf16[2,96,512]{2,1,0:T(8,128)(2,1)S(1)}, u32[]{:S(2)}, u32[]{:S(2)}) collective-permute-start(bf16[2,96,512]{2,1,0:T(8,128)(2,1)} %add_convert_fusion.2), channel_id=1, source_target_pairs={{496,0},{0,16},{16,32},{32,48},{48,64},{64,80},{80,96},{96,112},{1... | collective-permute-start | bytes 589832 | tf_op jit(solution)/shard_map/while/body/eval_jaxpr/ppermute | solution.py:15
  1769.0 18.7 %collective-permute-start.1 = (bf16[2,96,512]{2,1,0:T(8,128)(2,1)}, bf16[2,96,512]{2,1,0:T(8,128)(2,1)S(1)}, u32[]{:S(2)}, u32[]{:S(2)}) collective-permute-start(bf16[2,96,512]{2,1,0:T(8,128)(2,1)} %add_convert_fusion.2), channel_id=1, source_target_pairs={{496,0},{0,16},{16,32},{32,48},{48,64},{64,80},{80,96},{96,112},{1... | collective-permute-start | bytes 589832 | tf_op jit(solution)/shard_map/while/body/eval_jaxpr/ppermute | solution.py:15
  (59 other events, 964.2 us)
Sparse Core Ops, SparseCore 0:
  10.7 751.5 all-gather.1
where the time goes:
time: 1800 us
  waiting for transfers between devices  1270 us (71%)
  other arithmetic  136 us (8%)
  starting transfers between devices  135 us (8%)
  blocking collectives  109 us (6%)
  local copies, waits for them, and re-layouts  94.5 us (5%)
  loops' own time  24.3 us (1%)
    all_gather x1, waiting for transfers between devices, on_device(): whole = lax.all_gather(pairs, ('blk', 'roll'), axis=1, tiled=True)  746 us
    ppermute x64, waiting for transfers between devices, passed_along(): return lax.ppermute(block, axis, route)  521 us
    ppermute x64, starting transfers between devices, passed_along(): return lax.ppermute(block, axis, route)  135 us
    unnamed x1, blocking collectives  109 us
    while x96, local copies, waits for them, and re-layouts  72.8 us
    convert_element_type x32, other arithmetic, cycle_step(): grad_sums = (grad_sums.astype(jnp.float32) + pair_add).astype(jnp.bfloat16)  52.6 us
    and x32, other arithmetic, cycle_step(): allowed = live[:, None] & (rollout_pos[:, None] >= key_pos[None, :])  44.3 us
  transfers between devices with their start and end apart: 65, of which 62 were waited for; matrix products, arithmetic and copies ran while one was open for 8% of the time, Pallas kernels for 0%

commit v1 on v0

v1 whole, which is shorter than its diff:
```python
import functools

import jax
import jax.numpy as jnp
from jax import lax
from jax.experimental import pallas as pl
from jax.experimental.pallas import tpu as pltpu
from jax.sharding import PartitionSpec as P

KVH = 4
HD = 128
GRP = 8
SCALE = HD ** (-0.5)
LOG2E = 1.4426950408889634
DEAD = 1e30

F32 = jnp.float32
BF16 = jnp.bfloat16
NN = (((1,), (0,)), ((), ()))
NT = (((1,), (1,)), ((), ()))
TN = (((0,), (0,)), ((), ()))


def dot(left, right, dims):
    return lax.dot_general(left, right, dims, preferred_element_type=F32)


def weigh(keys, values, query, grads, lse_row, delta_row, keep):
    scores = dot(keys, query, NT)
    dprobs = dot(values, grads, NT)
    probs = jnp.exp2(scores * (SCALE * LOG2E) - lse_row)
    if keep is not None:
        probs = jnp.where(keep, probs, 0.0)
    dscores = (probs * (dprobs - delta_row)).astype(BF16)
    return probs.astype(BF16), dscores


def kernel(
    info, q_ref, g_ref, rows_ref, pq_ref, pg_ref, prows_ref, kv_ref,
    dq_ref, dkv_ref, pdq_ref,
    qs, gs, wts, dsc, acc, pkv,
    *, span, share,
):
    square, live, first = info[0], info[1], info[2]
    pitch = span + share
    squares = kv_ref.shape[0] // pitch
    plen = squares * share
    for h in range(GRP):
        qs[h * span : (h + 1) * span, :] = q_ref[:, h * HD : (h + 1) * HD]
        gs[h * span : (h + 1) * span, :] = g_ref[:, h * HD : (h + 1) * HD]
    acc[...] = jnp.zeros_like(acc)

    def heads(keys, values, count, keep):
        for h in range(GRP):
            at = slice(h * span, (h + 1) * span)
            weights, dscores = weigh(
                keys, values, qs[at, :], gs[at, :],
                rows_ref[h : h + 1, :], rows_ref[GRP + h : GRP + h + 1, :], keep,
            )
            wts[0:count, at] = weights
            dsc[0:count, at] = dscores
            acc[at, :] += dot(dscores, keys, TN)
        dkeys = dot(dsc[0:count, :], qs[...], NN) * SCALE
        dvalues = dot(wts[0:count, :], gs[...], NN)
        return dkeys, dvalues

    for j in range(squares):
        pkv[j * share : (j + 1) * share, :] = kv_ref[j * pitch + span : (j + 1) * pitch, :]

    keys, values = pkv[:, 0:HD], pkv[:, HD : 2 * HD]
    spot = lax.broadcasted_iota(jnp.int32, (plen, pq_ref.shape[0]), 0)
    row = lax.broadcasted_iota(jnp.int32, (plen, pq_ref.shape[0]), 1) + first
    weights, dscores = weigh(
        keys, values, pq_ref[...], pg_ref[...], prows_ref[0:1, :], prows_ref[1:2, :], spot <= row
    )
    pdq_ref[...] = (dot(dscores, keys, TN) * SCALE).astype(BF16)
    own_dk = dot(dscores, pq_ref[...], NN) * SCALE
    own_dv = dot(weights, pg_ref[...], NN)

    def put_prompt(dkeys, dvalues):
        for j in range(squares):
            at = slice(j * share, (j + 1) * share)
            to = slice(j * pitch + span, (j + 1) * pitch)
            dkv_ref[to, 0:HD] = dkeys[at, :].astype(BF16)
            dkv_ref[to, HD : 2 * HD] = dvalues[at, :].astype(BF16)

    def put(base, dkeys, dvalues):
        dkv_ref[pl.ds(base, span), 0:HD] = dkeys.astype(BF16)
        dkv_ref[pl.ds(base, span), HD : 2 * HD] = dvalues.astype(BF16)

    def empty(j, carry):
        dkv_ref[pl.ds(pl.multiple_of(j * pitch, 16), span), :] = jnp.zeros((span, 2 * HD), BF16)
        return carry

    @pl.when(live == 0)
    def _():
        put_prompt(own_dk, own_dv)
        lax.fori_loop(0, squares, empty, 0)

    @pl.when(live != 0)
    def _():
        dkeys, dvalues = heads(keys, values, plen, None)
        put_prompt(own_dk + dkeys, own_dv + dvalues)

        def whole(j, carry):
            base = pl.multiple_of(j * pitch, 16)
            tile = kv_ref[pl.ds(base, span), :]
            put(base, *heads(tile[:, 0:HD], tile[:, HD : 2 * HD], span, None))
            return carry

        lax.fori_loop(0, square, whole, 0)
        base = pl.multiple_of(square * pitch, 16)
        tile = kv_ref[pl.ds(base, span), :]
        spot = lax.broadcasted_iota(jnp.int32, (span, span), 0)
        row = lax.broadcasted_iota(jnp.int32, (span, span), 1)
        put(base, *heads(tile[:, 0:HD], tile[:, HD : 2 * HD], span, spot <= row))
        lax.fori_loop(square + 1, squares, empty, 0)

    for h in range(GRP):
        dq_ref[:, h * HD : (h + 1) * HD] = (acc[h * span : (h + 1) * span, :] * SCALE).astype(BF16)


def backward(info, query, grads, rows, p_query, p_grad, p_rows, kv, span, share):
    squares = kv.shape[0] // (span + share)
    plen = squares * share
    widest = max(span, plen)
    pairs = GRP * span * (plen + (squares + 1) * span // 2)
    vmem = pl.BlockSpec(memory_space=pltpu.VMEM)
    return pl.pallas_call(
        functools.partial(kernel, span=span, share=share),
        out_shape=(
            jax.ShapeDtypeStruct(query.shape, BF16),
            jax.ShapeDtypeStruct(kv.shape, BF16),
            jax.ShapeDtypeStruct(p_query.shape, BF16),
        ),
        in_specs=[pl.BlockSpec(memory_space=pltpu.SMEM)] + [vmem] * 7,
        out_specs=(vmem, vmem, vmem),
        scratch_shapes=[
            pltpu.VMEM((GRP * span, HD), BF16),
            pltpu.VMEM((GRP * span, HD), BF16),
            pltpu.VMEM((widest, GRP * span), BF16),
            pltpu.VMEM((widest, GRP * span), BF16),
            pltpu.VMEM((GRP * span, HD), F32),
            pltpu.VMEM((plen, 2 * HD), BF16),
        ],
        compiler_params=pltpu.CompilerParams(vmem_limit_bytes=40 * 1024 * 1024),
        cost_estimate=pl.CostEstimate(
            flops=pairs * HD * 10, bytes_accessed=6 * 1024 * 1024, transcendentals=pairs
        ),
    )(info, query, grads, rows, p_query, p_grad, p_rows, kv)


def row_delta(grads, outputs):
    height = grads.shape[0]
    heads = grads.shape[1] // HD
    return jnp.sum(
        grads.reshape(height, heads, HD).astype(F32) * outputs.reshape(height, heads, HD).astype(F32),
        axis=2,
    )


def on_device(
    p_query, p_key, p_value, p_out, p_grad, p_lse,
    r_query, r_key, r_value, r_out, r_grad, r_lse, lengths,
):
    blocks = lax.axis_size("blk")
    rolls = lax.axis_size("roll")
    owner = lax.axis_index("blk")
    member = lax.axis_index("roll")
    squares = blocks // KVH
    square = owner // KVH
    rows = r_query.shape[1]
    span = KVH * rows
    near = [[s * KVH + m for m in range(KVH)] for s in range(squares)]
    far = [[s * KVH + m for s in range(squares)] for m in range(KVH)]
    width = GRP * HD

    def trade(block):
        return lax.all_to_all(block, "blk", 0, 0, tiled=True, axis_index_groups=near)

    own = jnp.concatenate([p_key, p_value], axis=1)
    sent = jnp.broadcast_to(own[None], (rolls,) + own.shape)
    prompt = lax.all_to_all(sent, "roll", 0, 0, tiled=True).reshape(-1, own.shape[1])
    part = prompt.shape[0]
    share = KVH * part

    both = jnp.concatenate([jnp.concatenate([r_key[0], r_value[0]], axis=1), prompt], axis=0)
    height = both.shape[0]
    both = both.reshape(height, 2, KVH, HD).transpose(2, 0, 1, 3).reshape(KVH, height, 2 * HD)
    both = trade(both)
    both = jnp.concatenate(
        [both[:, :rows].reshape(span, 2 * HD), both[:, rows:].reshape(share, 2 * HD)], axis=0
    )
    kv = lax.all_gather(both, "blk", axis=0, tiled=True, axis_index_groups=far)

    def spread(block):
        return trade(block.reshape(rows, KVH, width).transpose(1, 0, 2)).reshape(span, width)

    query = spread(r_query[0])
    grads = spread(r_grad[0])
    position = owner * rows + jnp.arange(rows)
    alive = position < lengths[0]
    lse_rows = jnp.where(alive[:, None], r_lse[0] * LOG2E, DEAD)
    delta = row_delta(r_grad[0], r_out[0])
    pair = jnp.stack([lse_rows.T.reshape(KVH, GRP, rows), delta.T.reshape(KVH, GRP, rows)], axis=1)
    pair = trade(pair.reshape(KVH, 2 * GRP, rows)).transpose(1, 0, 2).reshape(2 * GRP, span)

    there = [(m * squares + s, s * KVH + m) for m in range(KVH) for s in range(squares)]
    back = [(b, a) for a, b in there]
    p_rows = jnp.concatenate([p_lse * LOG2E, row_delta(p_grad, p_out)], axis=1).T
    p_pack = lax.ppermute(jnp.concatenate([p_query, p_grad], axis=1), "blk", there)
    p_rows = lax.ppermute(p_rows, "blk", there)

    info = jnp.stack(
        [square, (square * span < lengths[0]).astype(jnp.int32), member * p_query.shape[0]]
    ).astype(jnp.int32)
    dq, dkv, p_dq = backward(
        info, query, grads, pair, p_pack[:, :HD], p_pack[:, HD:], p_rows, kv, span, share
    )
    p_dq = lax.ppermute(p_dq, "blk", back)
    summed = lax.psum_scatter(dkv, "blk", scatter_dimension=0, tiled=True, axis_index_groups=far)
    r_dq = trade(dq.reshape(KVH, rows, width)).transpose(1, 0, 2).reshape(1, rows, KVH * width)

    summed = jnp.concatenate(
        [
            summed[:span].reshape(KVH, rows, 2 * HD),
            summed[span:].reshape(KVH, part, 2 * HD),
        ],
        axis=1,
    )
    summed = trade(summed).reshape(KVH, height, 2, HD).transpose(2, 1, 0, 3)
    summed = summed.reshape(2, height, KVH * HD)
    terms = summed[:, rows:].reshape(2, rolls, part // rolls, KVH * HD).transpose(1, 0, 2, 3)
    terms = lax.all_to_all(terms, "roll", 0, 0, tiled=True)
    total = jnp.sum(terms.astype(F32), axis=0).astype(BF16)
    return (p_dq, total[0], total[1], r_dq, summed[0, :rows][None], summed[1, :rows][None])


def solution(mesh):
    placed = (
        P("roll", "blk"),
        P(("blk", "roll"), None),
        P(("blk", "roll"), None),
        P("roll", "blk"),
        P("roll", "blk"),
        P("roll", "blk"),
        P("roll", "blk", None),
        P("roll", "blk", None),
        P("roll", "blk", None),
        P("roll", "blk", None),
        P("roll", "blk", None),
        P("roll", "blk", None),
        P("roll"),
    )
    return jax.shard_map(
        on_device,
        mesh=mesh,
        in_specs=placed,
        out_specs=(
            P("roll", "blk"),
            P(("blk", "roll"), None),
            P(("blk", "roll"), None),
            P("roll", "blk", None),
            P("roll", "blk", None),
            P("roll", "blk", None),
        ),
        check_vma=False,
    )
```

time: 1800 us -> 256 us (0.14)
  the two profiles are of different devices: /device:TPU:6 before, /device:TPU:73 now
where the time goes in v1:
time: 256 us; the launch traced here: 255 us
  waiting for transfers between devices  137 us (54%)
  starting transfers between devices  63.3 us (25%)
  Pallas kernels  18 us (7%)
  local copies, waits for them, and re-layouts  15.4 us (6%)
  between operations  15 us (6%)
  other arithmetic  6.18 us (2%)
    reduce_scatter x1, waiting for transfers between devices, on_device(): lax.psum_scatter(dkv, 'blk', scatter_dimension=0, tiled=True, axis_index_...  72.8 us
    all_gather x1, waiting for transfers between devices, on_device(): kv = lax.all_gather(both, 'blk', axis=0, tiled=True, axis_index_groups=far)  32.8 us
    all_to_all x6, starting transfers between devices, trade(): lax.all_to_all(block, 'blk', 0, 0, tiled=True, axis_index_groups=near)  25.7 us
    pallas_call x1, Pallas kernels, backward(): pl.pallas_call(functools.partial(kernel, span=span, share=share), out_sha...  18 us
    ppermute x1, starting transfers between devices, on_device(): lax.ppermute(jnp.concatenate([p_query, p_grad], axis=1), 'blk', there)  13.6 us
    ppermute x1, waiting for transfers between devices, on_device(): p_dq = lax.ppermute(p_dq, 'blk', back)  10.3 us
    all_to_all x1, starting transfers between devices, on_device(): terms = lax.all_to_all(terms, 'roll', 0, 0, tiled=True)  9.57 us
    all_to_all x6, waiting for transfers between devices, trade(): lax.all_to_all(block, 'blk', 0, 0, tiled=True, axis_index_groups=near)  8.67 us
  transfers between devices with their start and end apart: 13, of which 9 were waited for; matrix products, arithmetic and copies ran while one was open for 6% of the time, Pallas kernels for 0%

profile of v1, /device:TPU:73, one launch (start us, length us, event | category | flops | bytes accessed | tf_op | source)
XLA Modules:
  0.0 255.2 jit_solution(16952574188751361113)
XLA Ops:
  7.2 0.7 maximum_reduce_fusion
  7.9 0.5 broadcast.14
  8.4 0.8 reduce.7
  9.3 0.6 reshape.104
  9.9 6.7 %all-to-all-start.3 = ((bf16[16,2,512]{2,1,0:T(2,128)(2,1)}), bf16[16,2,512]{2,1,0:T(2,128)(2,1)S(1)}, u32[]{:S(2)}, u32[]{:S(2)}) async-start(bf16[16,2,512]{2,1,0:T(2,128)(2,1)} %reshape.104), calls=%async_computation.3 | async-start | bytes 65536 | tf_op jit(solution)/shard_map/all_to_all | solution.py:183
  17.3 1.6 multiply_bitcast_fusion
  18.8 0.3 copy.64
  19.2 0.5 reduce_sum.32
  19.8 0.6 copy_bitcast_fusion.3
  20.5 3.4 %all-to-all-done.3 = bf16[16,2,512]{2,1,0:T(2,128)(2,1)S(1)} async-done(((bf16[16,2,512]{2,1,0:T(2,128)(2,1)}), bf16[16,2,512]{2,1,0:T(2,128)(2,1)S(1)}, u32[]{:S(2)}, u32[]{:S(2)}) %all-to-all-start.3) | async-done | bytes 32800 | tf_op jit(solution)/shard_map/all_to_all | solution.py:183
  23.9 4.3 %all-to-all-start.2 = ((f32[4,16,96]{2,1,0:T(8,128)}), f32[4,16,96]{2,1,0:T(8,128)S(1)}, u32[]{:S(2)}, u32[]{:S(2)}) async-start(f32[4,16,96]{2,1,0:T(8,128)} %copy_bitcast_fusion.3), calls=%async_computation.2 | async-start | bytes 65536 | tf_op jit(solution)/shard_map/all_to_all | solution.py:179
  28.6 0.2 copy.59
  28.8 0.8 reshape.91
  29.7 1.2 all-to-all-done.2
  30.9 4.4 %all-to-all-start.4 = ((bf16[4,112,256]{2,1,0:T(8,128)(2,1)}), bf16[4,112,256]{2,1,0:T(8,128)(2,1)S(1)}, u32[]{:S(2)}, u32[]{:S(2)}) async-start(bf16[4,112,256]{2,1,0:T(8,128)(2,1)} %reshape.91), calls=%async_computation.4 | async-start | bytes 458752 | tf_op jit(solution)/shard_map/all_to_all | solution.py:179
  35.2 0.6 reshape_squeeze.8
  35.8 1.1 copy.72
  36.9 2.2 all-to-all-done.4
  39.1 3.7 %all-to-all-start = ((bf16[4,96,1024]{2,1,0:T(8,128)(2,1)}), bf16[4,96,1024]{2,1,0:T(8,128)(2,1)S(1)}, u32[]{:S(2)}, u32[]{:S(2)}) async-start(bf16[4,96,1024]{2,1,0:T(8,128)(2,1)} %bitcast.47), calls=%async_computation | async-start | bytes 1572864 | tf_op jit(solution)/shard_map/all_to_all | solution.py:179
  42.9 0.7 pad_maximum_fusion
  43.6 0.6 reshape_squeeze.9
  44.3 1.1 copy.71
  45.4 5.3 %all-to-all-done = bf16[4,96,1024]{2,1,0:T(8,128)(2,1)S(1)} async-done(((bf16[4,96,1024]{2,1,0:T(8,128)(2,1)}), bf16[4,96,1024]{2,1,0:T(8,128)(2,1)S(1)}, u32[]{:S(2)}, u32[]{:S(2)}) %all-to-all-start) | async-done | bytes 786464 | tf_op jit(solution)/shard_map/all_to_all | solution.py:179
  50.7 4.7 %all-to-all-start.1 = ((bf16[4,96,1024]{2,1,0:T(8,128)(2,1)}), bf16[4,96,1024]{2,1,0:T(8,128)(2,1)S(1)}, u32[]{:S(2)}, u32[]{:S(2)}) async-start(bf16[4,96,1024]{2,1,0:T(8,128)(2,1)} %bitcast.46), calls=%async_computation.1 | async-start | bytes 1572864 | tf_op jit(solution)/shard_map/all_to_all | solution.py:179
  55.5 13.6 %collective-permute-start = (bf16[32,256]{1,0:T(8,128)(2,1)S(1)}, bf16[32,256]{1,0:T(8,128)(2,1)S(1)}, u32[]{:S(2)}, u32[]{:S(2)}) collective-permute-start(bf16[32,256]{1,0:T(8,128)(2,1)S(1)} %pad_maximum_fusion.3), channel_id=1, source_target_pairs={{0,0},{16,64},{32,128},{48,192},{64,256},{80,320},{96,384},{112,44... | collective-permute-start | bytes 49160 | tf_op jit(solution)/shard_map/ppermute | solution.py:211
  69.2 4.1 %collective-permute-start.1 = (f32[2,32]{1,0:T(2,128)S(1)}, f32[2,32]{1,0:T(2,128)S(1)}, u32[]{:S(2)}, u32[]{:S(2)}) collective-permute-start(f32[2,32]{1,0:T(2,128)S(1)} %maximum_bitcast_fusion.1), channel_id=1, source_target_pairs={{0,0},{16,64},{32,128},{48,192},{64,256},{80,320},{96,384},{112,44... | collective-permute-start | bytes 776 | tf_op jit(solution)/shard_map/ppermute | solution.py:212
  73.5 3.5 %collective-permute-done.1.prows_ref = f32[2,32]{1,0:T(2,128)S(1)} collective-permute-done((f32[2,32]{1,0:T(2,128)S(1)}, f32[2,32]{1,0:T(2,128)S(1)}, u32[]{:S(2)}, u32[]{:S(2)}) %collective-permute-start.1) | collective-permute-done | bytes 288 | tf_op jit(solution)/shard_map/ppermute | solution.py:212
  77.1 32.8 %all-gather.2.cloned.1.call-done.kv_ref = bf16[3584,256]{1,0:T(8,128)(2,1)} async-done(((bf16[448,256]{1,0:T(8,128)(2,1)}), bf16[3584,256]{1,0:T(8,128)(2,1)}) %all-gather.2.cloned.1.call-update) | async-done | bytes 1835024 | tf_op jit(solution)/shard_map/all_gather | solution.py:194
  109.8 1.5 copy-done
  111.3 18.0 %shard_map.172 = (bf16[384,1024]{1,0:T(8,128)(2,1)}, bf16[3584,256]{1,0:T(8,128)(2,1)}, bf16[32,128]{1,0:T(8,128)(2,1)S(1)}) custom-call(s32[3]{0:T(128)S(1)} %pad_add_fusion.info, bf16[384,1024]{1,0:T(8,128)(2,1)S(1)} %bitcast.51, bf16[384,1024]{1,0:T(8,128)(2,1)S(1)} %bitcast.52, f32[16,384]{1,0:T(8,128)S(1)} %reshape.90.rows_ref, ...), custom_call_target="tpu_custom_call" | custom-call | flops 8808038400 | bytes 6291456 | tf_op jit(solution)/shard_map/pallas_call | solution.py:129
  129.4 3.5 %all-to-all-start.7 = ((bf16[4,96,1024]{2,1,0:T(8,128)(2,1)}), bf16[4,96,1024]{2,1,0:T(8,128)(2,1)S(1)}, u32[]{:S(2)}, u32[]{:S(2)}) async-start(bf16[4,96,1024]{2,1,0:T(8,128)(2,1)} %bitcast.25), calls=%async_computation.8 | async-start | bytes 1572864 | tf_op jit(solution)/shard_map/all_to_all | solution.py:179
  132.9 72.8 %reduce-scatter.2.cloned.1.call-done = bf16[448,256]{1,0:T(8,128)(2,1)} async-done(((bf16[3584,256]{1,0:T(8,128)(2,1)}), bf16[448,256]{1,0:T(8,128)(2,1)}) %reduce-scatter.2.cloned.1.call-update) | async-done | bytes 229392 | tf_op jit(solution)/shard_map/reduce_scatter | solution.py:221
  205.7 0.9 slice.50
  206.6 0.8 slice.51
  207.4 0.7 pad_maximum_fusion.1
  208.1 5.1 %all-to-all-start.5 = ((bf16[4,112,256]{2,1,0:T(8,128)(2,1)}), bf16[4,112,256]{2,1,0:T(8,128)(2,1)S(1)}, u32[]{:S(2)}, u32[]{:S(2)}) async-start(bf16[4,112,256]{2,1,0:T(8,128)(2,1)} %pad_maximum_fusion.1), calls=%async_computation.6 | async-start | bytes 458752 | tf_op jit(solution)/shard_map/all_to_all | solution.py:179
  213.2 3.7 %collective-permute-start.2 = (bf16[32,128]{1,0:T(8,128)(2,1)S(1)}, bf16[32,128]{1,0:T(8,128)(2,1)S(1)}, u32[]{:S(2)}, u32[]{:S(2)}) collective-permute-start(bf16[32,128]{1,0:T(8,128)(2,1)S(1)} %get-tuple-element.9), channel_id=1, source_target_pairs={{0,0},{64,16},{128,32},{192,48},{256,64},{320,80},{384,96},{448,11... | collective-permute-start | bytes 24584 | tf_op jit(solution)/shard_map/ppermute | solution.py:220
  216.8 10.3 %collective-permute-done.2 = bf16[32,128]{1,0:T(8,128)(2,1)S(1)} collective-permute-done((bf16[32,128]{1,0:T(8,128)(2,1)S(1)}, bf16[32,128]{1,0:T(8,128)(2,1)S(1)}, u32[]{:S(2)}, u32[]{:S(2)}) %collective-permute-start.2) | collective-permute-done | bytes 8224 | tf_op jit(solution)/shard_map/ppermute | solution.py:220
  227.2 0.6 copy.61
  227.8 1.5 reshape.100
  229.6 0.6 slice_bitcast_fusion
  230.2 9.6 %all-to-all-start.6 = ((bf16[16,2,1,512]{3,1,2,0:T(2,128)(2,1)}), bf16[16,2,1,512]{3,1,2,0:T(2,128)(2,1)S(1)}, u32[]{:S(2)}, u32[]{:S(2)}) async-start(bf16[16,2,1,512]{3,1,2,0:T(2,128)(2,1)} %slice_bitcast_fusion), calls=%async_computation.7 | async-start | bytes 65536 | tf_op jit(solution)/shard_map/all_to_all | solution.py:234
  239.8 0.3 fusion.1
  240.1 0.7 copy.62
  240.7 0.7 copy.63
  241.4 5.7 %all-to-all-done.6 = bf16[16,2,1,512]{3,1,2,0:T(2,128)(2,1)S(1)} async-done(((bf16[16,2,1,512]{3,1,2,0:T(2,128)(2,1)}), bf16[16,2,1,512]{3,1,2,0:T(2,128)(2,1)S(1)}, u32[]{:S(2)}, u32[]{:S(2)}) %all-to-all-start.6) | async-done | bytes 32800 | tf_op jit(solution)/shard_map/all_to_all | solution.py:234
  247.2 0.6 fusion.3
  247.8 0.6 copy.76
  (51 shorter events, 1.4 us)
Async XLA Ops:
  9.9 14.0 %all-to-all-start.3 = ((bf16[16,2,512]{2,1,0:T(2,128)(2,1)}), bf16[16,2,512]{2,1,0:T(2,128)(2,1)S(1)}, u32[]{:S(2)}, u32[]{:S(2)}) async-start(bf16[16,2,512]{2,1,0:T(2,128)(2,1)} %reshape.104), calls=%async_computation.3 | async-start | bytes 65536 | tf_op jit(solution)/shard_map/all_to_all | solution.py:183
  19.1 0.7 copy-start.6
  19.1 1.3 copy-start.3
  19.1 1.4 copy-start.4
  19.6 15.6 %copy-start.2 = (bf16[1,96,4096]{2,1,0:T(8,128)(2,1)S(1)}, bf16[1,96,4096]{2,1,0:T(8,128)(2,1)}, u32[]{:S(2)}) copy-start(bf16[1,96,4096]{2,1,0:T(8,128)(2,1)} %param.19) | copy-start | bytes 2359300
  23.9 6.9 %all-to-all-start.2 = ((f32[4,16,96]{2,1,0:T(8,128)}), f32[4,16,96]{2,1,0:T(8,128)S(1)}, u32[]{:S(2)}, u32[]{:S(2)}) async-start(f32[4,16,96]{2,1,0:T(8,128)} %copy_bitcast_fusion.3), calls=%async_computation.2 | async-start | bytes 65536 | tf_op jit(solution)/shard_map/all_to_all | solution.py:179
  30.9 8.2 %all-to-all-start.4 = ((bf16[4,112,256]{2,1,0:T(8,128)(2,1)}), bf16[4,112,256]{2,1,0:T(8,128)(2,1)S(1)}, u32[]{:S(2)}, u32[]{:S(2)}) async-start(bf16[4,112,256]{2,1,0:T(8,128)(2,1)} %reshape.91), calls=%async_computation.4 | async-start | bytes 458752 | tf_op jit(solution)/shard_map/all_to_all | solution.py:179
  36.9 6.7 %copy-start.1 = (bf16[1,96,4096]{2,1,0:T(8,128)(2,1)S(1)}, bf16[1,96,4096]{2,1,0:T(8,128)(2,1)}, u32[]{:S(2)}) copy-start(bf16[1,96,4096]{2,1,0:T(8,128)(2,1)} %param.23) | copy-start | bytes 2359300
  39.1 11.6 %all-to-all-start = ((bf16[4,96,1024]{2,1,0:T(8,128)(2,1)}), bf16[4,96,1024]{2,1,0:T(8,128)(2,1)S(1)}, u32[]{:S(2)}, u32[]{:S(2)}) async-start(bf16[4,96,1024]{2,1,0:T(8,128)(2,1)} %bitcast.47), calls=%async_computation | async-start | bytes 1572864 | tf_op jit(solution)/shard_map/all_to_all | solution.py:179
  42.8 67.0 %all-gather.2.cloned.1.call-start = ((), (), s32[]{:S(2)}) async-start(), calls=%async_computation.9 | async-start | bytes 2064384 | tf_op jit(solution)/shard_map/all_gather | solution.py:194
  44.2 11.2 %copy-start.5 = (bf16[32,128]{1,0:T(8,128)(2,1)S(1)}, bf16[32,128]{1,0:T(8,128)(2,1)}, u32[]{:S(2)}) copy-start(bf16[32,128]{1,0:T(8,128)(2,1)} %param.17) | copy-start | bytes 24580
  44.2 11.2 %copy-start.8 = (bf16[32,128]{1,0:T(8,128)(2,1)S(1)}, bf16[32,128]{1,0:T(8,128)(2,1)}, u32[]{:S(2)}) copy-start(bf16[32,128]{1,0:T(8,128)(2,1)} %param.13) | copy-start | bytes 24580
  44.2 24.8 %copy-start.7 = (bf16[32,128]{1,0:T(8,128)(2,1)S(1)}, bf16[32,128]{1,0:T(8,128)(2,1)}, u32[]{:S(2)}) copy-start(bf16[32,128]{1,0:T(8,128)(2,1)} %param.16) | copy-start | bytes 24580
  44.2 24.9 %copy-start.9 = (f32[32,1]{0,1:T(1,128)S(1)}, f32[32,1]{0,1:T(1,128)}, u32[]{:S(2)}) copy-start(f32[32,1]{0,1:T(1,128)} %param.18) | copy-start | bytes 388
  50.7 26.3 %all-to-all-start.1 = ((bf16[4,96,1024]{2,1,0:T(8,128)(2,1)}), bf16[4,96,1024]{2,1,0:T(8,128)(2,1)S(1)}, u32[]{:S(2)}, u32[]{:S(2)}) async-start(bf16[4,96,1024]{2,1,0:T(8,128)(2,1)} %bitcast.46), calls=%async_computation.1 | async-start | bytes 1572864 | tf_op jit(solution)/shard_map/all_to_all | solution.py:179
  55.4 150.2 %reduce-scatter.2.cloned.1.call-start = ((), (), s32[]{:S(2)}) async-start(), calls=%async_computation.10 | async-start | bytes 2064384 | tf_op jit(solution)/shard_map/reduce_scatter | solution.py:221
  55.5 17.9 %collective-permute-start = (bf16[32,256]{1,0:T(8,128)(2,1)S(1)}, bf16[32,256]{1,0:T(8,128)(2,1)S(1)}, u32[]{:S(2)}, u32[]{:S(2)}) collective-permute-start(bf16[32,256]{1,0:T(8,128)(2,1)S(1)} %pad_maximum_fusion.3), channel_id=1, source_target_pairs={{0,0},{16,64},{32,128},{48,192},{64,256},{80,320},{96,384},{112,44... | collective-permute-start | bytes 49160 | tf_op jit(solution)/shard_map/ppermute | solution.py:211
  69.2 7.8 %collective-permute-start.1 = (f32[2,32]{1,0:T(2,128)S(1)}, f32[2,32]{1,0:T(2,128)S(1)}, u32[]{:S(2)}, u32[]{:S(2)}) collective-permute-start(f32[2,32]{1,0:T(2,128)S(1)} %maximum_bitcast_fusion.1), channel_id=1, source_target_pairs={{0,0},{16,64},{32,128},{48,192},{64,256},{80,320},{96,384},{112,44... | collective-permute-start | bytes 776 | tf_op jit(solution)/shard_map/ppermute | solution.py:212
  109.8 1.5 copy-start
  129.4 78.7 %all-to-all-start.7 = ((bf16[4,96,1024]{2,1,0:T(8,128)(2,1)}), bf16[4,96,1024]{2,1,0:T(8,128)(2,1)S(1)}, u32[]{:S(2)}, u32[]{:S(2)}) async-start(bf16[4,96,1024]{2,1,0:T(8,128)(2,1)} %bitcast.25), calls=%async_computation.8 | async-start | bytes 1572864 | tf_op jit(solution)/shard_map/all_to_all | solution.py:179
  208.1 21.2 %all-to-all-start.5 = ((bf16[4,112,256]{2,1,0:T(8,128)(2,1)}), bf16[4,112,256]{2,1,0:T(8,128)(2,1)S(1)}, u32[]{:S(2)}, u32[]{:S(2)}) async-start(bf16[4,112,256]{2,1,0:T(8,128)(2,1)} %pad_maximum_fusion.1), calls=%async_computation.6 | async-start | bytes 458752 | tf_op jit(solution)/shard_map/all_to_all | solution.py:179
  213.2 14.0 %collective-permute-start.2 = (bf16[32,128]{1,0:T(8,128)(2,1)S(1)}, bf16[32,128]{1,0:T(8,128)(2,1)S(1)}, u32[]{:S(2)}, u32[]{:S(2)}) collective-permute-start(bf16[32,128]{1,0:T(8,128)(2,1)S(1)} %get-tuple-element.9), channel_id=1, source_target_pairs={{0,0},{64,16},{128,32},{192,48},{256,64},{320,80},{384,96},{448,11... | collective-permute-start | bytes 24584 | tf_op jit(solution)/shard_map/ppermute | solution.py:220
  230.2 16.9 %all-to-all-start.6 = ((bf16[16,2,1,512]{3,1,2,0:T(2,128)(2,1)}), bf16[16,2,1,512]{3,1,2,0:T(2,128)(2,1)S(1)}, u32[]{:S(2)}, u32[]{:S(2)}) async-start(bf16[16,2,1,512]{3,1,2,0:T(2,128)(2,1)} %slice_bitcast_fusion), calls=%async_computation.7 | async-start | bytes 65536 | tf_op jit(solution)/shard_map/all_to_all | solution.py:234
Sparse Core Ops, SparseCore 0:
  45.7 64.0 all-gather.1
  129.5 76.1 reduce-scatter.1

commit v2 on v1

v2 whole, which is shorter than its diff:
```python
import functools

import jax
import jax.numpy as jnp
from jax import lax
from jax.experimental import pallas as pl
from jax.experimental.pallas import tpu as pltpu
from jax.sharding import PartitionSpec as P

KVH = 4
HD = 128
GRP = 8
SCALE = HD ** (-0.5)
LOG2E = 1.4426950408889634
DEAD = 1e30

F32 = jnp.float32
BF16 = jnp.bfloat16
NN = (((1,), (0,)), ((), ()))
NT = (((1,), (1,)), ((), ()))
TN = (((0,), (0,)), ((), ()))


def dot(left, right, dims):
    return lax.dot_general(left, right, dims, preferred_element_type=F32)


def weigh(keys, values, query, grads, lse_row, delta_row, keep):
    scores = dot(keys, query, NT)
    dprobs = dot(values, grads, NT)
    probs = jnp.exp2(scores * (SCALE * LOG2E) - lse_row)
    if keep is not None:
        probs = jnp.where(keep, probs, 0.0)
    dscores = (probs * (dprobs - delta_row)).astype(BF16)
    return probs.astype(BF16), dscores


def terms(refs, keys, values, at, keep, acc):
    q_ref, g_ref, rows_ref = refs
    weights, dscores = weigh(
        keys, values, q_ref[at, :], g_ref[at, :], rows_ref[0:1, at], rows_ref[1:2, at], keep
    )
    acc[:, at] += dot(keys.T, dscores, NN)
    return dot(dscores, q_ref[at, :], NN), dot(weights, g_ref[at, :], NN)


def own_kernel(info, q_ref, g_ref, rows_ref, spot_ref, kv_ref, d_ref, acc):
    live = info[1]
    chunk = kv_ref.shape[0] // KVH
    group = q_ref.shape[0] // KVH
    acc[...] = jnp.zeros_like(acc)
    d_ref[...] = jnp.zeros_like(d_ref)

    @pl.when(live != 0)
    def _():
        for c in range(KVH):
            reach = (c + 1) * chunk
            place = lax.broadcasted_iota(jnp.int32, (reach, group), 0)
            dk, dv = terms(
                (q_ref, g_ref, rows_ref), kv_ref[0:reach, 0:HD], kv_ref[0:reach, HD : 2 * HD],
                slice(c * group, (c + 1) * group), place <= spot_ref[...] + c * chunk, acc,
            )
            d_ref[0:reach, 0:HD] += dk * SCALE
            d_ref[0:reach, HD : 2 * HD] += dv


def lower_kernel(info, q_ref, g_ref, rows_ref, kv_ref, dq_in, d_ref, dq_ref, acc, *, span):
    square, live = info[0], info[1]
    squares = kv_ref.shape[0] // span
    columns = q_ref.shape[0]
    group = columns // KVH
    acc[...] = dq_in[...]
    used = jnp.where(live != 0, square, 0)

    def whole(j, carry):
        block = pl.ds(pl.multiple_of(j * span, 16), span)
        keys, values = kv_ref[block, 0:HD], kv_ref[block, HD : 2 * HD]
        dkeys = dvalues = 0.0
        for c in range(0, columns, 2 * group):
            dk, dv = terms((q_ref, g_ref, rows_ref), keys, values, slice(c, c + 2 * group), None, acc)
            dkeys, dvalues = dkeys + dk, dvalues + dv
        d_ref[block, 0:HD] = (dkeys * SCALE).astype(BF16)
        d_ref[block, HD : 2 * HD] = dvalues.astype(BF16)
        return carry

    def empty(j, carry):
        d_ref[pl.ds(pl.multiple_of(j * span, 16), span), :] = jnp.zeros((span, 2 * HD), BF16)
        return carry

    lax.fori_loop(0, used, whole, 0)
    lax.fori_loop(used, squares, empty, 0)
    dq_ref[...] = (acc[...].T * SCALE).astype(BF16)


def prompt_kernel(
    info, q_ref, g_ref, rows_ref, pq_ref, pg_ref, prows_ref, kv_ref, dq_in,
    d_ref, dq_ref, pdq_ref, acc, total,
    *, blocks,
):
    live, start = info[1], info[2]
    columns = q_ref.shape[0]
    group = columns // KVH
    plen = kv_ref.shape[0]
    rolls = plen // blocks
    acc[...] = dq_in[...]
    keys, values = kv_ref[:, 0:HD], kv_ref[:, HD : 2 * HD]
    shape = (plen, pq_ref.shape[0])
    index = lax.broadcasted_iota(jnp.int32, shape, 0)
    place = lax.rem(index, blocks) * rolls + lax.div(index, blocks)
    row = lax.broadcasted_iota(jnp.int32, shape, 1) + start
    weights, dscores = weigh(
        keys, values, pq_ref[...], pg_ref[...], prows_ref[0:1, :], prows_ref[1:2, :], place <= row
    )
    pdq_ref[...] = (dot(dscores, keys, TN) * SCALE).astype(BF16)
    total[:, 0:HD] = dot(dscores, pq_ref[...], NN)
    total[:, HD : 2 * HD] = dot(weights, pg_ref[...], NN)

    @pl.when(live != 0)
    def _():
        for c in range(0, columns, 2 * group):
            at = slice(c, c + 2 * group)
            dk, dv = terms((q_ref, g_ref, rows_ref), keys, values, at, None, acc)
            total[:, 0:HD] += dk
            total[:, HD : 2 * HD] += dv

    d_ref[:, 0:HD] = (total[:, 0:HD] * SCALE).astype(BF16)
    d_ref[:, HD : 2 * HD] = total[:, HD : 2 * HD].astype(BF16)
    dq_ref[...] = acc[...]


def call(body, info, operands, outs, scratch, pairs):
    vmem = pl.BlockSpec(memory_space=pltpu.VMEM)
    return pl.pallas_call(
        body,
        out_shape=outs,
        in_specs=[pl.BlockSpec(memory_space=pltpu.SMEM)] + [vmem] * len(operands),
        out_specs=(vmem,) * len(outs),
        scratch_shapes=scratch,
        compiler_params=pltpu.CompilerParams(vmem_limit_bytes=40 * 1024 * 1024),
        cost_estimate=pl.CostEstimate(
            flops=pairs * HD * 10, bytes_accessed=4 * 1024 * 1024, transcendentals=pairs
        ),
    )(info, *operands)


def own_backward(info, fixed, spot, block):
    turned = fixed[0].shape[::-1]
    return call(
        own_kernel,
        info,
        (*fixed, spot, block),
        (jax.ShapeDtypeStruct(block.shape, F32), jax.ShapeDtypeStruct(turned, F32)),
        [],
        turned[1] * block.shape[0] * 5 // 8,
    )


def lower_backward(info, fixed, kv, carried, span):
    turned = carried.shape
    return call(
        functools.partial(lower_kernel, span=span),
        info,
        (*fixed, kv, carried),
        (jax.ShapeDtypeStruct(kv.shape, BF16), jax.ShapeDtypeStruct(turned[::-1], BF16)),
        [pltpu.VMEM(turned, F32)],
        turned[1] * kv.shape[0],
    )


def prompt_backward(info, fixed, prompt_rows, kv, carried, blocks):
    turned = carried.shape
    return call(
        functools.partial(prompt_kernel, blocks=blocks),
        info,
        (*fixed, *prompt_rows, kv, carried),
        (
            jax.ShapeDtypeStruct(kv.shape, BF16),
            jax.ShapeDtypeStruct(turned, F32),
            jax.ShapeDtypeStruct(prompt_rows[0].shape, BF16),
        ),
        [pltpu.VMEM(turned, F32), pltpu.VMEM(kv.shape, F32)],
        turned[1] * kv.shape[0],
    )


def row_delta(grads, outputs):
    height = grads.shape[0]
    heads = grads.shape[1] // HD
    return jnp.sum(
        grads.reshape(height, heads, HD).astype(F32) * outputs.reshape(height, heads, HD).astype(F32),
        axis=2,
    )


def on_device(
    p_query, p_key, p_value, p_out, p_grad, p_lse,
    r_query, r_key, r_value, r_out, r_grad, r_lse, lengths,
):
    blocks = lax.axis_size("blk")
    rolls = lax.axis_size("roll")
    owner = lax.axis_index("blk")
    member = lax.axis_index("roll")
    squares = blocks // KVH
    square = owner // KVH
    rows = r_query.shape[1]
    span = KVH * rows
    near = [[s * KVH + m for m in range(KVH)] for s in range(squares)]

    far = [[s * KVH + m for s in range(squares)] for m in range(KVH)]
    part = p_key.shape[0]

    def trade(block):
        return lax.all_to_all(block, "blk", 0, 0, tiled=True, axis_index_groups=near)

    def together(*arrays):
        return lax.optimization_barrier(arrays)

    both = jnp.concatenate(
        [jnp.concatenate([r_key[0], r_value[0]], axis=1), jnp.concatenate([p_key, p_value], axis=1)]
    )
    height = rows + part
    both = both.reshape(height, 2, KVH, HD).transpose(2, 0, 1, 3).reshape(KVH, height, 2 * HD)
    both = trade(both)
    mine = both[:, :rows].reshape(span, 2 * HD)
    prompt = both[:, rows:].reshape(KVH * part, 2 * HD)

    kv = lax.all_gather(mine, "blk", axis=0, tiled=True, axis_index_groups=far)
    r_query, r_grad, r_lse, prompt, mine = together(r_query, r_grad, r_lse, prompt, mine)

    def heads_first(block):
        heads = block.reshape(rows, KVH, GRP, HD).transpose(1, 2, 0, 3)
        return heads.reshape(KVH, GRP * rows, HD)

    query = trade(heads_first(r_query[0])).reshape(KVH * GRP * rows, HD)
    grads = trade(heads_first(r_grad[0])).reshape(KVH * GRP * rows, HD)
    position = owner * rows + jnp.arange(rows)
    alive = position < lengths[0]
    lse_rows = jnp.where(alive[:, None], r_lse[0] * LOG2E, DEAD)
    delta = row_delta(r_grad[0], r_out[0])
    pair = jnp.stack([lse_rows.T.reshape(KVH, GRP, rows), delta.T.reshape(KVH, GRP, rows)], axis=1)
    pair = trade(pair.reshape(KVH, 2 * GRP, rows)).reshape(KVH, 2, GRP * rows)
    pair = pair.transpose(1, 0, 2).reshape(2, KVH * GRP * rows)

    prompt = jnp.broadcast_to(prompt[None], (squares,) + prompt.shape)
    prompt = lax.all_to_all(prompt, "blk", 0, 0, tiled=True, axis_index_groups=far)
    prompt = prompt.reshape(blocks * part, 2 * HD)
    prompt = jnp.broadcast_to(prompt[None], (rolls,) + prompt.shape)
    prompt = lax.all_to_all(prompt, "roll", 0, 0, tiled=True).reshape(-1, 2 * HD)
    prompt = prompt.reshape(rolls, blocks, part, 2 * HD).transpose(0, 2, 1, 3).reshape(-1, 2 * HD)

    there = [(m * squares + s, s * KVH + m) for m in range(KVH) for s in range(squares)]
    back = [(b, a) for a, b in there]
    p_rows = jnp.concatenate([p_lse * LOG2E, row_delta(p_grad, p_out)], axis=1).T
    p_pack = lax.ppermute(jnp.concatenate([p_query, p_grad], axis=1), "blk", there)
    p_rows = lax.ppermute(p_rows, "blk", there)
    prompt_rows = (p_pack[:, :HD], p_pack[:, HD:], p_rows)

    info = jnp.stack(
        [square, square * span < lengths[0], member * p_query.shape[0], squares]
    ).astype(jnp.int32)
    spot = jnp.tile(jnp.arange(rows, dtype=jnp.int32), GRP)[None]
    fixed = (query, grads, pair)

    own, dq = own_backward(info, fixed, spot, mine)
    prompt_terms, dq, p_dq = prompt_backward(info, fixed, prompt_rows, prompt, dq, blocks)
    lower, dq = lower_backward(info, fixed, kv, dq, span)
    lower = lax.psum_scatter(lower, "blk", scatter_dimension=0, tiled=True, axis_index_groups=far)
    summed = (own + lower.astype(F32)).astype(BF16)

    prompt_terms = prompt_terms.reshape(rolls, part, blocks, 2 * HD).transpose(0, 2, 1, 3)
    prompt_terms = lax.all_to_all(prompt_terms.reshape(rolls, blocks * part, 2 * HD), "roll", 0, 0, tiled=True)
    prompt_terms = jnp.sum(prompt_terms.astype(F32), axis=0).astype(BF16)
    prompt_terms = lax.all_to_all(
        prompt_terms.reshape(squares, KVH * part, 2 * HD), "blk", 0, 0, tiled=True, axis_index_groups=far
    )
    prompt_terms = jnp.sum(prompt_terms.astype(F32), axis=0).astype(BF16)

    p_dq = lax.ppermute(p_dq, "blk", back)
    r_dq = trade(dq.reshape(KVH, GRP * rows, HD)).reshape(KVH, GRP, rows, HD)
    summed, r_dq, p_dq = together(summed, r_dq, p_dq)
    r_dq = r_dq.transpose(2, 0, 1, 3).reshape(1, rows, KVH * GRP * HD)

    summed = jnp.concatenate(
        [summed.reshape(KVH, rows, 2 * HD), prompt_terms.reshape(KVH, part, 2 * HD)], axis=1
    )
    summed = trade(summed).reshape(KVH, height, 2, HD).transpose(2, 1, 0, 3)
    summed = summed.reshape(2, height, KVH * HD)
    return (
        p_dq, summed[0, rows:], summed[1, rows:],
        r_dq, summed[0, :rows][None], summed[1, :rows][None],
    )


def solution(mesh):
    placed = (
        P("roll", "blk"),
        P(("blk", "roll"), None),
        P(("blk", "roll"), None),
        P("roll", "blk"),
        P("roll", "blk"),
        P("roll", "blk"),
        P("roll", "blk", None),
        P("roll", "blk", None),
        P("roll", "blk", None),
        P("roll", "blk", None),
        P("roll", "blk", None),
        P("roll", "blk", None),
        P("roll"),
    )
    return jax.shard_map(
        on_device,
        mesh=mesh,
        in_specs=placed,
        out_specs=(
            P("roll", "blk"),
            P(("blk", "roll"), None),
            P(("blk", "roll"), None),
            P("roll", "blk", None),
            P("roll", "blk", None),
            P("roll", "blk", None),
        ),
        check_vma=False,
    )
```

time: 256 us -> 227 us (0.89)
  the two profiles are of different devices: /device:TPU:73 before, /device:TPU:6 now
where the time goes in v2:
time: 227 us; the launch traced here: 226 us
  waiting for transfers between devices  83.1 us (37%)
  blocking collectives  49 us (22%)
  starting transfers between devices  45.2 us (20%)
  local copies, waits for them, and re-layouts  17.6 us (8%)
  between operations  15.1 us (7%)
  Pallas kernels  11.2 us (5%)
  other arithmetic  4.34 us (2%)
    all_to_all x1, blocking collectives, on_device(): lax.all_to_all(prompt_terms.reshape(squares, KVH * part, 2 * HD), 'blk',...  36.1 us
    all_gather x1, waiting for transfers between devices, on_device(): kv = lax.all_gather(mine, 'blk', axis=0, tiled=True, axis_index_groups=far)  24 us
    all_to_all x6, waiting for transfers between devices, trade(): lax.all_to_all(block, 'blk', 0, 0, tiled=True, axis_index_groups=near)  23.9 us
    all_to_all x6, starting transfers between devices, trade(): lax.all_to_all(block, 'blk', 0, 0, tiled=True, axis_index_groups=near)  21.5 us
    reduce_scatter x1, waiting for transfers between devices, on_device(): lax.psum_scatter(lower, 'blk', scatter_dimension=0, tiled=True, axis_inde...  21.4 us
    all_to_all x1, starting transfers between devices, on_device(): lax.all_to_all(prompt, 'blk', 0, 0, tiled=True, axis_index_groups=far)  14.2 us
    all_to_all x1, blocking collectives, on_device(): lax.all_to_all(prompt_terms.reshape(rolls, blocks * part, 2 * HD), 'roll'...  12.9 us
    pallas_call x3, Pallas kernels, call(): pl.pallas_call(body, out_shape=outs, in_specs=[pl.BlockSpec(memory_space=...  11.2 us
  transfers between devices with their start and end apart: 13, of which 9 were waited for; matrix products, arithmetic and copies ran while one was open for 4% of the time, Pallas kernels for 4%

profile of v2, /device:TPU:6, one launch (start us, length us, event | category | flops | bytes accessed | tf_op | source)
XLA Modules:
  0.0 225.5 jit_solution(18280684387902885722)
XLA Ops:
  7.2 1.1 maximum_maximum_fusion
  8.7 0.7 copy.71
  9.4 4.2 %all-to-all-start = ((bf16[4,97,256]{2,1,0:T(8,128)(2,1)}), bf16[4,97,256]{2,1,0:T(8,128)(2,1)S(1)}, u32[]{:S(2)}, u32[]{:S(2)}) async-start(bf16[4,97,256]{2,1,0:T(8,128)(2,1)} %copy.71), calls=%async_computation | async-start | bytes 425984 | tf_op jit(solution)/shard_map/all_to_all | solution.py:213
  14.3 4.6 %all-to-all-done = bf16[4,97,256]{2,1,0:T(8,128)(2,1)S(1)} async-done(((bf16[4,97,256]{2,1,0:T(8,128)(2,1)}), bf16[4,97,256]{2,1,0:T(8,128)(2,1)S(1)}, u32[]{:S(2)}, u32[]{:S(2)}) %all-to-all-start) | async-done | bytes 198688 | tf_op jit(solution)/shard_map/all_to_all | solution.py:213
  18.9 0.7 slice.33
  19.6 0.6 broadcast_in_dim.28
  20.2 14.2 %all-to-all-start.4 = ((bf16[8,4,256]{2,1,0:T(4,128)(2,1)}), bf16[8,4,256]{2,1,0:T(4,128)(2,1)S(1)}, u32[]{:S(2)}, u32[]{:S(2)}) async-start(bf16[8,4,256]{2,1,0:T(4,128)(2,1)} %broadcast_in_dim.28), calls=%async_computation.4 | async-start | bytes 32768 | tf_op jit(solution)/shard_map/all_to_all | solution.py:245
  34.9 0.5 reduce_sum.44
  35.6 0.6 copy_bitcast_fusion.3
  36.3 10.8 %all-to-all-done.4 = bf16[8,4,256]{2,1,0:T(4,128)(2,1)S(1)} async-done(((bf16[8,4,256]{2,1,0:T(4,128)(2,1)}), bf16[8,4,256]{2,1,0:T(4,128)(2,1)S(1)}, u32[]{:S(2)}, u32[]{:S(2)}) %all-to-all-start.4) | async-done | bytes 16416 | tf_op jit(solution)/shard_map/all_to_all | solution.py:245
  47.0 3.3 %all-to-all-start.3 = ((f32[4,16,96]{2,1,0:T(8,128)}), f32[4,16,96]{2,1,0:T(8,128)S(1)}, u32[]{:S(2)}, u32[]{:S(2)}) async-start(f32[4,16,96]{2,1,0:T(8,128)} %copy_bitcast_fusion.3), calls=%async_computation.3 | async-start | bytes 65536 | tf_op jit(solution)/shard_map/all_to_all | solution.py:213
  50.5 1.2 copy.72
  51.6 3.4 %all-to-all-done.3 = f32[4,16,96]{2,1,0:T(8,128)S(1)} async-done(((f32[4,16,96]{2,1,0:T(8,128)}), f32[4,16,96]{2,1,0:T(8,128)S(1)}, u32[]{:S(2)}, u32[]{:S(2)}) %all-to-all-start.3) | async-done | bytes 24608 | tf_op jit(solution)/shard_map/all_to_all | solution.py:213
  55.0 3.5 %all-to-all-start.1 = ((bf16[4,768,128]{2,1,0:T(8,128)(2,1)}), bf16[4,768,128]{2,1,0:T(8,128)(2,1)S(1)}, u32[]{:S(2)}, u32[]{:S(2)}) async-start(bf16[4,768,128]{2,1,0:T(8,128)(2,1)} %bitcast.9), calls=%async_computation.1 | async-start | bytes 1572864 | tf_op jit(solution)/shard_map/all_to_all | solution.py:213
  58.7 1.2 copy.73
  59.9 6.6 %all-to-all-done.1 = bf16[4,768,128]{2,1,0:T(8,128)(2,1)S(1)} async-done(((bf16[4,768,128]{2,1,0:T(8,128)(2,1)}), bf16[4,768,128]{2,1,0:T(8,128)(2,1)S(1)}, u32[]{:S(2)}, u32[]{:S(2)}) %all-to-all-start.1) | async-done | bytes 786464 | tf_op jit(solution)/shard_map/all_to_all | solution.py:213
  66.5 3.5 %all-to-all-start.2 = ((bf16[4,768,128]{2,1,0:T(8,128)(2,1)}), bf16[4,768,128]{2,1,0:T(8,128)(2,1)S(1)}, u32[]{:S(2)}, u32[]{:S(2)}) async-start(bf16[4,768,128]{2,1,0:T(8,128)(2,1)} %bitcast.12), calls=%async_computation.2 | async-start | bytes 1572864 | tf_op jit(solution)/shard_map/all_to_all | solution.py:213
  70.0 0.7 all-gather.2.cloned.1.call-update
  70.9 0.7 collective-permute-start.1
  71.6 0.7 collective-permute-start
  72.5 5.7 %all-to-all-done.2 = bf16[4,768,128]{2,1,0:T(8,128)(2,1)S(1)} async-done(((bf16[4,768,128]{2,1,0:T(8,128)(2,1)}), bf16[4,768,128]{2,1,0:T(8,128)(2,1)S(1)}, u32[]{:S(2)}, u32[]{:S(2)}) %all-to-all-start.2) | async-done | bytes 786464 | tf_op jit(solution)/shard_map/all_to_all | solution.py:213
  78.2 0.7 broadcast_in_dim.30
  78.9 7.4 %all-to-all-start.5 = ((bf16[16,32,256]{2,1,0:T(8,128)(2,1)}), bf16[16,32,256]{2,1,0:T(8,128)(2,1)S(1)}, u32[]{:S(2)}, u32[]{:S(2)}) async-start(bf16[16,32,256]{2,1,0:T(8,128)(2,1)} %broadcast_in_dim.30), calls=%async_computation.5 | async-start | bytes 524288 | tf_op jit(solution)/shard_map/all_to_all | solution.py:248
  86.5 3.7 %shard_map.172 = (f32[384,256]{1,0:T(8,128)S(1)}, f32[128,3072]{1,0:T(8,128)S(1)}) custom-call(s32[4]{0:T(128)S(1)} %pad_add_fusion.info, bf16[3072,128]{1,0:T(8,128)(2,1)S(1)} %bitcast.75, bf16[3072,128]{1,0:T(8,128)(2,1)S(1)} %bitcast.78, f32[2,3072]{1,0:T(2,128)S(1)} %bitcast.85, s32[1,768]{1,0:T(1,128)S(1)} %broadcast_in_dim_tile.3.spot_ref, ...), custom_call_target="tpu_custom_call" | custom-call | flops 943718400 | bytes 4194304 | tf_op jit(solution)/shard_map/pallas_call | solution.py:133
  90.2 1.1 copy-done.2
  91.4 2.3 %all-to-all-done.5 = bf16[16,32,256]{2,1,0:T(8,128)(2,1)S(1)} async-done(((bf16[16,32,256]{2,1,0:T(8,128)(2,1)}), bf16[16,32,256]{2,1,0:T(8,128)(2,1)S(1)}, u32[]{:S(2)}, u32[]{:S(2)}) %all-to-all-start.5) | async-done | bytes 262176 | tf_op jit(solution)/shard_map/all_to_all | solution.py:248
  93.7 1.4 copy-done.3
  95.1 5.2 %shard_map.173 = (bf16[512,256]{1,0:T(8,128)(2,1)S(1)}, f32[128,3072]{1,0:T(8,128)S(1)}, bf16[32,128]{1,0:T(8,128)(2,1)S(1)}) custom-call(s32[4]{0:T(128)S(1)} %pad_add_fusion.info, bf16[3072,128]{1,0:T(8,128)(2,1)S(1)} %bitcast.76, bf16[3072,128]{1,0:T(8,128)(2,1)S(1)} %bitcast.79, f32[2,3072]{1,0:T(2,128)S(1)} %bitcast.86, ...), custom_call_target="tpu_custom_call" | custom-call | flops 2013265920 | bytes 4194304 | tf_op jit(solution)/shard_map/pallas_call | solution.py:133
  100.3 1.1 copy-done.4
  101.4 24.0 %all-gather.2.cloned.1.call-done.kv_ref = bf16[3072,256]{1,0:T(8,128)(2,1)} async-done(((bf16[384,256]{1,0:T(8,128)(2,1)}), bf16[3072,256]{1,0:T(8,128)(2,1)}) %all-gather.2.cloned.1.call-update) | async-done | bytes 1572880 | tf_op jit(solution)/shard_map/all_gather | solution.py:227
  125.4 1.4 copy-done.1
  126.8 1.4 copy-done.5
  128.2 2.3 %shard_map.174 = (bf16[3072,256]{1,0:T(8,128)(2,1)}, bf16[3072,128]{1,0:T(8,128)(2,1)}) custom-call(s32[4]{0:T(128)S(1)} %pad_add_fusion.info, bf16[3072,128]{1,0:T(8,128)(2,1)S(1)} %bitcast.77, bf16[3072,128]{1,0:T(8,128)(2,1)S(1)} %bitcast.80, f32[2,3072]{1,0:T(2,128)S(1)} %bitcast.87, bf16[3072,256]{1,0:T(8,128)(2,1)S(1)} %copy-done.1, ...), custom_call_target="tpu_custom_call" | custom-call | flops 12079595520 | bytes 4194304 | tf_op jit(solution)/shard_map/pallas_call | solution.py:133
  130.6 12.9 %all_to_all.50 = bf16[16,32,256]{2,1,0:T(8,128)(2,1)S(1)} all-to-all(bf16[16,32,256]{2,1,0:T(8,128)(2,1)S(1)} %bitcast.84), channel_id=1, replica_groups=mesh['blk'=32,'roll'=16] {'roll'}, dimensions={0} | all-to-all | bytes 524288 | tf_op jit(solution)/shard_map/all_to_all | solution.py:271
  143.6 36.1 %all_to_all.51 = bf16[8,4,256]{2,1,0:T(4,128)(2,1)S(1)} all-to-all(bf16[8,4,256]{2,1,0:T(4,128)(2,1)S(1)} %reshape.101), channel_id=1, replica_groups={{0,64,128,192,256,320,384,448},{16,80,144,208,272,336,400,464},{32,96,1..., dimensions={0} | all-to-all | bytes 32768 | tf_op jit(solution)/shard_map/all_to_all | solution.py:273
  179.6 3.5 %all-to-all-start.6 = ((bf16[4,768,128]{2,1,0:T(8,128)(2,1)}), bf16[4,768,128]{2,1,0:T(8,128)(2,1)S(1)}, u32[]{:S(2)}, u32[]{:S(2)}) async-start(bf16[4,768,128]{2,1,0:T(8,128)(2,1)} %bitcast.26), calls=%async_computation.7 | async-start | bytes 1572864 | tf_op jit(solution)/shard_map/all_to_all | solution.py:213
  183.1 0.7 collective-permute-start.2
  183.8 21.4 %reduce-scatter.2.cloned.1.call-done = bf16[384,256]{1,0:T(8,128)(2,1)} async-done(((bf16[3072,256]{1,0:T(8,128)(2,1)}), bf16[384,256]{1,0:T(8,128)(2,1)}) %reduce-scatter.2.cloned.1.call-update) | async-done | bytes 196624 | tf_op jit(solution)/shard_map/reduce_scatter | solution.py:267
  205.2 1.0 add_convert_fusion
  206.2 0.7 pad_maximum_fusion
  206.9 3.5 %all-to-all-start.9 = ((bf16[4,97,256]{2,1,0:T(8,128)(2,1)}), bf16[4,97,256]{2,1,0:T(8,128)(2,1)S(1)}, u32[]{:S(2)}, u32[]{:S(2)}) async-start(bf16[4,97,256]{2,1,0:T(8,128)(2,1)} %pad_maximum_fusion), calls=%async_computation.10 | async-start | bytes 425984 | tf_op jit(solution)/shard_map/all_to_all | solution.py:213
  210.4 0.3 copy.93
  210.7 1.2 reshape.105
  212.0 3.7 %all-to-all-done.9 = bf16[4,97,256]{2,1,0:T(8,128)(2,1)S(1)} async-done(((bf16[4,97,256]{2,1,0:T(8,128)(2,1)}), bf16[4,97,256]{2,1,0:T(8,128)(2,1)S(1)}, u32[]{:S(2)}, u32[]{:S(2)}) %all-to-all-start.9) | async-done | bytes 198688 | tf_op jit(solution)/shard_map/all_to_all | solution.py:213
  215.9 0.6 slice_bitcast_fusion
  216.8 0.7 copy.81
  217.4 0.7 copy.80
  218.1 0.6 copy.99
  (59 shorter events, 2.6 us)
Async XLA Ops:
  7.2 27.3 %copy-start.6 = (bf16[1,96,4096]{2,1,0:T(8,128)(2,1)S(1)}, bf16[1,96,4096]{2,1,0:T(8,128)(2,1)}, u32[]{:S(2)}) copy-start(bf16[1,96,4096]{2,1,0:T(8,128)(2,1)} %param.23) | copy-start | bytes 2359300
  7.2 27.3 %copy-start.8 = (bf16[1,96,4096]{2,1,0:T(8,128)(2,1)S(1)}, bf16[1,96,4096]{2,1,0:T(8,128)(2,1)}, u32[]{:S(2)}) copy-start(bf16[1,96,4096]{2,1,0:T(8,128)(2,1)} %param.22) | copy-start | bytes 2359300
  9.4 9.4 %all-to-all-start = ((bf16[4,97,256]{2,1,0:T(8,128)(2,1)}), bf16[4,97,256]{2,1,0:T(8,128)(2,1)S(1)}, u32[]{:S(2)}, u32[]{:S(2)}) async-start(bf16[4,97,256]{2,1,0:T(8,128)(2,1)} %copy.71), calls=%async_computation | async-start | bytes 425984 | tf_op jit(solution)/shard_map/all_to_all | solution.py:213
  20.2 26.8 %all-to-all-start.4 = ((bf16[8,4,256]{2,1,0:T(4,128)(2,1)}), bf16[8,4,256]{2,1,0:T(4,128)(2,1)S(1)}, u32[]{:S(2)}, u32[]{:S(2)}) async-start(bf16[8,4,256]{2,1,0:T(4,128)(2,1)} %broadcast_in_dim.28), calls=%async_computation.4 | async-start | bytes 32768 | tf_op jit(solution)/shard_map/all_to_all | solution.py:245
  34.9 0.7 copy-start.10
  34.9 15.4 %copy-start.7 = (bf16[1,96,4096]{2,1,0:T(8,128)(2,1)S(1)}, bf16[1,96,4096]{2,1,0:T(8,128)(2,1)}, u32[]{:S(2)}) copy-start(bf16[1,96,4096]{2,1,0:T(8,128)(2,1)} %param.19) | copy-start | bytes 2359300
  47.0 8.0 %all-to-all-start.3 = ((f32[4,16,96]{2,1,0:T(8,128)}), f32[4,16,96]{2,1,0:T(8,128)S(1)}, u32[]{:S(2)}, u32[]{:S(2)}) async-start(f32[4,16,96]{2,1,0:T(8,128)} %copy_bitcast_fusion.3), calls=%async_computation.3 | async-start | bytes 65536 | tf_op jit(solution)/shard_map/all_to_all | solution.py:213
  55.0 11.5 %all-to-all-start.1 = ((bf16[4,768,128]{2,1,0:T(8,128)(2,1)}), bf16[4,768,128]{2,1,0:T(8,128)(2,1)S(1)}, u32[]{:S(2)}, u32[]{:S(2)}) async-start(bf16[4,768,128]{2,1,0:T(8,128)(2,1)} %bitcast.9), calls=%async_computation.1 | async-start | bytes 1572864 | tf_op jit(solution)/shard_map/all_to_all | solution.py:213
  58.7 12.1 %copy-start.9 = (bf16[32,128]{1,0:T(8,128)(2,1)S(1)}, bf16[32,128]{1,0:T(8,128)(2,1)}, u32[]{:S(2)}) copy-start(bf16[32,128]{1,0:T(8,128)(2,1)} %param.17) | copy-start | bytes 24580
  58.7 12.1 %copy-start.11 = (bf16[32,128]{1,0:T(8,128)(2,1)S(1)}, bf16[32,128]{1,0:T(8,128)(2,1)}, u32[]{:S(2)}) copy-start(bf16[32,128]{1,0:T(8,128)(2,1)} %param.16) | copy-start | bytes 24580
  58.7 12.2 %copy-start.13 = (f32[32,1]{0,1:T(1,128)S(1)}, f32[32,1]{0,1:T(1,128)}, u32[]{:S(2)}) copy-start(f32[32,1]{0,1:T(1,128)} %param.18) | copy-start | bytes 388
  58.7 12.9 %copy-start.12 = (bf16[32,128]{1,0:T(8,128)(2,1)S(1)}, bf16[32,128]{1,0:T(8,128)(2,1)}, u32[]{:S(2)}) copy-start(bf16[32,128]{1,0:T(8,128)(2,1)} %param.13) | copy-start | bytes 24580
  59.9 26.6 %copy-start = (bf16[4,96,256]{2,1,0:T(8,128)(2,1)S(1)}, bf16[4,96,256]{2,1,0:T(8,128)(2,1)}, u32[]{:S(2)}) copy-start(bf16[4,96,256]{2,1,0:T(8,128)(2,1)} %slice.33) | copy-start | bytes 589828
  66.5 11.7 %all-to-all-start.2 = ((bf16[4,768,128]{2,1,0:T(8,128)(2,1)}), bf16[4,768,128]{2,1,0:T(8,128)(2,1)S(1)}, u32[]{:S(2)}, u32[]{:S(2)}) async-start(bf16[4,768,128]{2,1,0:T(8,128)(2,1)} %bitcast.12), calls=%async_computation.2 | async-start | bytes 1572864 | tf_op jit(solution)/shard_map/all_to_all | solution.py:213
  70.0 55.4 %all-gather.2.cloned.1.call-start = ((), (), s32[]{:S(2)}) async-start(), calls=%async_computation.11 | async-start | bytes 1769472 | tf_op jit(solution)/shard_map/all_gather | solution.py:227
  70.9 20.5 %collective-permute-start.1 = (f32[2,32]{1,0:T(2,128)S(1)}, f32[2,32]{1,0:T(2,128)S(1)}, u32[]{:S(2)}, u32[]{:S(2)}) collective-permute-start(f32[2,32]{1,0:T(2,128)S(1)} %maximum_bitcast_fusion), channel_id=1, source_target_pairs={{0,0},{16,64},{32,128},{48,192},{64,256},{80,320},{96,384},{112,44... | collective-permute-start | bytes 776 | tf_op jit(solution)/shard_map/ppermute | solution.py:255
  71.6 14.8 %collective-permute-start = (bf16[32,256]{1,0:T(8,128)(2,1)S(1)}, bf16[32,256]{1,0:T(8,128)(2,1)S(1)}, u32[]{:S(2)}, u32[]{:S(2)}) collective-permute-start(bf16[32,256]{1,0:T(8,128)(2,1)S(1)} %pad_maximum_fusion.2), channel_id=1, source_target_pairs={{0,0},{16,64},{32,128},{48,192},{64,256},{80,320},{96,384},{112,44... | collective-permute-start | bytes 49160 | tf_op jit(solution)/shard_map/ppermute | solution.py:254
  78.9 14.8 %all-to-all-start.5 = ((bf16[16,32,256]{2,1,0:T(8,128)(2,1)}), bf16[16,32,256]{2,1,0:T(8,128)(2,1)S(1)}, u32[]{:S(2)}, u32[]{:S(2)}) async-start(bf16[16,32,256]{2,1,0:T(8,128)(2,1)} %broadcast_in_dim.30), calls=%async_computation.5 | async-start | bytes 524288 | tf_op jit(solution)/shard_map/all_to_all | solution.py:248
  86.3 118.9 %reduce-scatter.2.cloned.1.call-start = ((), (), s32[]{:S(2)}) async-start(), calls=%async_computation.12 | async-start | bytes 1769472 | tf_op jit(solution)/shard_map/reduce_scatter | solution.py:267
  90.2 1.1 copy-start.2
  93.7 1.4 copy-start.3
  100.3 1.1 copy-start.4
  125.4 1.4 copy-start.1
  126.8 1.4 copy-start.5
  179.6 26.6 %all-to-all-start.6 = ((bf16[4,768,128]{2,1,0:T(8,128)(2,1)}), bf16[4,768,128]{2,1,0:T(8,128)(2,1)S(1)}, u32[]{:S(2)}, u32[]{:S(2)}) async-start(bf16[4,768,128]{2,1,0:T(8,128)(2,1)} %bitcast.26), calls=%async_computation.7 | async-start | bytes 1572864 | tf_op jit(solution)/shard_map/all_to_all | solution.py:213
  183.1 23.1 %collective-permute-start.2 = (bf16[32,128]{1,0:T(8,128)(2,1)S(1)}, bf16[32,128]{1,0:T(8,128)(2,1)S(1)}, u32[]{:S(2)}, u32[]{:S(2)}) collective-permute-start(bf16[32,128]{1,0:T(8,128)(2,1)S(1)} %get-tuple-element.31), channel_id=1, source_target_pairs={{0,0},{64,16},{128,32},{192,48},{256,64},{320,80},{384,96},{448,11... | collective-permute-start | bytes 24584 | tf_op jit(solution)/shard_map/ppermute | solution.py:278
  206.9 8.8 %all-to-all-start.9 = ((bf16[4,97,256]{2,1,0:T(8,128)(2,1)}), bf16[4,97,256]{2,1,0:T(8,128)(2,1)S(1)}, u32[]{:S(2)}, u32[]{:S(2)}) async-start(bf16[4,97,256]{2,1,0:T(8,128)(2,1)} %pad_maximum_fusion), calls=%async_computation.10 | async-start | bytes 425984 | tf_op jit(solution)/shard_map/all_to_all | solution.py:213
Sparse Core Ops, SparseCore 0:
  72.9 52.4 all-gather.1
  130.7 74.4 reduce-scatter.1

commit v3 on v2

--- a/solution.py
+++ b/solution.py
@@ -64,17 +64,18 @@
             d_ref[0:reach, HD : 2 * HD] += dv
 
 
-def lower_kernel(info, q_ref, g_ref, rows_ref, kv_ref, dq_in, d_ref, dq_ref, acc, *, span):
+def lower_kernel(info, q_ref, g_ref, rows_ref, kv_ref, dq_in, d_ref, acc, *, span, pitch):
     square, live = info[0], info[1]
-    squares = kv_ref.shape[0] // span
+    squares = kv_ref.shape[0] // pitch
     columns = q_ref.shape[0]
     group = columns // KVH
     acc[...] = dq_in[...]
     used = jnp.where(live != 0, square, 0)
 
     def whole(j, carry):
+        source = pl.ds(pl.multiple_of(j * pitch, 16), span)
         block = pl.ds(pl.multiple_of(j * span, 16), span)
-        keys, values = kv_ref[block, 0:HD], kv_ref[block, HD : 2 * HD]
+        keys, values = kv_ref[source, 0:HD], kv_ref[source, HD : 2 * HD]
         dkeys = dvalues = 0.0
         for c in range(0, columns, 2 * group):
             dk, dv = terms((q_ref, g_ref, rows_ref), keys, values, slice(c, c + 2 * group), None, acc)
@@ -89,7 +90,6 @@
 
     lax.fori_loop(0, used, whole, 0)
     lax.fori_loop(used, squares, empty, 0)
-    dq_ref[...] = (acc[...].T * SCALE).astype(BF16)
 
 
 def prompt_kernel(
@@ -125,7 +125,7 @@
 
     d_ref[:, 0:HD] = (total[:, 0:HD] * SCALE).astype(BF16)
     d_ref[:, HD : 2 * HD] = total[:, HD : 2 * HD].astype(BF16)
-    dq_ref[...] = acc[...]
+    dq_ref[...] = (acc[...].T * SCALE).astype(BF16)
 
 
 def call(body, info, operands, outs, scratch, pairs):
@@ -151,35 +151,38 @@
         (*fixed, spot, block),
         (jax.ShapeDtypeStruct(block.shape, F32), jax.ShapeDtypeStruct(turned, F32)),
         [],
-        turned[1] * block.shape[0] * 5 // 8,
-    )
-
-
-def lower_backward(info, fixed, kv, carried, span):
-    turned = carried.shape
+        block.shape[0],
+    )
+
+
+def lower_backward(info, fixed, kv, carried, span, pitch):
+    query = fixed[0]
     return call(
-        functools.partial(lower_kernel, span=span),
+        functools.partial(lower_kernel, span=span, pitch=pitch),
         info,
         (*fixed, kv, carried),
-        (jax.ShapeDtypeStruct(kv.shape, BF16), jax.ShapeDtypeStruct(turned[::-1], BF16)),
-        [pltpu.VMEM(turned, F32)],
-        turned[1] * kv.shape[0],
+        (
+            jax.ShapeDtypeStruct((kv.shape[0] // pitch * span, kv.shape[1]), BF16),
+            jax.ShapeDtypeStruct(carried.shape, F32),
+        ),
+        [],
+        query.shape[0] * kv.shape[0],
     )
 
 
 def prompt_backward(info, fixed, prompt_rows, kv, carried, blocks):
-    turned = carried.shape
+    query = fixed[0]
     return call(
         functools.partial(prompt_kernel, blocks=blocks),
         info,
         (*fixed, *prompt_rows, kv, carried),
         (
             jax.ShapeDtypeStruct(kv.shape, BF16),
-            jax.ShapeDtypeStruct(turned, F32),
+            jax.ShapeDtypeStruct(query.shape, BF16),
             jax.ShapeDtypeStruct(prompt_rows[0].shape, BF16),
         ),
-        [pltpu.VMEM(turned, F32), pltpu.VMEM(kv.shape, F32)],
-        turned[1] * kv.shape[0],
+        [pltpu.VMEM(carried.shape, F32), pltpu.VMEM(kv.shape, F32)],
+        query.shape[0] * kv.shape[0],
     )
 
 
@@ -190,6 +193,15 @@
         grads.reshape(height, heads, HD).astype(F32) * outputs.reshape(height, heads, HD).astype(F32),
         axis=2,
     )
+
+
+def three(rows):
+    parts = []
+    for _ in range(3):
+        part = lax.reduce_precision(rows, 8, 7)
+        parts.append(part.astype(BF16))
+        rows = rows - part
+    return jnp.concatenate(parts, axis=1)
 
 
 def on_device(
@@ -224,36 +236,34 @@
     mine = both[:, :rows].reshape(span, 2 * HD)
     prompt = both[:, rows:].reshape(KVH * part, 2 * HD)
 
-    kv = lax.all_gather(mine, "blk", axis=0, tiled=True, axis_index_groups=far)
-    r_query, r_grad, r_lse, prompt, mine = together(r_query, r_grad, r_lse, prompt, mine)
+    few = KVH * part
+    spare = jnp.zeros((-few % 16, 2 * HD), BF16)
+    pitch = span + few + spare.shape[0]
+    kv = jnp.concatenate([mine, prompt, spare], axis=0)
+    kv = lax.all_gather(kv, "blk", axis=0, tiled=True, axis_index_groups=far)
+    r_query, r_grad, r_lse, mine = together(r_query, r_grad, r_lse, mine)
 
     def heads_first(block):
         heads = block.reshape(rows, KVH, GRP, HD).transpose(1, 2, 0, 3)
         return heads.reshape(KVH, GRP * rows, HD)
 
     query = trade(heads_first(r_query[0])).reshape(KVH * GRP * rows, HD)
-    grads = trade(heads_first(r_grad[0])).reshape(KVH * GRP * rows, HD)
     position = owner * rows + jnp.arange(rows)
     alive = position < lengths[0]
     lse_rows = jnp.where(alive[:, None], r_lse[0] * LOG2E, DEAD)
     delta = row_delta(r_grad[0], r_out[0])
-    pair = jnp.stack([lse_rows.T.reshape(KVH, GRP, rows), delta.T.reshape(KVH, GRP, rows)], axis=1)
-    pair = trade(pair.reshape(KVH, 2 * GRP, rows)).reshape(KVH, 2, GRP * rows)
-    pair = pair.transpose(1, 0, 2).reshape(2, KVH * GRP * rows)
-
-    prompt = jnp.broadcast_to(prompt[None], (squares,) + prompt.shape)
-    prompt = lax.all_to_all(prompt, "blk", 0, 0, tiled=True, axis_index_groups=far)
-    prompt = prompt.reshape(blocks * part, 2 * HD)
-    prompt = jnp.broadcast_to(prompt[None], (rolls,) + prompt.shape)
-    prompt = lax.all_to_all(prompt, "roll", 0, 0, tiled=True).reshape(-1, 2 * HD)
-    prompt = prompt.reshape(rolls, blocks, part, 2 * HD).transpose(0, 2, 1, 3).reshape(-1, 2 * HD)
+    pair = jnp.stack([lse_rows.T.reshape(KVH, GRP * rows), delta.T.reshape(KVH, GRP * rows)], axis=1)
+    pair = three(pair.reshape(KVH, -1, HD))
+    grads = trade(jnp.concatenate([heads_first(r_grad[0]), pair], axis=1))
+    pair = grads[:, GRP * rows :].reshape(KVH, 3, 2, GRP * rows).astype(F32)
+    pair = ((pair[:, 2] + pair[:, 1]) + pair[:, 0]).transpose(1, 0, 2).reshape(2, KVH * GRP * rows)
+    grads = grads[:, : GRP * rows].reshape(KVH * GRP * rows, HD)
 
     there = [(m * squares + s, s * KVH + m) for m in range(KVH) for s in range(squares)]
     back = [(b, a) for a, b in there]
     p_rows = jnp.concatenate([p_lse * LOG2E, row_delta(p_grad, p_out)], axis=1).T
     p_pack = lax.ppermute(jnp.concatenate([p_query, p_grad], axis=1), "blk", there)
     p_rows = lax.ppermute(p_rows, "blk", there)
-    prompt_rows = (p_pack[:, :HD], p_pack[:, HD:], p_rows)
 
     info = jnp.stack(
         [square, square * span < lengths[0], member * p_query.shape[0], squares]
@@ -262,10 +272,18 @@
     fixed = (query, grads, pair)
 
     own, dq = own_backward(info, fixed, spot, mine)
-    prompt_terms, dq, p_dq = prompt_backward(info, fixed, prompt_rows, prompt, dq, blocks)
-    lower, dq = lower_backward(info, fixed, kv, dq, span)
+    kv, p_pack, p_rows = together(kv, p_pack, p_rows)
+    prompt_rows = (p_pack[:, :HD], p_pack[:, HD:], p_rows)
+    lower, dq = lower_backward(info, fixed, kv, dq, span, pitch)
+    prompt = kv.reshape(squares, pitch, 2 * HD)[:, span : span + few].reshape(blocks * part, 2 * HD)
+    lower, prompt = together(lower, prompt)
     lower = lax.psum_scatter(lower, "blk", scatter_dimension=0, tiled=True, axis_index_groups=far)
     summed = (own + lower.astype(F32)).astype(BF16)
+
+    prompt = jnp.broadcast_to(prompt[None], (rolls,) + prompt.shape)
+    prompt = lax.all_to_all(prompt, "roll", 0, 0, tiled=True).reshape(-1, 2 * HD)
+    prompt = prompt.reshape(rolls, blocks, part, 2 * HD).transpose(0, 2, 1, 3).reshape(-1, 2 * HD)
+    prompt_terms, dq, p_dq = prompt_backward(info, fixed, prompt_rows, prompt, dq, blocks)
 
     prompt_terms = prompt_terms.reshape(rolls, part, blocks, 2 * HD).transpose(0, 2, 1, 3)
     prompt_terms = lax.all_to_all(prompt_terms.reshape(rolls, blocks * part, 2 * HD), "roll", 0, 0, tiled=True)

time: 227 us -> 208 us (0.916)
  starting transfers between devices: 45.2 us -> 29.5 us
  waiting for transfers between devices: 83.1 us -> 78.3 us
    reduce_scatter x1, waiting for transfers between devices: 21.4 us -> 0.02 us  [on_device(): lax.psum_scatter(lower, 'blk', scatter_dimension=0, tiled=True, axis_inde...]
    all_to_all x1 -> x0, starting transfers between devices: 14.2 us -> none  [on_device(): lax.all_to_all(prompt, 'blk', 0, 0, tiled=True, axis_index_groups=far)]
    all_gather x1, waiting for transfers between devices: 24 us -> 37.7 us  [on_device(): kv = lax.all_gather(kv, 'blk', axis=0, tiled=True, axis_index_groups=far)]
    all_to_all x1 -> x0, waiting for transfers between devices: 10.8 us -> none  [on_device(): lax.all_to_all(prompt, 'blk', 0, 0, tiled=True, axis_index_groups=far)]
    all_to_all x6 -> x5, waiting for transfers between devices: 23.9 us -> 33.2 us  [trade(): lax.all_to_all(block, 'blk', 0, 0, tiled=True, axis_index_groups=near)]
    all_to_all x1, waiting for transfers between devices: 2.32 us -> 7.34 us  [on_device(): lax.all_to_all(prompt, 'roll', 0, 0, tiled=True).reshape(-1, 2 * HD)]
    all_to_all x6 -> x5, starting transfers between devices: 21.5 us -> 20.4 us  [trade(): lax.all_to_all(block, 'blk', 0, 0, tiled=True, axis_index_groups=near)]
    unnamed x35 -> x33, local copies, waits for them, and re-layouts: 9.21 us -> 9.14 us
  transfers between devices with their start and end apart: 13 -> 11, of which waited for: 9 -> 7; matrix products, arithmetic and copies ran while one was open for 4% -> 3% of each run, Pallas kernels for 4% -> 5%
where the time goes in v3:
time: 208 us; the launch traced here: 205 us
  waiting for transfers between devices  78.3 us (38%)
  blocking collectives  48.2 us (23%)
  starting transfers between devices  29.5 us (14%)
  local copies, waits for them, and re-layouts  15.7 us (8%)
  between operations  15.1 us (7%)
  Pallas kernels  12.2 us (6%)
  other arithmetic  5.57 us (3%)
    all_gather x1, waiting for transfers between devices, on_device(): kv = lax.all_gather(kv, 'blk', axis=0, tiled=True, axis_index_groups=far)  37.7 us
    all_to_all x1, blocking collectives, on_device(): lax.all_to_all(prompt_terms.reshape(squares, KVH * part, 2 * HD), 'blk',...  36.5 us
    all_to_all x5, waiting for transfers between devices, trade(): lax.all_to_all(block, 'blk', 0, 0, tiled=True, axis_index_groups=near)  33.2 us
    all_to_all x5, starting transfers between devices, trade(): lax.all_to_all(block, 'blk', 0, 0, tiled=True, axis_index_groups=near)  20.4 us
    pallas_call x3, Pallas kernels, call(): pl.pallas_call(body, out_shape=outs, in_specs=[pl.BlockSpec(memory_space=...  12.2 us
    all_to_all x1, blocking collectives, on_device(): lax.all_to_all(prompt_terms.reshape(rolls, blocks * part, 2 * HD), 'roll'...  11.8 us
    unnamed x33, local copies, waits for them, and re-layouts  9.14 us
    all_to_all x1, waiting for transfers between devices, on_device(): lax.all_to_all(prompt, 'roll', 0, 0, tiled=True).reshape(-1, 2 * HD)  7.34 us
  transfers between devices with their start and end apart: 11, of which 7 were waited for; matrix products, arithmetic and copies ran while one was open for 3% of the time, Pallas kernels for 5%

profile of v3, /device:TPU:6, one launch (start us, length us, event | category | flops | bytes accessed | tf_op | source)
XLA Modules:
  0.0 204.5 jit_solution(11173031435933645166)
XLA Ops:
  7.2 1.1 maximum_maximum_fusion
  8.4 0.2 copy.100
  8.7 0.7 copy.76
  9.4 4.2 %all-to-all-start = ((bf16[4,97,256]{2,1,0:T(8,128)(2,1)}), bf16[4,97,256]{2,1,0:T(8,128)(2,1)S(1)}, u32[]{:S(2)}, u32[]{:S(2)}) async-start(bf16[4,97,256]{2,1,0:T(8,128)(2,1)} %copy.76), calls=%async_computation | async-start | bytes 425984 | tf_op jit(solution)/shard_map/all_to_all | solution.py:225
  14.3 4.6 %all-to-all-done = bf16[4,97,256]{2,1,0:T(8,128)(2,1)S(1)} async-done(((bf16[4,97,256]{2,1,0:T(8,128)(2,1)}), bf16[4,97,256]{2,1,0:T(8,128)(2,1)S(1)}, u32[]{:S(2)}, u32[]{:S(2)}) %all-to-all-start) | async-done | bytes 198688 | tf_op jit(solution)/shard_map/all_to_all | solution.py:225
  18.9 0.2 multiply_bitcast_fusion
  19.1 0.3 copy.93
  19.4 0.5 reduce_sum.44
  20.3 0.2 copy.92
  20.4 0.3 copy.78
  20.7 1.0 pad_maximum_fusion
  21.7 3.5 %all-to-all-start.2 = ((bf16[4,804,128]{2,1,0:T(8,128)(2,1)}), bf16[4,804,128]{2,1,0:T(8,128)(2,1)S(1)}, u32[]{:S(2)}, u32[]{:S(2)}) async-start(bf16[4,804,128]{2,1,0:T(8,128)(2,1)} %pad_maximum_fusion), calls=%async_computation.2 | async-start | bytes 1654784 | tf_op jit(solution)/shard_map/all_to_all | solution.py:225
  25.4 0.8 maximum_maximum_fusion.1
  26.2 0.2 copy.91
  26.4 1.2 copy.77
  27.6 7.7 %all-to-all-done.2 = bf16[4,804,128]{2,1,0:T(8,128)(2,1)S(1)} async-done(((bf16[4,804,128]{2,1,0:T(8,128)(2,1)}), bf16[4,804,128]{2,1,0:T(8,128)(2,1)S(1)}, u32[]{:S(2)}, u32[]{:S(2)}) %all-to-all-start.2) | async-done | bytes 823328 | tf_op jit(solution)/shard_map/all_to_all | solution.py:225
  35.3 3.5 %all-to-all-start.1 = ((bf16[4,768,128]{2,1,0:T(8,128)(2,1)}), bf16[4,768,128]{2,1,0:T(8,128)(2,1)S(1)}, u32[]{:S(2)}, u32[]{:S(2)}) async-start(bf16[4,768,128]{2,1,0:T(8,128)(2,1)} %bitcast.9), calls=%async_computation.1 | async-start | bytes 1572864 | tf_op jit(solution)/shard_map/all_to_all | solution.py:225
  38.9 0.7 collective-permute-start
  39.7 0.7 collective-permute-start.1
  40.7 8.9 %all-to-all-done.1 = bf16[4,768,128]{2,1,0:T(8,128)(2,1)S(1)} async-done(((bf16[4,768,128]{2,1,0:T(8,128)(2,1)}), bf16[4,768,128]{2,1,0:T(8,128)(2,1)S(1)}, u32[]{:S(2)}, u32[]{:S(2)}) %all-to-all-start.1) | async-done | bytes 786464 | tf_op jit(solution)/shard_map/all_to_all | solution.py:225
  49.6 3.7 %shard_map.172 = (f32[384,256]{1,0:T(8,128)S(1)}, f32[128,3072]{1,0:T(8,128)S(1)}) custom-call(s32[4]{0:T(128)S(1)} %pad_add_fusion.info, bf16[3072,128]{1,0:T(8,128)(2,1)S(1)} %bitcast.73, bf16[3072,128]{1,0:T(8,128)(2,1)S(1)} %bitcast.76, f32[2,3072]{1,0:T(2,128)S(1)} %bitcast.83, s32[1,768]{1,0:T(1,128)S(1)} %broadcast_in_dim_tile.3.spot_ref, ...), custom_call_target="tpu_custom_call" | custom-call | flops 491520 | bytes 4194304 | tf_op jit(solution)/shard_map/pallas_call | solution.py:133
  53.3 1.1 copy-done.1
  54.5 37.7 %all-gather.2.cloned.1.call-done.kv_ref = bf16[3200,256]{1,0:T(8,128)(2,1)} async-done(((bf16[400,256]{1,0:T(8,128)(2,1)}), bf16[3200,256]{1,0:T(8,128)(2,1)}) %all-gather.2.cloned.1.call-update) | async-done | bytes 1638416 | tf_op jit(solution)/shard_map/all_gather | solution.py:243
  92.2 1.4 copy-done
  93.6 1.4 copy-done.2
  95.0 1.9 shard_map.173
  96.9 1.1 copy-done.3
  98.1 0.7 broadcast_in_dim.25
  98.9 7.0 %all-to-all-start.3 = ((bf16[16,32,256]{2,1,0:T(8,128)(2,1)}), bf16[16,32,256]{2,1,0:T(8,128)(2,1)S(1)}, u32[]{:S(2)}, u32[]{:S(2)}) async-start(bf16[16,32,256]{2,1,0:T(8,128)(2,1)} %broadcast_in_dim.25), calls=%async_computation.4 | async-start | bytes 524288 | tf_op jit(solution)/shard_map/all_to_all | solution.py:284
  105.9 7.3 %all-to-all-done.3 = bf16[16,32,256]{2,1,0:T(8,128)(2,1)S(1)} async-done(((bf16[16,32,256]{2,1,0:T(8,128)(2,1)}), bf16[16,32,256]{2,1,0:T(8,128)(2,1)S(1)}, u32[]{:S(2)}, u32[]{:S(2)}) %all-to-all-start.3) | async-done | bytes 262176 | tf_op jit(solution)/shard_map/all_to_all | solution.py:284
  113.2 1.4 copy-done.4
  114.6 6.5 %shard_map.174 = (bf16[512,256]{1,0:T(8,128)(2,1)S(1)}, bf16[3072,128]{1,0:T(8,128)(2,1)}, bf16[32,128]{1,0:T(8,128)(2,1)S(1)}) custom-call(s32[4]{0:T(128)S(1)} %pad_add_fusion.info, bf16[3072,128]{1,0:T(8,128)(2,1)S(1)} %bitcast.75, bf16[3072,128]{1,0:T(8,128)(2,1)S(1)} %bitcast.78, f32[2,3072]{1,0:T(2,128)S(1)} %bitcast.85, ...), custom_call_target="tpu_custom_call" | custom-call | flops 2013265920 | bytes 4194304 | tf_op jit(solution)/shard_map/pallas_call | solution.py:133
  121.2 11.8 %all_to_all.40 = bf16[16,32,256]{2,1,0:T(8,128)(2,1)S(1)} all-to-all(bf16[16,32,256]{2,1,0:T(8,128)(2,1)S(1)} %bitcast.82), channel_id=1, replica_groups=mesh['blk'=32,'roll'=16] {'roll'}, dimensions={0} | all-to-all | bytes 524288 | tf_op jit(solution)/shard_map/all_to_all | solution.py:289
  133.0 36.5 %all_to_all.41 = bf16[8,4,256]{2,1,0:T(4,128)(2,1)S(1)} all-to-all(bf16[8,4,256]{2,1,0:T(4,128)(2,1)S(1)} %reshape.109), channel_id=1, replica_groups={{0,64,128,192,256,320,384,448},{16,80,144,208,272,336,400,464},{32,96,1..., dimensions={0} | all-to-all | bytes 32768 | tf_op jit(solution)/shard_map/all_to_all | solution.py:291
  169.5 3.8 %all-to-all-start.4 = ((bf16[4,768,128]{2,1,0:T(8,128)(2,1)}), bf16[4,768,128]{2,1,0:T(8,128)(2,1)S(1)}, u32[]{:S(2)}, u32[]{:S(2)}) async-start(bf16[4,768,128]{2,1,0:T(8,128)(2,1)} %bitcast.27), calls=%async_computation.5 | async-start | bytes 1572864 | tf_op jit(solution)/shard_map/all_to_all | solution.py:225
  173.3 0.6 collective-permute-start.2
  174.0 1.0 add_convert_fusion
  175.0 8.3 %all-to-all-done.4 = bf16[4,768,128]{2,1,0:T(8,128)(2,1)S(1)} async-done(((bf16[4,768,128]{2,1,0:T(8,128)(2,1)}), bf16[4,768,128]{2,1,0:T(8,128)(2,1)S(1)}, u32[]{:S(2)}, u32[]{:S(2)}) %all-to-all-start.4) | async-done | bytes 786464 | tf_op jit(solution)/shard_map/all_to_all | solution.py:225
  183.4 0.7 pad_maximum_fusion.1
  184.1 5.4 %all-to-all-start.7 = ((bf16[4,97,256]{2,1,0:T(8,128)(2,1)}), bf16[4,97,256]{2,1,0:T(8,128)(2,1)S(1)}, u32[]{:S(2)}, u32[]{:S(2)}) async-start(bf16[4,97,256]{2,1,0:T(8,128)(2,1)} %pad_maximum_fusion.1), calls=%async_computation.8 | async-start | bytes 425984 | tf_op jit(solution)/shard_map/all_to_all | solution.py:225
  189.4 0.3 copy.98
  189.7 1.2 reshape.113
  191.0 3.7 %all-to-all-done.7 = bf16[4,97,256]{2,1,0:T(8,128)(2,1)S(1)} async-done(((bf16[4,97,256]{2,1,0:T(8,128)(2,1)}), bf16[4,97,256]{2,1,0:T(8,128)(2,1)S(1)}, u32[]{:S(2)}, u32[]{:S(2)}) %all-to-all-start.7) | async-done | bytes 198688 | tf_op jit(solution)/shard_map/all_to_all | solution.py:225
  194.9 0.6 slice_bitcast_fusion
  195.5 0.3 fusion.3
  195.8 0.7 copy.86
  196.4 0.7 copy.87
  197.1 0.6 copy.104
  (65 shorter events, 1.7 us)
Async XLA Ops:
  7.2 11.7 %copy-start.5 = (bf16[1,96,4096]{2,1,0:T(8,128)(2,1)S(1)}, bf16[1,96,4096]{2,1,0:T(8,128)(2,1)}, u32[]{:S(2)}) copy-start(bf16[1,96,4096]{2,1,0:T(8,128)(2,1)} %param.23) | copy-start | bytes 2359300
  7.2 11.7 %copy-start.7 = (bf16[1,96,4096]{2,1,0:T(8,128)(2,1)S(1)}, bf16[1,96,4096]{2,1,0:T(8,128)(2,1)}, u32[]{:S(2)}) copy-start(bf16[1,96,4096]{2,1,0:T(8,128)(2,1)} %param.22) | copy-start | bytes 2359300
  9.4 9.4 %all-to-all-start = ((bf16[4,97,256]{2,1,0:T(8,128)(2,1)}), bf16[4,97,256]{2,1,0:T(8,128)(2,1)S(1)}, u32[]{:S(2)}, u32[]{:S(2)}) async-start(bf16[4,97,256]{2,1,0:T(8,128)(2,1)} %copy.76), calls=%async_computation | async-start | bytes 425984 | tf_op jit(solution)/shard_map/all_to_all | solution.py:225
  19.4 0.7 copy-start.9
  20.7 5.5 %copy-start.6 = (bf16[1,96,4096]{2,1,0:T(8,128)(2,1)S(1)}, bf16[1,96,4096]{2,1,0:T(8,128)(2,1)}, u32[]{:S(2)}) copy-start(bf16[1,96,4096]{2,1,0:T(8,128)(2,1)} %param.19) | copy-start | bytes 2359300
  21.7 13.6 %all-to-all-start.2 = ((bf16[4,804,128]{2,1,0:T(8,128)(2,1)}), bf16[4,804,128]{2,1,0:T(8,128)(2,1)S(1)}, u32[]{:S(2)}, u32[]{:S(2)}) async-start(bf16[4,804,128]{2,1,0:T(8,128)(2,1)} %pad_maximum_fusion), calls=%async_computation.2 | async-start | bytes 1654784 | tf_op jit(solution)/shard_map/all_to_all | solution.py:225
  25.2 66.9 %all-gather.2.cloned.1.call-start = ((), (), s32[]{:S(2)}) async-start(), calls=%async_computation.9 | async-start | bytes 1843200 | tf_op jit(solution)/shard_map/all_gather | solution.py:243
  26.4 12.5 %copy-start.8 = (bf16[32,128]{1,0:T(8,128)(2,1)S(1)}, bf16[32,128]{1,0:T(8,128)(2,1)}, u32[]{:S(2)}) copy-start(bf16[32,128]{1,0:T(8,128)(2,1)} %param.17) | copy-start | bytes 24580
  26.4 12.5 %copy-start.11 = (bf16[32,128]{1,0:T(8,128)(2,1)S(1)}, bf16[32,128]{1,0:T(8,128)(2,1)}, u32[]{:S(2)}) copy-start(bf16[32,128]{1,0:T(8,128)(2,1)} %param.13) | copy-start | bytes 24580
  26.4 13.2 %copy-start.10 = (bf16[32,128]{1,0:T(8,128)(2,1)S(1)}, bf16[32,128]{1,0:T(8,128)(2,1)}, u32[]{:S(2)}) copy-start(bf16[32,128]{1,0:T(8,128)(2,1)} %param.16) | copy-start | bytes 24580
  26.4 13.3 %copy-start.12 = (f32[32,1]{0,1:T(1,128)S(1)}, f32[32,1]{0,1:T(1,128)}, u32[]{:S(2)}) copy-start(f32[32,1]{0,1:T(1,128)} %param.18) | copy-start | bytes 388
  35.3 14.3 %all-to-all-start.1 = ((bf16[4,768,128]{2,1,0:T(8,128)(2,1)}), bf16[4,768,128]{2,1,0:T(8,128)(2,1)S(1)}, u32[]{:S(2)}, u32[]{:S(2)}) async-start(bf16[4,768,128]{2,1,0:T(8,128)(2,1)} %bitcast.9), calls=%async_computation.1 | async-start | bytes 1572864 | tf_op jit(solution)/shard_map/all_to_all | solution.py:225
  38.8 135.2 %reduce-scatter.2.cloned.1.call-start = ((), (), s32[]{:S(2)}) async-start(), calls=%async_computation.10 | async-start | bytes 1769472 | tf_op jit(solution)/shard_map/reduce_scatter | solution.py:280
  38.9 15.6 %collective-permute-start = (bf16[32,256]{1,0:T(8,128)(2,1)S(1)}, bf16[32,256]{1,0:T(8,128)(2,1)S(1)}, u32[]{:S(2)}, u32[]{:S(2)}) collective-permute-start(bf16[32,256]{1,0:T(8,128)(2,1)S(1)} %pad_maximum_fusion.3), channel_id=1, source_target_pairs={{0,0},{16,64},{32,128},{48,192},{64,256},{80,320},{96,384},{112,44... | collective-permute-start | bytes 49160 | tf_op jit(solution)/shard_map/ppermute | solution.py:265
  39.7 14.7 %collective-permute-start.1 = (f32[2,32]{1,0:T(2,128)S(1)}, f32[2,32]{1,0:T(2,128)S(1)}, u32[]{:S(2)}, u32[]{:S(2)}) collective-permute-start(f32[2,32]{1,0:T(2,128)S(1)} %maximum_bitcast_fusion), channel_id=1, source_target_pairs={{0,0},{16,64},{32,128},{48,192},{64,256},{80,320},{96,384},{112,44... | collective-permute-start | bytes 776 | tf_op jit(solution)/shard_map/ppermute | solution.py:266
  53.3 1.1 copy-start.1
  92.2 1.4 copy-start
  93.6 1.4 copy-start.2
  96.9 1.1 copy-start.3
  98.9 14.4 %all-to-all-start.3 = ((bf16[16,32,256]{2,1,0:T(8,128)(2,1)}), bf16[16,32,256]{2,1,0:T(8,128)(2,1)S(1)}, u32[]{:S(2)}, u32[]{:S(2)}) async-start(bf16[16,32,256]{2,1,0:T(8,128)(2,1)} %broadcast_in_dim.25), calls=%async_computation.4 | async-start | bytes 524288 | tf_op jit(solution)/shard_map/all_to_all | solution.py:284
  113.2 1.4 copy-start.4
  169.5 13.9 %all-to-all-start.4 = ((bf16[4,768,128]{2,1,0:T(8,128)(2,1)}), bf16[4,768,128]{2,1,0:T(8,128)(2,1)S(1)}, u32[]{:S(2)}, u32[]{:S(2)}) async-start(bf16[4,768,128]{2,1,0:T(8,128)(2,1)} %bitcast.27), calls=%async_computation.5 | async-start | bytes 1572864 | tf_op jit(solution)/shard_map/all_to_all | solution.py:225
  173.3 1.7 collective-permute-start.2
  184.1 10.6 %all-to-all-start.7 = ((bf16[4,97,256]{2,1,0:T(8,128)(2,1)}), bf16[4,97,256]{2,1,0:T(8,128)(2,1)S(1)}, u32[]{:S(2)}, u32[]{:S(2)}) async-start(bf16[4,97,256]{2,1,0:T(8,128)(2,1)} %pad_maximum_fusion.1), calls=%async_computation.8 | async-start | bytes 425984 | tf_op jit(solution)/shard_map/all_to_all | solution.py:225
Sparse Core Ops, SparseCore 0:
  28.2 63.9 all-gather.1
  98.3 72.0 reduce-scatter.1

commit v4 on v3

--- a/solution.py
+++ b/solution.py
@@ -128,7 +128,7 @@
     dq_ref[...] = (acc[...].T * SCALE).astype(BF16)
 
 
-def call(body, info, operands, outs, scratch, pairs):
+def call(body, info, operands, outs, scratch, pairs, moved=4 * 1024 * 1024):
     vmem = pl.BlockSpec(memory_space=pltpu.VMEM)
     return pl.pallas_call(
         body,
@@ -138,7 +138,7 @@
         scratch_shapes=scratch,
         compiler_params=pltpu.CompilerParams(vmem_limit_bytes=40 * 1024 * 1024),
         cost_estimate=pl.CostEstimate(
-            flops=pairs * HD * 10, bytes_accessed=4 * 1024 * 1024, transcendentals=pairs
+            flops=pairs * HD * 10, bytes_accessed=moved, transcendentals=pairs
         ),
     )(info, *operands)
 
@@ -151,7 +151,8 @@
         (*fixed, spot, block),
         (jax.ShapeDtypeStruct(block.shape, F32), jax.ShapeDtypeStruct(turned, F32)),
         [],
-        block.shape[0],
+        0,
+        0,
     )
 
 
@@ -182,7 +183,7 @@
             jax.ShapeDtypeStruct(prompt_rows[0].shape, BF16),
         ),
         [pltpu.VMEM(carried.shape, F32), pltpu.VMEM(kv.shape, F32)],
-        query.shape[0] * kv.shape[0],
+        query.shape[0] * kv.shape[0] * 25,
     )
 
 
@@ -236,24 +237,24 @@
     mine = both[:, :rows].reshape(span, 2 * HD)
     prompt = both[:, rows:].reshape(KVH * part, 2 * HD)
 
-    few = KVH * part
-    spare = jnp.zeros((-few % 16, 2 * HD), BF16)
-    pitch = span + few + spare.shape[0]
-    kv = jnp.concatenate([mine, prompt, spare], axis=0)
-    kv = lax.all_gather(kv, "blk", axis=0, tiled=True, axis_index_groups=far)
-    r_query, r_grad, r_lse, mine = together(r_query, r_grad, r_lse, mine)
-
-    def heads_first(block):
-        heads = block.reshape(rows, KVH, GRP, HD).transpose(1, 2, 0, 3)
-        return heads.reshape(KVH, GRP * rows, HD)
-
-    query = trade(heads_first(r_query[0])).reshape(KVH * GRP * rows, HD)
     position = owner * rows + jnp.arange(rows)
     alive = position < lengths[0]
     lse_rows = jnp.where(alive[:, None], r_lse[0] * LOG2E, DEAD)
     delta = row_delta(r_grad[0], r_out[0])
     pair = jnp.stack([lse_rows.T.reshape(KVH, GRP * rows), delta.T.reshape(KVH, GRP * rows)], axis=1)
     pair = three(pair.reshape(KVH, -1, HD))
+    few = KVH * part
+    spare = jnp.zeros((-few % 16, 2 * HD), BF16)
+    pitch = span + few + spare.shape[0]
+    kv = jnp.concatenate([mine, prompt, spare], axis=0)
+    kv, r_query, r_grad, pair, mine = together(kv, r_query, r_grad, pair, mine)
+    kv = lax.all_gather(kv, "blk", axis=0, tiled=True, axis_index_groups=far)
+
+    def heads_first(block):
+        heads = block.reshape(rows, KVH, GRP, HD).transpose(1, 2, 0, 3)
+        return heads.reshape(KVH, GRP * rows, HD)
+
+    query = trade(heads_first(r_query[0])).reshape(KVH * GRP * rows, HD)
     grads = trade(jnp.concatenate([heads_first(r_grad[0]), pair], axis=1))
     pair = grads[:, GRP * rows :].reshape(KVH, 3, 2, GRP * rows).astype(F32)
     pair = ((pair[:, 2] + pair[:, 1]) + pair[:, 0]).transpose(1, 0, 2).reshape(2, KVH * GRP * rows)
@@ -272,11 +273,10 @@
     fixed = (query, grads, pair)
 
     own, dq = own_backward(info, fixed, spot, mine)
-    kv, p_pack, p_rows = together(kv, p_pack, p_rows)
+    kv, p_pack, p_rows, own, dq = together(kv, p_pack, p_rows, own, dq)
     prompt_rows = (p_pack[:, :HD], p_pack[:, HD:], p_rows)
     lower, dq = lower_backward(info, fixed, kv, dq, span, pitch)
     prompt = kv.reshape(squares, pitch, 2 * HD)[:, span : span + few].reshape(blocks * part, 2 * HD)
-    lower, prompt = together(lower, prompt)
     lower = lax.psum_scatter(lower, "blk", scatter_dimension=0, tiled=True, axis_index_groups=far)
     summed = (own + lower.astype(F32)).astype(BF16)
 

time: 208 us -> 208 us (level)
  blocking collectives: 48.2 us -> 51.2 us
  starting transfers between devices: 29.5 us -> 27.3 us
    reduce_scatter x1, waiting for transfers between devices: 0.02 us -> 11.8 us  [on_device(): lax.psum_scatter(lower, 'blk', scatter_dimension=0, tiled=True, axis_inde...]
    all_to_all x5, waiting for transfers between devices: 33.2 us -> 24.8 us  [trade(): lax.all_to_all(block, 'blk', 0, 0, tiled=True, axis_index_groups=near)]
    all_to_all x1, waiting for transfers between devices: 7.34 us -> 1.33 us  [on_device(): lax.all_to_all(prompt, 'roll', 0, 0, tiled=True).reshape(-1, 2 * HD)]
    unnamed x33 -> x35, local copies, waits for them, and re-layouts: 9.14 us -> 9.61 us
  transfers between devices with their start and end apart: 11 -> 11, of which waited for: 7 -> 8; matrix products, arithmetic and copies ran while one was open for 3% -> 3% of each run, Pallas kernels for 5% -> 6%
where the time goes in v4:
time: 208 us; the launch traced here: 205 us
  waiting for transfers between devices  76.4 us (37%)
  blocking collectives  51.2 us (25%)
  starting transfers between devices  27.3 us (13%)
  local copies, waits for them, and re-layouts  16.9 us (8%)
  between operations  15.2 us (7%)
  Pallas kernels  12.3 us (6%)
  other arithmetic  5.59 us (3%)
    all_to_all x1, blocking collectives, on_device(): lax.all_to_all(prompt_terms.reshape(squares, KVH * part, 2 * HD), 'blk',...  38.2 us
    all_gather x1, waiting for transfers between devices, on_device(): kv = lax.all_gather(kv, 'blk', axis=0, tiled=True, axis_index_groups=far)  37.7 us
    all_to_all x5, waiting for transfers between devices, trade(): lax.all_to_all(block, 'blk', 0, 0, tiled=True, axis_index_groups=near)  24.8 us
    all_to_all x5, starting transfers between devices, trade(): lax.all_to_all(block, 'blk', 0, 0, tiled=True, axis_index_groups=near)  18.6 us
    all_to_all x1, blocking collectives, on_device(): lax.all_to_all(prompt_terms.reshape(rolls, blocks * part, 2 * HD), 'roll'...  13 us
    pallas_call x3, Pallas kernels, call(): pl.pallas_call(body, out_shape=outs, in_specs=[pl.BlockSpec(memory_space=...  12.3 us
    reduce_scatter x1, waiting for transfers between devices, on_device(): lax.psum_scatter(lower, 'blk', scatter_dimension=0, tiled=True, axis_inde...  11.8 us
    unnamed x35, local copies, waits for them, and re-layouts  9.61 us
  transfers between devices with their start and end apart: 11, of which 8 were waited for; matrix products, arithmetic and copies ran while one was open for 3% of the time, Pallas kernels for 6%

profile of v4, /device:TPU:6, one launch (start us, length us, event | category | flops | bytes accessed | tf_op | source)
XLA Modules:
  0.0 204.8 jit_solution(4696443976758479284)
XLA Ops:
  7.2 1.1 maximum_maximum_fusion
  8.7 0.7 copy.76
  9.4 4.2 %all-to-all-start = ((bf16[4,97,256]{2,1,0:T(8,128)(2,1)}), bf16[4,97,256]{2,1,0:T(8,128)(2,1)S(1)}, u32[]{:S(2)}, u32[]{:S(2)}) async-start(bf16[4,97,256]{2,1,0:T(8,128)(2,1)} %copy.76), calls=%async_computation | async-start | bytes 425984 | tf_op jit(solution)/shard_map/all_to_all | solution.py:226
  14.5 0.5 copy-done.10
  15.1 0.3 copy.91
  15.4 0.5 reduce_sum.44
  16.2 2.6 %all-to-all-done = bf16[4,97,256]{2,1,0:T(8,128)(2,1)S(1)} async-done(((bf16[4,97,256]{2,1,0:T(8,128)(2,1)}), bf16[4,97,256]{2,1,0:T(8,128)(2,1)S(1)}, u32[]{:S(2)}, u32[]{:S(2)}) %all-to-all-start) | async-done | bytes 198688 | tf_op jit(solution)/shard_map/all_to_all | solution.py:226
  18.9 0.8 maximum_maximum_fusion.1
  19.9 0.3 copy.81
  20.2 1.0 pad_maximum_fusion
  21.2 3.5 %all-to-all-start.2 = ((bf16[4,804,128]{2,1,0:T(8,128)(2,1)}), bf16[4,804,128]{2,1,0:T(8,128)(2,1)S(1)}, u32[]{:S(2)}, u32[]{:S(2)}) async-start(bf16[4,804,128]{2,1,0:T(8,128)(2,1)} %pad_maximum_fusion), calls=%async_computation.2 | async-start | bytes 1654784 | tf_op jit(solution)/shard_map/all_to_all | solution.py:226
  24.7 0.7 all-gather.2.cloned.1.call-update
  25.6 1.2 copy.80
  26.8 7.9 %all-to-all-done.2 = bf16[4,804,128]{2,1,0:T(8,128)(2,1)S(1)} async-done(((bf16[4,804,128]{2,1,0:T(8,128)(2,1)}), bf16[4,804,128]{2,1,0:T(8,128)(2,1)S(1)}, u32[]{:S(2)}, u32[]{:S(2)}) %all-to-all-start.2) | async-done | bytes 823328 | tf_op jit(solution)/shard_map/all_to_all | solution.py:226
  34.8 3.5 %all-to-all-start.1 = ((bf16[4,768,128]{2,1,0:T(8,128)(2,1)}), bf16[4,768,128]{2,1,0:T(8,128)(2,1)S(1)}, u32[]{:S(2)}, u32[]{:S(2)}) async-start(bf16[4,768,128]{2,1,0:T(8,128)(2,1)} %bitcast.15), calls=%async_computation.1 | async-start | bytes 1572864 | tf_op jit(solution)/shard_map/all_to_all | solution.py:226
  38.3 0.7 collective-permute-start
  39.1 0.7 collective-permute-start.1
  40.1 8.9 %all-to-all-done.1 = bf16[4,768,128]{2,1,0:T(8,128)(2,1)S(1)} async-done(((bf16[4,768,128]{2,1,0:T(8,128)(2,1)}), bf16[4,768,128]{2,1,0:T(8,128)(2,1)S(1)}, u32[]{:S(2)}, u32[]{:S(2)}) %all-to-all-start.1) | async-done | bytes 786464 | tf_op jit(solution)/shard_map/all_to_all | solution.py:226
  49.1 3.7 %shard_map.172 = (f32[384,256]{1,0:T(8,128)S(1)}, f32[128,3072]{1,0:T(8,128)S(1)}) custom-call(s32[4]{0:T(128)S(1)} %pad_add_fusion.info, bf16[3072,128]{1,0:T(8,128)(2,1)S(1)} %bitcast.73, bf16[3072,128]{1,0:T(8,128)(2,1)S(1)} %bitcast.76, f32[2,3072]{1,0:T(2,128)S(1)} %bitcast.83, s32[1,768]{1,0:T(1,128)S(1)} %broadcast_in_dim_tile.3.spot_ref, ...), custom_call_target="tpu_custom_call" | custom-call | tf_op jit(solution)/shard_map/pallas_call | solution.py:133
  52.8 1.1 copy-done.1
  53.9 37.7 %all-gather.2.cloned.1.call-done.kv_ref = bf16[3200,256]{1,0:T(8,128)(2,1)} async-done(((bf16[400,256]{1,0:T(8,128)(2,1)}), bf16[3200,256]{1,0:T(8,128)(2,1)}) %all-gather.2.cloned.1.call-update) | async-done | bytes 1638416 | tf_op jit(solution)/shard_map/all_gather | solution.py:251
  91.7 0.8 slice.63
  92.5 0.7 broadcast_in_dim.27
  93.2 6.6 %all-to-all-start.3 = ((bf16[16,32,256]{2,1,0:T(8,128)(2,1)}), bf16[16,32,256]{2,1,0:T(8,128)(2,1)S(1)}, u32[]{:S(2)}, u32[]{:S(2)}) async-start(bf16[16,32,256]{2,1,0:T(8,128)(2,1)} %broadcast_in_dim.27), calls=%async_computation.4 | async-start | bytes 524288 | tf_op jit(solution)/shard_map/all_to_all | solution.py:284
  99.9 1.4 copy-done
  101.3 1.4 copy-done.2
  102.7 1.9 shard_map.173
  104.7 1.1 copy-done.3
  105.9 1.3 all-to-all-done.3
  107.2 1.4 copy-done.4
  108.6 6.6 %shard_map.174 = (bf16[512,256]{1,0:T(8,128)(2,1)S(1)}, bf16[3072,128]{1,0:T(8,128)(2,1)}, bf16[32,128]{1,0:T(8,128)(2,1)S(1)}) custom-call(s32[4]{0:T(128)S(1)} %pad_add_fusion.info, bf16[3072,128]{1,0:T(8,128)(2,1)S(1)} %bitcast.75, bf16[3072,128]{1,0:T(8,128)(2,1)S(1)} %bitcast.78, f32[2,3072]{1,0:T(2,128)S(1)} %bitcast.85, ...), custom_call_target="tpu_custom_call" | custom-call | flops 50331648000 | bytes 4194304 | tf_op jit(solution)/shard_map/pallas_call | solution.py:133
  115.2 13.0 %all_to_all.40 = bf16[16,32,256]{2,1,0:T(8,128)(2,1)S(1)} all-to-all(bf16[16,32,256]{2,1,0:T(8,128)(2,1)S(1)} %bitcast.82), channel_id=1, replica_groups=mesh['blk'=32,'roll'=16] {'roll'}, dimensions={0} | all-to-all | bytes 524288 | tf_op jit(solution)/shard_map/all_to_all | solution.py:289
  128.3 38.2 %all_to_all.41 = bf16[8,4,256]{2,1,0:T(4,128)(2,1)S(1)} all-to-all(bf16[8,4,256]{2,1,0:T(4,128)(2,1)S(1)} %reshape.105), channel_id=1, replica_groups={{0,64,128,192,256,320,384,448},{16,80,144,208,272,336,400,464},{32,96,1..., dimensions={0} | all-to-all | bytes 32768 | tf_op jit(solution)/shard_map/all_to_all | solution.py:291
  166.4 4.0 %all-to-all-start.4 = ((bf16[4,768,128]{2,1,0:T(8,128)(2,1)}), bf16[4,768,128]{2,1,0:T(8,128)(2,1)S(1)}, u32[]{:S(2)}, u32[]{:S(2)}) async-start(bf16[4,768,128]{2,1,0:T(8,128)(2,1)} %bitcast.27), calls=%async_computation.5 | async-start | bytes 1572864 | tf_op jit(solution)/shard_map/all_to_all | solution.py:226
  170.5 0.6 collective-permute-start.2
  171.1 11.8 %reduce-scatter.2.cloned.1.call-done = bf16[384,256]{1,0:T(8,128)(2,1)} async-done(((bf16[3072,256]{1,0:T(8,128)(2,1)}), bf16[384,256]{1,0:T(8,128)(2,1)}) %reduce-scatter.2.cloned.1.call-update) | async-done | bytes 196624 | tf_op jit(solution)/shard_map/reduce_scatter | solution.py:280
  183.0 1.0 add_convert_fusion
  184.0 1.6 all-to-all-done.4
  185.6 0.7 pad_maximum_fusion.1
  186.3 3.4 %all-to-all-start.7 = ((bf16[4,97,256]{2,1,0:T(8,128)(2,1)}), bf16[4,97,256]{2,1,0:T(8,128)(2,1)S(1)}, u32[]{:S(2)}, u32[]{:S(2)}) async-start(bf16[4,97,256]{2,1,0:T(8,128)(2,1)} %pad_maximum_fusion.1), calls=%async_computation.8 | async-start | bytes 425984 | tf_op jit(solution)/shard_map/all_to_all | solution.py:226
  189.7 0.3 copy.98
  190.0 1.2 reshape.109
  191.2 3.7 %all-to-all-done.7 = bf16[4,97,256]{2,1,0:T(8,128)(2,1)S(1)} async-done(((bf16[4,97,256]{2,1,0:T(8,128)(2,1)}), bf16[4,97,256]{2,1,0:T(8,128)(2,1)S(1)}, u32[]{:S(2)}, u32[]{:S(2)}) %all-to-all-start.7) | async-done | bytes 198688 | tf_op jit(solution)/shard_map/all_to_all | solution.py:226
  195.2 0.3 fusion.3
  195.4 0.6 slice_bitcast_fusion
  196.0 0.7 copy.86
  196.7 0.7 copy.87
  197.3 0.6 copy.104
  (68 shorter events, 2.2 us)
Async XLA Ops:
  7.2 7.1 %copy-start.8 = (bf16[1,96,4096]{2,1,0:T(8,128)(2,1)S(1)}, bf16[1,96,4096]{2,1,0:T(8,128)(2,1)}, u32[]{:S(2)}) copy-start(bf16[1,96,4096]{2,1,0:T(8,128)(2,1)} %param.22) | copy-start | bytes 2359300
  7.2 7.1 %copy-start.5 = (bf16[1,96,4096]{2,1,0:T(8,128)(2,1)S(1)}, bf16[1,96,4096]{2,1,0:T(8,128)(2,1)}, u32[]{:S(2)}) copy-start(bf16[1,96,4096]{2,1,0:T(8,128)(2,1)} %param.23) | copy-start | bytes 2359300
  9.4 9.4 %all-to-all-start = ((bf16[4,97,256]{2,1,0:T(8,128)(2,1)}), bf16[4,97,256]{2,1,0:T(8,128)(2,1)S(1)}, u32[]{:S(2)}, u32[]{:S(2)}) async-start(bf16[4,97,256]{2,1,0:T(8,128)(2,1)} %copy.76), calls=%async_computation | async-start | bytes 425984 | tf_op jit(solution)/shard_map/all_to_all | solution.py:226
  14.3 0.7 copy-start.10
  15.4 4.3 %copy-start.6 = (bf16[1,96,4096]{2,1,0:T(8,128)(2,1)S(1)}, bf16[1,96,4096]{2,1,0:T(8,128)(2,1)}, u32[]{:S(2)}) copy-start(bf16[1,96,4096]{2,1,0:T(8,128)(2,1)} %param.23) | copy-start | bytes 2359300
  20.2 5.2 %copy-start.7 = (bf16[1,96,4096]{2,1,0:T(8,128)(2,1)S(1)}, bf16[1,96,4096]{2,1,0:T(8,128)(2,1)}, u32[]{:S(2)}) copy-start(bf16[1,96,4096]{2,1,0:T(8,128)(2,1)} %param.19) | copy-start | bytes 2359300
  21.2 13.6 %all-to-all-start.2 = ((bf16[4,804,128]{2,1,0:T(8,128)(2,1)}), bf16[4,804,128]{2,1,0:T(8,128)(2,1)S(1)}, u32[]{:S(2)}, u32[]{:S(2)}) async-start(bf16[4,804,128]{2,1,0:T(8,128)(2,1)} %pad_maximum_fusion), calls=%async_computation.2 | async-start | bytes 1654784 | tf_op jit(solution)/shard_map/all_to_all | solution.py:226
  24.7 67.0 %all-gather.2.cloned.1.call-start = ((), (), s32[]{:S(2)}) async-start(), calls=%async_computation.9 | async-start | bytes 1843200 | tf_op jit(solution)/shard_map/all_gather | solution.py:251
  25.6 12.7 %copy-start.9 = (bf16[32,128]{1,0:T(8,128)(2,1)S(1)}, bf16[32,128]{1,0:T(8,128)(2,1)}, u32[]{:S(2)}) copy-start(bf16[32,128]{1,0:T(8,128)(2,1)} %param.17) | copy-start | bytes 24580
  25.6 12.7 %copy-start.12 = (bf16[32,128]{1,0:T(8,128)(2,1)S(1)}, bf16[32,128]{1,0:T(8,128)(2,1)}, u32[]{:S(2)}) copy-start(bf16[32,128]{1,0:T(8,128)(2,1)} %param.13) | copy-start | bytes 24580
  25.6 13.4 %copy-start.11 = (bf16[32,128]{1,0:T(8,128)(2,1)S(1)}, bf16[32,128]{1,0:T(8,128)(2,1)}, u32[]{:S(2)}) copy-start(bf16[32,128]{1,0:T(8,128)(2,1)} %param.16) | copy-start | bytes 24580
  25.6 13.5 %copy-start.13 = (f32[32,1]{0,1:T(1,128)S(1)}, f32[32,1]{0,1:T(1,128)}, u32[]{:S(2)}) copy-start(f32[32,1]{0,1:T(1,128)} %param.18) | copy-start | bytes 388
  34.8 14.3 %all-to-all-start.1 = ((bf16[4,768,128]{2,1,0:T(8,128)(2,1)}), bf16[4,768,128]{2,1,0:T(8,128)(2,1)S(1)}, u32[]{:S(2)}, u32[]{:S(2)}) async-start(bf16[4,768,128]{2,1,0:T(8,128)(2,1)} %bitcast.15), calls=%async_computation.1 | async-start | bytes 1572864 | tf_op jit(solution)/shard_map/all_to_all | solution.py:226
  38.3 15.6 %collective-permute-start = (bf16[32,256]{1,0:T(8,128)(2,1)S(1)}, bf16[32,256]{1,0:T(8,128)(2,1)S(1)}, u32[]{:S(2)}, u32[]{:S(2)}) collective-permute-start(bf16[32,256]{1,0:T(8,128)(2,1)S(1)} %pad_maximum_fusion.4), channel_id=1, source_target_pairs={{0,0},{16,64},{32,128},{48,192},{64,256},{80,320},{96,384},{112,44... | collective-permute-start | bytes 49160 | tf_op jit(solution)/shard_map/ppermute | solution.py:266
  39.1 14.8 %collective-permute-start.1 = (f32[2,32]{1,0:T(2,128)S(1)}, f32[2,32]{1,0:T(2,128)S(1)}, u32[]{:S(2)}, u32[]{:S(2)}) collective-permute-start(f32[2,32]{1,0:T(2,128)S(1)} %maximum_bitcast_fusion), channel_id=1, source_target_pairs={{0,0},{16,64},{32,128},{48,192},{64,256},{80,320},{96,384},{112,44... | collective-permute-start | bytes 776 | tf_op jit(solution)/shard_map/ppermute | solution.py:267
  52.8 1.2 copy-start.1
  93.2 14.0 %all-to-all-start.3 = ((bf16[16,32,256]{2,1,0:T(8,128)(2,1)}), bf16[16,32,256]{2,1,0:T(8,128)(2,1)S(1)}, u32[]{:S(2)}, u32[]{:S(2)}) async-start(bf16[16,32,256]{2,1,0:T(8,128)(2,1)} %broadcast_in_dim.27), calls=%async_computation.4 | async-start | bytes 524288 | tf_op jit(solution)/shard_map/all_to_all | solution.py:284
  99.8 83.2 %reduce-scatter.2.cloned.1.call-start = ((), (), s32[]{:S(2)}) async-start(), calls=%async_computation.10 | async-start | bytes 1769472 | tf_op jit(solution)/shard_map/reduce_scatter | solution.py:280
  99.9 1.4 copy-start
  101.3 1.4 copy-start.2
  104.7 1.2 copy-start.3
  107.2 1.4 copy-start.4
  166.4 19.2 %all-to-all-start.4 = ((bf16[4,768,128]{2,1,0:T(8,128)(2,1)}), bf16[4,768,128]{2,1,0:T(8,128)(2,1)S(1)}, u32[]{:S(2)}, u32[]{:S(2)}) async-start(bf16[4,768,128]{2,1,0:T(8,128)(2,1)} %bitcast.27), calls=%async_computation.5 | async-start | bytes 1572864 | tf_op jit(solution)/shard_map/all_to_all | solution.py:226
  170.5 13.5 %collective-permute-start.2 = (bf16[32,128]{1,0:T(8,128)(2,1)S(1)}, bf16[32,128]{1,0:T(8,128)(2,1)S(1)}, u32[]{:S(2)}, u32[]{:S(2)}) collective-permute-start(bf16[32,128]{1,0:T(8,128)(2,1)S(1)} %get-tuple-element.41), channel_id=1, source_target_pairs={{0,0},{64,16},{128,32},{192,48},{256,64},{320,80},{384,96},{448,11... | collective-permute-start | bytes 24584 | tf_op jit(solution)/shard_map/ppermute | solution.py:296
  186.3 8.6 %all-to-all-start.7 = ((bf16[4,97,256]{2,1,0:T(8,128)(2,1)}), bf16[4,97,256]{2,1,0:T(8,128)(2,1)S(1)}, u32[]{:S(2)}, u32[]{:S(2)}) async-start(bf16[4,97,256]{2,1,0:T(8,128)(2,1)} %pad_maximum_fusion.1), calls=%async_computation.8 | async-start | bytes 425984 | tf_op jit(solution)/shard_map/all_to_all | solution.py:226
Sparse Core Ops, SparseCore 0:
  27.6 64.0 all-gather.1
  106.0 76.9 reduce-scatter.1

commit v5 on v4

--- a/solution.py
+++ b/solution.py
@@ -64,36 +64,82 @@
             d_ref[0:reach, HD : 2 * HD] += dv
 
 
-def lower_kernel(info, q_ref, g_ref, rows_ref, kv_ref, dq_in, d_ref, acc, *, span, pitch):
+def lower_kernel(
+    info, q_ref, g_ref, rows_ref, kv_ref, d_ref, acc, taken, given, blank, in_sem, out_sem, blank_sem,
+    *, span, pitch,
+):
     square, live = info[0], info[1]
     squares = kv_ref.shape[0] // pitch
     columns = q_ref.shape[0]
     group = columns // KVH
-    acc[...] = dq_in[...]
     used = jnp.where(live != 0, square, 0)
+    acc[...] = jnp.zeros_like(acc)
+    blank[...] = jnp.zeros_like(blank)
+
+    def place(j):
+        return d_ref.at[pl.ds(pl.multiple_of(j * span, 16), span), :]
+
+    def take(j, slot):
+        source = kv_ref.at[pl.ds(pl.multiple_of(j * pitch, 16), span), :]
+        return pltpu.make_async_copy(source, taken.at[slot], in_sem.at[slot])
+
+    def give(j, slot):
+        return pltpu.make_async_copy(given.at[slot], place(j), out_sem.at[slot])
+
+    def clear(j):
+        return pltpu.make_async_copy(blank, place(j), blank_sem.at[j])
+
+    @pl.when(used > 0)
+    def _():
+        take(0, 0).start()
+
+    def begin(j, carry):
+        clear(j).start()
+        return carry
 
     def whole(j, carry):
-        source = pl.ds(pl.multiple_of(j * pitch, 16), span)
-        block = pl.ds(pl.multiple_of(j * span, 16), span)
-        keys, values = kv_ref[source, 0:HD], kv_ref[source, HD : 2 * HD]
+        slot = lax.rem(j, 2)
+
+        @pl.when(j + 1 < used)
+        def _():
+            take(j + 1, 1 - slot).start()
+
+        take(j, slot).wait()
+        keys, values = taken[slot, :, 0:HD], taken[slot, :, HD : 2 * HD]
         dkeys = dvalues = 0.0
         for c in range(0, columns, 2 * group):
             dk, dv = terms((q_ref, g_ref, rows_ref), keys, values, slice(c, c + 2 * group), None, acc)
             dkeys, dvalues = dkeys + dk, dvalues + dv
-        d_ref[block, 0:HD] = (dkeys * SCALE).astype(BF16)
-        d_ref[block, HD : 2 * HD] = dvalues.astype(BF16)
+
+        @pl.when(j >= 2)
+        def _():
+            give(j - 2, slot).wait()
+
+        given[slot, :, 0:HD] = (dkeys * SCALE).astype(BF16)
+        given[slot, :, HD : 2 * HD] = dvalues.astype(BF16)
+        give(j, slot).start()
         return carry
 
-    def empty(j, carry):
-        d_ref[pl.ds(pl.multiple_of(j * span, 16), span), :] = jnp.zeros((span, 2 * HD), BF16)
+    def end(j, carry):
+        clear(j).wait()
         return carry
 
+    lax.fori_loop(used, squares, begin, 0)
     lax.fori_loop(0, used, whole, 0)
-    lax.fori_loop(used, squares, empty, 0)
+
+    @pl.when(used >= 2)
+    def _():
+        give(used - 2, lax.rem(used, 2)).wait()
+
+    @pl.when(used >= 1)
+    def _():
+        give(used - 1, lax.rem(used + 1, 2)).wait()
+
+    lax.fori_loop(used, squares, end, 0)
 
 
 def prompt_kernel(
-    info, q_ref, g_ref, rows_ref, pq_ref, pg_ref, prows_ref, kv_ref, dq_in,
+    info, q_ref, g_ref, rows_ref, pq_ref, pg_ref, prows_ref, kv_ref, lower_dq, own_dq,
     d_ref, dq_ref, pdq_ref, acc, total,
     *, blocks,
 ):
@@ -102,7 +148,7 @@
     group = columns // KVH
     plen = kv_ref.shape[0]
     rolls = plen // blocks
-    acc[...] = dq_in[...]
+    acc[...] = lower_dq[...] + own_dq[...]
     keys, values = kv_ref[:, 0:HD], kv_ref[:, HD : 2 * HD]
     shape = (plen, pq_ref.shape[0])
     index = lax.broadcasted_iota(jnp.int32, shape, 0)
@@ -156,19 +202,33 @@
     )
 
 
-def lower_backward(info, fixed, kv, carried, span, pitch):
+def lower_backward(info, fixed, kv, span, pitch):
     query = fixed[0]
-    return call(
+    squares = kv.shape[0] // pitch
+    pairs = query.shape[0] * kv.shape[0]
+    vmem = pl.BlockSpec(memory_space=pltpu.VMEM)
+    whole = pl.BlockSpec(memory_space=pl.ANY)
+    return pl.pallas_call(
         functools.partial(lower_kernel, span=span, pitch=pitch),
-        info,
-        (*fixed, kv, carried),
-        (
-            jax.ShapeDtypeStruct((kv.shape[0] // pitch * span, kv.shape[1]), BF16),
-            jax.ShapeDtypeStruct(carried.shape, F32),
+        out_shape=(
+            jax.ShapeDtypeStruct((squares * span, kv.shape[1]), BF16),
+            jax.ShapeDtypeStruct(query.shape[::-1], F32),
         ),
-        [],
-        query.shape[0] * kv.shape[0],
-    )
+        in_specs=[pl.BlockSpec(memory_space=pltpu.SMEM), vmem, vmem, vmem, whole],
+        out_specs=(whole, vmem),
+        scratch_shapes=[
+            pltpu.VMEM((2, span, kv.shape[1]), BF16),
+            pltpu.VMEM((2, span, kv.shape[1]), BF16),
+            pltpu.VMEM((span, kv.shape[1]), BF16),
+            pltpu.SemaphoreType.DMA((2,)),
+            pltpu.SemaphoreType.DMA((2,)),
+            pltpu.SemaphoreType.DMA((squares,)),
+        ],
+        compiler_params=pltpu.CompilerParams(vmem_limit_bytes=40 * 1024 * 1024),
+        cost_estimate=pl.CostEstimate(
+            flops=pairs * HD * 10, bytes_accessed=4 * 1024 * 1024, transcendentals=pairs
+        ),
+    )(info, *fixed, kv)
 
 
 def prompt_backward(info, fixed, prompt_rows, kv, carried, blocks):
@@ -176,14 +236,14 @@
     return call(
         functools.partial(prompt_kernel, blocks=blocks),
         info,
-        (*fixed, *prompt_rows, kv, carried),
+        (*fixed, *prompt_rows, kv, *carried),
         (
             jax.ShapeDtypeStruct(kv.shape, BF16),
             jax.ShapeDtypeStruct(query.shape, BF16),
             jax.ShapeDtypeStruct(prompt_rows[0].shape, BF16),
         ),
-        [pltpu.VMEM(carried.shape, F32), pltpu.VMEM(kv.shape, F32)],
-        query.shape[0] * kv.shape[0] * 25,
+        [pltpu.VMEM(carried[0].shape, F32), pltpu.VMEM(kv.shape, F32)],
+        query.shape[0] * kv.shape[0],
     )
 
 
@@ -272,29 +332,46 @@
     spot = jnp.tile(jnp.arange(rows, dtype=jnp.int32), GRP)[None]
     fixed = (query, grads, pair)
 
-    own, dq = own_backward(info, fixed, spot, mine)
-    kv, p_pack, p_rows, own, dq = together(kv, p_pack, p_rows, own, dq)
+    own, own_dq = own_backward(info, fixed, spot, mine)
+    kv, p_pack, p_rows, own, own_dq = together(kv, p_pack, p_rows, own, own_dq)
     prompt_rows = (p_pack[:, :HD], p_pack[:, HD:], p_rows)
-    lower, dq = lower_backward(info, fixed, kv, dq, span, pitch)
+    lower, lower_dq = lower_backward(info, fixed, kv, span, pitch)
     prompt = kv.reshape(squares, pitch, 2 * HD)[:, span : span + few].reshape(blocks * part, 2 * HD)
+    lower, prompt = together(lower, prompt)
     lower = lax.psum_scatter(lower, "blk", scatter_dimension=0, tiled=True, axis_index_groups=far)
     summed = (own + lower.astype(F32)).astype(BF16)
 
     prompt = jnp.broadcast_to(prompt[None], (rolls,) + prompt.shape)
     prompt = lax.all_to_all(prompt, "roll", 0, 0, tiled=True).reshape(-1, 2 * HD)
     prompt = prompt.reshape(rolls, blocks, part, 2 * HD).transpose(0, 2, 1, 3).reshape(-1, 2 * HD)
-    prompt_terms, dq, p_dq = prompt_backward(info, fixed, prompt_rows, prompt, dq, blocks)
+    prompt_terms, dq, p_dq = prompt_backward(
+        info, fixed, prompt_rows, prompt, (lower_dq, own_dq), blocks
+    )
+
+    place = owner % KVH
+    dq = dq.reshape(KVH, GRP * rows, HD)
+    r_dq = jnp.zeros_like(dq)
+    pieces = []
+    for distance in range(KVH):
+        partner = place ^ distance
+        piece = lax.dynamic_index_in_dim(dq, partner, 0, keepdims=True)
+        if distance:
+            piece = lax.ppermute(piece, "blk", [(i, i ^ distance) for i in range(blocks)])
+        pieces.append(piece)
 
     prompt_terms = prompt_terms.reshape(rolls, part, blocks, 2 * HD).transpose(0, 2, 1, 3)
     prompt_terms = lax.all_to_all(prompt_terms.reshape(rolls, blocks * part, 2 * HD), "roll", 0, 0, tiled=True)
     prompt_terms = jnp.sum(prompt_terms.astype(F32), axis=0).astype(BF16)
+    prompt_terms, *pieces = together(prompt_terms, *pieces)
+    for distance, piece in enumerate(pieces):
+        r_dq = lax.dynamic_update_slice_in_dim(r_dq, piece, place ^ distance, 0)
+    r_dq = r_dq.reshape(KVH, GRP, rows, HD)
     prompt_terms = lax.all_to_all(
         prompt_terms.reshape(squares, KVH * part, 2 * HD), "blk", 0, 0, tiled=True, axis_index_groups=far
     )
     prompt_terms = jnp.sum(prompt_terms.astype(F32), axis=0).astype(BF16)
 
     p_dq = lax.ppermute(p_dq, "blk", back)
-    r_dq = trade(dq.reshape(KVH, GRP * rows, HD)).reshape(KVH, GRP, rows, HD)
     summed, r_dq, p_dq = together(summed, r_dq, p_dq)
     r_dq = r_dq.transpose(2, 0, 1, 3).reshape(1, rows, KVH * GRP * HD)
 

time: 208 us -> 215 us (1.034); the launches traced: 205 us -> 214 us
  blocking collectives: 51.2 us -> 0 us
  starting transfers between devices: 27.3 us -> 60.6 us
  waiting for transfers between devices: 76.4 us -> 104 us
    all_to_all x2 -> x0, blocking collectives: 51.2 us -> none  [the longest x1 38.2 us: on_device(): lax.all_to_all(prompt_terms.reshape(squares, KVH * part, 2 * HD), 'blk',...]
    all_to_all x0 -> x2, starting transfers between devices: none -> 27.5 us  [the longest x1 22.2 us: on_device(): lax.all_to_all(prompt_terms.reshape(squares, KVH * part, 2 * HD), 'blk',...]
    ppermute x0 -> x3, waiting for transfers between devices: none -> 22.6 us  [on_device(): lax.ppermute(piece, 'blk', [(i, i ^ distance) for i in range(blocks)])]
    all_to_all x0 -> x2, waiting for transfers between devices: none -> 12.3 us  [the longest x1 12.3 us: on_device(): lax.all_to_all(prompt_terms.reshape(squares, KVH * part, 2 * HD), 'blk',...]
    reduce_scatter x1, waiting for transfers between devices: 11.8 us -> 0.02 us  [on_device(): lax.psum_scatter(lower, 'blk', scatter_dimension=0, tiled=True, axis_inde...]
    ppermute x0 -> x3, starting transfers between devices: none -> 9.47 us  [on_device(): lax.ppermute(piece, 'blk', [(i, i ^ distance) for i in range(blocks)])]
    all_to_all x1, waiting for transfers between devices: 1.33 us -> 7.34 us  [on_device(): lax.all_to_all(prompt, 'roll', 0, 0, tiled=True).reshape(-1, 2 * HD)]
    all_to_all x5 -> x4, starting transfers between devices: 18.6 us -> 14.6 us  [trade(): lax.all_to_all(block, 'blk', 0, 0, tiled=True, axis_index_groups=near)]
  transfers between devices with their start and end apart: 11 -> 15, of which waited for: 8 -> 9; matrix products, arithmetic and copies ran while one was open for 3% -> 3% of each run, Pallas kernels for 6% -> 5%
where the time goes in v5:
time: 215 us; the launch traced here: 214 us
  waiting for transfers between devices  104 us (48%)
  starting transfers between devices  60.6 us (28%)
  local copies, waits for them, and re-layouts  17.1 us (8%)
  between operations  15.3 us (7%)
  Pallas kernels  12 us (6%)
  other arithmetic  5.58 us (3%)
    all_gather x1, waiting for transfers between devices, on_device(): kv = lax.all_gather(kv, 'blk', axis=0, tiled=True, axis_index_groups=far)  37.7 us
    all_to_all x4, waiting for transfers between devices, trade(): lax.all_to_all(block, 'blk', 0, 0, tiled=True, axis_index_groups=near)  23.1 us
    ppermute x3, waiting for transfers between devices, on_device(): lax.ppermute(piece, 'blk', [(i, i ^ distance) for i in range(blocks)])  22.6 us
    all_to_all x1, starting transfers between devices, on_device(): lax.all_to_all(prompt_terms.reshape(squares, KVH * part, 2 * HD), 'blk',...  22.2 us
    all_to_all x4, starting transfers between devices, trade(): lax.all_to_all(block, 'blk', 0, 0, tiled=True, axis_index_groups=near)  14.6 us
    all_to_all x1, waiting for transfers between devices, on_device(): lax.all_to_all(prompt_terms.reshape(squares, KVH * part, 2 * HD), 'blk',...  12.3 us
    pallas_call x2, Pallas kernels, call(): pl.pallas_call(body, out_shape=outs, in_specs=[pl.BlockSpec(memory_space=...  10.1 us
    unnamed x35, local copies, waits for them, and re-layouts  9.64 us
  transfers between devices with their start and end apart: 15, of which 9 were waited for; matrix products, arithmetic and copies ran while one was open for 3% of the time, Pallas kernels for 5%

profile of v5, /device:TPU:6, one launch (start us, length us, event | category | flops | bytes accessed | tf_op | source)
XLA Modules:
  0.0 214.2 jit_solution(374116434912656339)
XLA Ops:
  7.2 1.1 maximum_maximum_fusion
  8.7 0.7 copy.74
  9.4 4.2 %all-to-all-start = ((bf16[4,97,256]{2,1,0:T(8,128)(2,1)}), bf16[4,97,256]{2,1,0:T(8,128)(2,1)S(1)}, u32[]{:S(2)}, u32[]{:S(2)}) async-start(bf16[4,97,256]{2,1,0:T(8,128)(2,1)} %copy.74), calls=%async_computation | async-start | bytes 425984 | tf_op jit(solution)/shard_map/all_to_all | solution.py:286
  14.5 0.5 copy-done.10
  15.4 0.5 reduce_sum.44
  16.2 2.6 %all-to-all-done = bf16[4,97,256]{2,1,0:T(8,128)(2,1)S(1)} async-done(((bf16[4,97,256]{2,1,0:T(8,128)(2,1)}), bf16[4,97,256]{2,1,0:T(8,128)(2,1)S(1)}, u32[]{:S(2)}, u32[]{:S(2)}) %all-to-all-start) | async-done | bytes 198688 | tf_op jit(solution)/shard_map/all_to_all | solution.py:286
  18.9 0.8 maximum_maximum_fusion.1
  19.9 0.3 copy.79
  20.2 1.0 pad_maximum_fusion
  21.2 3.5 %all-to-all-start.2 = ((bf16[4,804,128]{2,1,0:T(8,128)(2,1)}), bf16[4,804,128]{2,1,0:T(8,128)(2,1)S(1)}, u32[]{:S(2)}, u32[]{:S(2)}) async-start(bf16[4,804,128]{2,1,0:T(8,128)(2,1)} %pad_maximum_fusion), calls=%async_computation.2 | async-start | bytes 1654784 | tf_op jit(solution)/shard_map/all_to_all | solution.py:286
  24.7 0.7 all-gather.2.cloned.1.call-update
  25.6 1.2 copy.78
  26.8 7.9 %all-to-all-done.2 = bf16[4,804,128]{2,1,0:T(8,128)(2,1)S(1)} async-done(((bf16[4,804,128]{2,1,0:T(8,128)(2,1)}), bf16[4,804,128]{2,1,0:T(8,128)(2,1)S(1)}, u32[]{:S(2)}, u32[]{:S(2)}) %all-to-all-start.2) | async-done | bytes 823328 | tf_op jit(solution)/shard_map/all_to_all | solution.py:286
  34.8 3.5 %all-to-all-start.1 = ((bf16[4,768,128]{2,1,0:T(8,128)(2,1)}), bf16[4,768,128]{2,1,0:T(8,128)(2,1)S(1)}, u32[]{:S(2)}, u32[]{:S(2)}) async-start(bf16[4,768,128]{2,1,0:T(8,128)(2,1)} %bitcast.15), calls=%async_computation.1 | async-start | bytes 1572864 | tf_op jit(solution)/shard_map/all_to_all | solution.py:286
  38.3 0.7 collective-permute-start
  39.2 0.7 collective-permute-start.1
  40.2 8.9 %all-to-all-done.1 = bf16[4,768,128]{2,1,0:T(8,128)(2,1)S(1)} async-done(((bf16[4,768,128]{2,1,0:T(8,128)(2,1)}), bf16[4,768,128]{2,1,0:T(8,128)(2,1)S(1)}, u32[]{:S(2)}, u32[]{:S(2)}) %all-to-all-start.1) | async-done | bytes 786464 | tf_op jit(solution)/shard_map/all_to_all | solution.py:286
  49.0 3.7 %shard_map.172 = (f32[384,256]{1,0:T(8,128)S(1)}, f32[128,3072]{1,0:T(8,128)S(1)}) custom-call(s32[4]{0:T(128)S(1)} %pad_add_fusion.info, bf16[3072,128]{1,0:T(8,128)(2,1)S(1)} %bitcast.71, bf16[3072,128]{1,0:T(8,128)(2,1)S(1)} %bitcast.74, f32[2,3072]{1,0:T(2,128)S(1)} %bitcast.81, s32[1,768]{1,0:T(1,128)S(1)} %broadcast_in_dim_tile.3.spot_ref, ...), custom_call_target="tpu_custom_call" | custom-call | tf_op jit(solution)/shard_map/pallas_call | solution.py:179
  52.8 1.2 copy-done.1
  54.0 37.7 %all-gather.2.cloned.1.call-done.kv_ref = bf16[3200,256]{1,0:T(8,128)(2,1)} async-done(((bf16[400,256]{1,0:T(8,128)(2,1)}), bf16[3200,256]{1,0:T(8,128)(2,1)}) %all-gather.2.cloned.1.call-update) | async-done | bytes 1638416 | tf_op jit(solution)/shard_map/all_gather | solution.py:311
  91.6 1.4 copy-done
  93.1 1.9 shard_map.173
  95.0 1.1 copy-done.3
  96.2 0.7 broadcast_in_dim.29
  96.9 7.0 %all-to-all-start.3 = ((bf16[16,32,256]{2,1,0:T(8,128)(2,1)}), bf16[16,32,256]{2,1,0:T(8,128)(2,1)S(1)}, u32[]{:S(2)}, u32[]{:S(2)}) async-start(bf16[16,32,256]{2,1,0:T(8,128)(2,1)} %broadcast_in_dim.29), calls=%async_computation.4 | async-start | bytes 524288 | tf_op jit(solution)/shard_map/all_to_all | solution.py:345
  103.9 7.3 %all-to-all-done.3 = bf16[16,32,256]{2,1,0:T(8,128)(2,1)S(1)} async-done(((bf16[16,32,256]{2,1,0:T(8,128)(2,1)}), bf16[16,32,256]{2,1,0:T(8,128)(2,1)S(1)}, u32[]{:S(2)}, u32[]{:S(2)}) %all-to-all-start.3) | async-done | bytes 262176 | tf_op jit(solution)/shard_map/all_to_all | solution.py:345
  111.2 1.4 copy-done.2
  112.6 1.4 copy-done.4
  114.0 6.4 %shard_map.174 = (bf16[512,256]{1,0:T(8,128)(2,1)}, bf16[3072,128]{1,0:T(8,128)(2,1)S(1)}, bf16[32,128]{1,0:T(8,128)(2,1)S(1)}) custom-call(s32[4]{0:T(128)S(1)} %pad_add_fusion.info, bf16[3072,128]{1,0:T(8,128)(2,1)S(1)} %bitcast.73, bf16[3072,128]{1,0:T(8,128)(2,1)S(1)} %bitcast.76, f32[2,3072]{1,0:T(2,128)S(1)} %bitcast.83, ...), custom_call_target="tpu_custom_call" | custom-call | flops 2013265920 | bytes 4194304 | tf_op jit(solution)/shard_map/pallas_call | solution.py:179
  120.4 5.3 %all-to-all-start.4 = ((bf16[16,32,256]{2,1,0:T(8,128)(2,1)}), bf16[16,32,256]{2,1,0:T(8,128)(2,1)S(1)}, u32[]{:S(2)}, u32[]{:S(2)}) async-start(bf16[16,32,256]{2,1,0:T(8,128)(2,1)} %bitcast.27), calls=%async_computation.5 | async-start | bytes 524288 | tf_op jit(solution)/shard_map/all_to_all | solution.py:363
  125.8 3.4 %collective-permute-start.2 = (bf16[1,768,128]{2,1,0:T(8,128)(2,1)S(1)}, bf16[1,768,128]{2,1,0:T(8,128)(2,1)S(1)}, u32[]{:S(2)}, u32[]{:S(2)}) collective-permute-start(bf16[1,768,128]{2,1,0:T(8,128)(2,1)S(1)} %get-tuple-element.92), channel_id=1, source_target_pairs={{0,16},{16,0},{32,48},{48,32},{64,80},{80,64},{96,112},{112,96},{1... | collective-permute-start | bytes 589832 | tf_op jit(solution)/shard_map/ppermute | solution.py:359
  129.3 2.7 %collective-permute-start.3 = (bf16[1,768,128]{2,1,0:T(8,128)(2,1)S(1)}, bf16[1,768,128]{2,1,0:T(8,128)(2,1)S(1)}, u32[]{:S(2)}, u32[]{:S(2)}) collective-permute-start(bf16[1,768,128]{2,1,0:T(8,128)(2,1)S(1)} %get-tuple-element.91), channel_id=1, source_target_pairs={{0,32},{16,48},{32,0},{48,16},{64,96},{80,112},{96,64},{112,80},{1... | collective-permute-start | bytes 589832 | tf_op jit(solution)/shard_map/ppermute | solution.py:359
  131.9 3.4 %collective-permute-start.4 = (bf16[1,768,128]{2,1,0:T(8,128)(2,1)S(1)}, bf16[1,768,128]{2,1,0:T(8,128)(2,1)S(1)}, u32[]{:S(2)}, u32[]{:S(2)}) collective-permute-start(bf16[1,768,128]{2,1,0:T(8,128)(2,1)S(1)} %get-tuple-element.90), channel_id=1, source_target_pairs={{0,48},{16,32},{32,16},{48,0},{64,112},{80,96},{96,80},{112,64},{1... | collective-permute-start | bytes 589832 | tf_op jit(solution)/shard_map/ppermute | solution.py:359
  135.3 0.7 collective-permute-start.5
  136.1 12.1 %collective-permute-done.3 = bf16[1,768,128]{2,1,0:T(8,128)(2,1)S(1)} collective-permute-done((bf16[1,768,128]{2,1,0:T(8,128)(2,1)S(1)}, bf16[1,768,128]{2,1,0:T(8,128)(2,1)S(1)}, u32[]{:S(2)}, u32[]{:S(2)}) %collective-permute-start.3) | collective-permute-done | bytes 196640 | tf_op jit(solution)/shard_map/ppermute | solution.py:359
  148.2 10.4 %collective-permute-done.4 = bf16[1,768,128]{2,1,0:T(8,128)(2,1)S(1)} collective-permute-done((bf16[1,768,128]{2,1,0:T(8,128)(2,1)S(1)}, bf16[1,768,128]{2,1,0:T(8,128)(2,1)S(1)}, u32[]{:S(2)}, u32[]{:S(2)}) %collective-permute-start.4) | collective-permute-done | bytes 196640 | tf_op jit(solution)/shard_map/ppermute | solution.py:359
  158.6 0.6 reshape.109
  159.2 22.2 %all-to-all-start.5 = ((bf16[8,4,256]{2,1,0:T(4,128)(2,1)}), bf16[8,4,256]{2,1,0:T(4,128)(2,1)S(1)}, u32[]{:S(2)}, u32[]{:S(2)}) async-start(bf16[8,4,256]{2,1,0:T(4,128)(2,1)} %reshape.109), calls=%async_computation.6 | async-start | bytes 32768 | tf_op jit(solution)/shard_map/all_to_all | solution.py:369
  181.7 12.3 %all-to-all-done.5 = bf16[8,4,256]{2,1,0:T(4,128)(2,1)S(1)} async-done(((bf16[8,4,256]{2,1,0:T(4,128)(2,1)}), bf16[8,4,256]{2,1,0:T(4,128)(2,1)S(1)}, u32[]{:S(2)}, u32[]{:S(2)}) %all-to-all-start.5) | async-done | bytes 16416 | tf_op jit(solution)/shard_map/all_to_all | solution.py:369
  194.1 1.0 add_convert_fusion
  195.1 0.7 pad_maximum_fusion.1
  195.8 3.4 %all-to-all-start.6 = ((bf16[4,97,256]{2,1,0:T(8,128)(2,1)}), bf16[4,97,256]{2,1,0:T(8,128)(2,1)S(1)}, u32[]{:S(2)}, u32[]{:S(2)}) async-start(bf16[4,97,256]{2,1,0:T(8,128)(2,1)} %pad_maximum_fusion.1), calls=%async_computation.7 | async-start | bytes 425984 | tf_op jit(solution)/shard_map/all_to_all | solution.py:286
  199.4 1.2 reshape.113
  200.7 3.7 %all-to-all-done.6 = bf16[4,97,256]{2,1,0:T(8,128)(2,1)S(1)} async-done(((bf16[4,97,256]{2,1,0:T(8,128)(2,1)}), bf16[4,97,256]{2,1,0:T(8,128)(2,1)S(1)}, u32[]{:S(2)}, u32[]{:S(2)}) %all-to-all-start.6) | async-done | bytes 198688 | tf_op jit(solution)/shard_map/all_to_all | solution.py:286
  204.9 0.6 slice_bitcast_fusion
  205.5 0.7 copy.84
  206.1 0.7 copy.85
  206.8 0.6 copy.104
  (80 shorter events, 3.4 us)
Async XLA Ops:
  7.2 7.1 %copy-start.8 = (bf16[1,96,4096]{2,1,0:T(8,128)(2,1)S(1)}, bf16[1,96,4096]{2,1,0:T(8,128)(2,1)}, u32[]{:S(2)}) copy-start(bf16[1,96,4096]{2,1,0:T(8,128)(2,1)} %param.22) | copy-start | bytes 2359300
  7.2 7.1 %copy-start.5 = (bf16[1,96,4096]{2,1,0:T(8,128)(2,1)S(1)}, bf16[1,96,4096]{2,1,0:T(8,128)(2,1)}, u32[]{:S(2)}) copy-start(bf16[1,96,4096]{2,1,0:T(8,128)(2,1)} %param.23) | copy-start | bytes 2359300
  9.4 9.4 %all-to-all-start = ((bf16[4,97,256]{2,1,0:T(8,128)(2,1)}), bf16[4,97,256]{2,1,0:T(8,128)(2,1)S(1)}, u32[]{:S(2)}, u32[]{:S(2)}) async-start(bf16[4,97,256]{2,1,0:T(8,128)(2,1)} %copy.74), calls=%async_computation | async-start | bytes 425984 | tf_op jit(solution)/shard_map/all_to_all | solution.py:286
  14.3 0.7 copy-start.10
  15.4 4.3 %copy-start.6 = (bf16[1,96,4096]{2,1,0:T(8,128)(2,1)S(1)}, bf16[1,96,4096]{2,1,0:T(8,128)(2,1)}, u32[]{:S(2)}) copy-start(bf16[1,96,4096]{2,1,0:T(8,128)(2,1)} %param.23) | copy-start | bytes 2359300
  20.2 5.2 %copy-start.7 = (bf16[1,96,4096]{2,1,0:T(8,128)(2,1)S(1)}, bf16[1,96,4096]{2,1,0:T(8,128)(2,1)}, u32[]{:S(2)}) copy-start(bf16[1,96,4096]{2,1,0:T(8,128)(2,1)} %param.19) | copy-start | bytes 2359300
  21.2 13.6 %all-to-all-start.2 = ((bf16[4,804,128]{2,1,0:T(8,128)(2,1)}), bf16[4,804,128]{2,1,0:T(8,128)(2,1)S(1)}, u32[]{:S(2)}, u32[]{:S(2)}) async-start(bf16[4,804,128]{2,1,0:T(8,128)(2,1)} %pad_maximum_fusion), calls=%async_computation.2 | async-start | bytes 1654784 | tf_op jit(solution)/shard_map/all_to_all | solution.py:286
  24.7 67.0 %all-gather.2.cloned.1.call-start = ((), (), s32[]{:S(2)}) async-start(), calls=%async_computation.8 | async-start | bytes 1843200 | tf_op jit(solution)/shard_map/all_gather | solution.py:311
  25.6 12.7 %copy-start.9 = (bf16[32,128]{1,0:T(8,128)(2,1)S(1)}, bf16[32,128]{1,0:T(8,128)(2,1)}, u32[]{:S(2)}) copy-start(bf16[32,128]{1,0:T(8,128)(2,1)} %param.17) | copy-start | bytes 24580
  25.6 12.7 %copy-start.12 = (bf16[32,128]{1,0:T(8,128)(2,1)S(1)}, bf16[32,128]{1,0:T(8,128)(2,1)}, u32[]{:S(2)}) copy-start(bf16[32,128]{1,0:T(8,128)(2,1)} %param.13) | copy-start | bytes 24580
  25.6 13.4 %copy-start.11 = (bf16[32,128]{1,0:T(8,128)(2,1)S(1)}, bf16[32,128]{1,0:T(8,128)(2,1)}, u32[]{:S(2)}) copy-start(bf16[32,128]{1,0:T(8,128)(2,1)} %param.16) | copy-start | bytes 24580
  25.6 13.5 %copy-start.13 = (f32[32,1]{0,1:T(1,128)S(1)}, f32[32,1]{0,1:T(1,128)}, u32[]{:S(2)}) copy-start(f32[32,1]{0,1:T(1,128)} %param.18) | copy-start | bytes 388
  34.8 14.3 %all-to-all-start.1 = ((bf16[4,768,128]{2,1,0:T(8,128)(2,1)}), bf16[4,768,128]{2,1,0:T(8,128)(2,1)S(1)}, u32[]{:S(2)}, u32[]{:S(2)}) async-start(bf16[4,768,128]{2,1,0:T(8,128)(2,1)} %bitcast.15), calls=%async_computation.1 | async-start | bytes 1572864 | tf_op jit(solution)/shard_map/all_to_all | solution.py:286
  38.3 155.8 %reduce-scatter.2.cloned.1.call-start = ((), (), s32[]{:S(2)}) async-start(), calls=%async_computation.9 | async-start | bytes 1769472 | tf_op jit(solution)/shard_map/reduce_scatter | solution.py:341
  38.3 15.6 %collective-permute-start = (bf16[32,256]{1,0:T(8,128)(2,1)S(1)}, bf16[32,256]{1,0:T(8,128)(2,1)S(1)}, u32[]{:S(2)}, u32[]{:S(2)}) collective-permute-start(bf16[32,256]{1,0:T(8,128)(2,1)S(1)} %pad_maximum_fusion.4), channel_id=1, source_target_pairs={{0,0},{16,64},{32,128},{48,192},{64,256},{80,320},{96,384},{112,44... | collective-permute-start | bytes 49160 | tf_op jit(solution)/shard_map/ppermute | solution.py:326
  39.2 14.8 %collective-permute-start.1 = (f32[2,32]{1,0:T(2,128)S(1)}, f32[2,32]{1,0:T(2,128)S(1)}, u32[]{:S(2)}, u32[]{:S(2)}) collective-permute-start(f32[2,32]{1,0:T(2,128)S(1)} %maximum_bitcast_fusion), channel_id=1, source_target_pairs={{0,0},{16,64},{32,128},{48,192},{64,256},{80,320},{96,384},{112,44... | collective-permute-start | bytes 776 | tf_op jit(solution)/shard_map/ppermute | solution.py:327
  52.8 1.2 copy-start.1
  91.6 1.4 copy-start
  95.0 1.2 copy-start.3
  96.9 14.3 %all-to-all-start.3 = ((bf16[16,32,256]{2,1,0:T(8,128)(2,1)}), bf16[16,32,256]{2,1,0:T(8,128)(2,1)S(1)}, u32[]{:S(2)}, u32[]{:S(2)}) async-start(bf16[16,32,256]{2,1,0:T(8,128)(2,1)} %broadcast_in_dim.29), calls=%async_computation.4 | async-start | bytes 524288 | tf_op jit(solution)/shard_map/all_to_all | solution.py:345
  111.2 1.4 copy-start.2
  112.6 1.4 copy-start.4
  120.4 15.6 %all-to-all-start.4 = ((bf16[16,32,256]{2,1,0:T(8,128)(2,1)}), bf16[16,32,256]{2,1,0:T(8,128)(2,1)S(1)}, u32[]{:S(2)}, u32[]{:S(2)}) async-start(bf16[16,32,256]{2,1,0:T(8,128)(2,1)} %bitcast.27), calls=%async_computation.5 | async-start | bytes 524288 | tf_op jit(solution)/shard_map/all_to_all | solution.py:363
  125.8 10.2 %collective-permute-start.2 = (bf16[1,768,128]{2,1,0:T(8,128)(2,1)S(1)}, bf16[1,768,128]{2,1,0:T(8,128)(2,1)S(1)}, u32[]{:S(2)}, u32[]{:S(2)}) collective-permute-start(bf16[1,768,128]{2,1,0:T(8,128)(2,1)S(1)} %get-tuple-element.92), channel_id=1, source_target_pairs={{0,16},{16,0},{32,48},{48,32},{64,80},{80,64},{96,112},{112,96},{1... | collective-permute-start | bytes 589832 | tf_op jit(solution)/shard_map/ppermute | solution.py:359
  129.3 18.9 %collective-permute-start.3 = (bf16[1,768,128]{2,1,0:T(8,128)(2,1)S(1)}, bf16[1,768,128]{2,1,0:T(8,128)(2,1)S(1)}, u32[]{:S(2)}, u32[]{:S(2)}) collective-permute-start(bf16[1,768,128]{2,1,0:T(8,128)(2,1)S(1)} %get-tuple-element.91), channel_id=1, source_target_pairs={{0,32},{16,48},{32,0},{48,16},{64,96},{80,112},{96,64},{112,80},{1... | collective-permute-start | bytes 589832 | tf_op jit(solution)/shard_map/ppermute | solution.py:359
  131.9 26.7 %collective-permute-start.4 = (bf16[1,768,128]{2,1,0:T(8,128)(2,1)S(1)}, bf16[1,768,128]{2,1,0:T(8,128)(2,1)S(1)}, u32[]{:S(2)}, u32[]{:S(2)}) collective-permute-start(bf16[1,768,128]{2,1,0:T(8,128)(2,1)S(1)} %get-tuple-element.90), channel_id=1, source_target_pairs={{0,48},{16,32},{32,16},{48,0},{64,112},{80,96},{96,80},{112,64},{1... | collective-permute-start | bytes 589832 | tf_op jit(solution)/shard_map/ppermute | solution.py:359
  135.3 59.7 %collective-permute-start.5 = (bf16[32,128]{1,0:T(8,128)(2,1)S(1)}, bf16[32,128]{1,0:T(8,128)(2,1)S(1)}, u32[]{:S(2)}, u32[]{:S(2)}) collective-permute-start(bf16[32,128]{1,0:T(8,128)(2,1)S(1)} %get-tuple-element.55), channel_id=1, source_target_pairs={{0,0},{64,16},{128,32},{192,48},{256,64},{320,80},{384,96},{448,11... | collective-permute-start | bytes 24584 | tf_op jit(solution)/shard_map/ppermute | solution.py:374
  159.2 34.8 %all-to-all-start.5 = ((bf16[8,4,256]{2,1,0:T(4,128)(2,1)}), bf16[8,4,256]{2,1,0:T(4,128)(2,1)S(1)}, u32[]{:S(2)}, u32[]{:S(2)}) async-start(bf16[8,4,256]{2,1,0:T(4,128)(2,1)} %reshape.109), calls=%async_computation.6 | async-start | bytes 32768 | tf_op jit(solution)/shard_map/all_to_all | solution.py:369
  195.8 8.6 %all-to-all-start.6 = ((bf16[4,97,256]{2,1,0:T(8,128)(2,1)}), bf16[4,97,256]{2,1,0:T(8,128)(2,1)S(1)}, u32[]{:S(2)}, u32[]{:S(2)}) async-start(bf16[4,97,256]{2,1,0:T(8,128)(2,1)} %pad_maximum_fusion.1), calls=%async_computation.7 | async-start | bytes 425984 | tf_op jit(solution)/shard_map/all_to_all | solution.py:286
Sparse Core Ops, SparseCore 0:
  27.6 63.9 all-gather.1
  96.3 79.3 reduce-scatter.1
